TPU v7x, 32 devices: a whole 2x2x4 slice. The times are simulated.
32 devices in a mesh: layer: 4 (over y, x), dp: 8 (over z, core).
Axes of the slice: x: 2, y: 2, z: 4, core: 2. Of those that a mesh axis runs over, the one named last changes fastest.
Arguments:
- activations: bfloat16 [4, 5120, 2048], P('layer', 'dp'), may hold values from -6 to 6
- out_grads: bfloat16 [4, 5120, 512], P('layer', 'dp'), may hold values from -0.059814453 to 0.059814453
- a_inverse: bfloat16 [4, 2048, 2048], P('layer', 'dp'), may hold values from -1 to 3, as said below
- s_inverse: bfloat16 [4, 512, 512], P('layer'), may hold values from -1 to 3, as said below
- in_decay: float32 [4, 2048], P('layer', 'dp'), may hold values from 0 to 1
- out_decay: float32 [4, 512], P('layer'), may hold values from 0 to 1
Outputs:
- direction: bfloat16 [4, 2048, 512], P('layer', 'dp')
Inputs may be any that keep to these rules, and one draw needn't show every extreme that they name: `a_inverse`: each layer's matrix is a positive diagonal plus dense small entries. `s_inverse`: each layer's matrix is a positive diagonal plus dense small entries.
All inputs are finite; a program needn't handle non-finite values.
Results may differ from a plain program's by a relative error of at most 0.0036.
Values may be sent and summed in bfloat16 or wider, within the bound.
No kernel may reach another device: no remote copies, remote signals or barrier semaphores. Data moves between devices by JAX's collectives and lax.ppermute only.
A program may use at most 64 MiB of HBM per device.

v0:
```python
import jax
import jax.numpy as jnp
from jax import lax
from jax.sharding import PartitionSpec as P


def prefix(shard, axis, combine, identity, reverse):
    peers, here = (lax.axis_size(axis), lax.axis_index(axis))
    everything = jax.tree.map(lambda part: lax.all_gather(part, axis), shard)
    start = jax.tree.map(
        lambda part, zero: jnp.broadcast_to(jnp.asarray(zero, part.dtype), part.shape),
        shard,
        identity,
    )

    def turn(k, before):
        at = peers - 1 - k if reverse else k
        reached = at > here if reverse else at < here
        new = combine(before, jax.tree.map(lambda part: part[at], everything))
        return jax.tree.map(lambda a, b: jnp.where(reached, a, b), new, before)

    return lax.fori_loop(0, peers, turn, start)


def compose(earlier, later):
    joined = later[2] + later[0][:, None] * later[1][None, :] * earlier[2]
    return (later[0] * earlier[0], later[1] * earlier[1], joined)


def shards(activations, out_grads, a_inverse, s_inverse, in_decay, out_decay):
    inputs_here = activations[0]
    grads_here = out_grads[0]
    contract = (((0,), (0,)), ((), ()))
    window_cols = inputs_here
    grad_rows = lax.psum_scatter(
        lax.dot_general(window_cols, grads_here, contract, preferred_element_type=jnp.float32),
        "dp",
        scatter_dimension=0,
        tiled=True,
    )
    rates_in = in_decay[0]
    rates_out = out_decay[0]
    coupling = rates_in[:, None] * rates_out[None, :]
    identity = (jnp.ones_like(rates_in), jnp.ones_like(rates_out), jnp.zeros_like(grad_rows))
    later_solved = prefix((rates_in, rates_out, grad_rows), "layer", compose, identity, True)[2]
    upper_solved = grad_rows + coupling * later_solved
    s_applied = jnp.dot(
        upper_solved.astype(jnp.bfloat16), s_inverse[0], preferred_element_type=jnp.float32
    ).astype(jnp.bfloat16)
    a_rows = a_inverse[0]
    window_cols = a_rows
    solved = jnp.dot(
        window_cols,
        lax.all_gather(s_applied, "dp", axis=0, tiled=True),
        preferred_element_type=jnp.float32,
    )
    earlier_state = prefix(
        (rates_in, rates_out, coupling * solved), "layer", compose, identity, False
    )[2]
    lower_solved = solved + earlier_state
    return lower_solved.astype(jnp.bfloat16)[None]


def solution(mesh):
    placed = (
        P("layer", "dp", None),
        P("layer", "dp", None),
        P("layer", "dp", None),
        P("layer", None, None),
        P("layer", "dp"),
        P("layer", None),
    )
    return jax.shard_map(
        shards, mesh=mesh, in_specs=placed, out_specs=P("layer", "dp", None), check_vma=False
    )
```

profile of v0, /device:TPU:0, one launch (start us, length us, event | category | flops | bytes accessed | tf_op | source)
XLA Modules:
  0.0 189.8 jit_solution(3948895402247803283)
XLA Ops:
  6.5 0.0 copy-start
  6.5 0.0 reduce-scatter.2.cloned.1.call-start
  6.5 1.7 copy-done
  8.3 4.9 %fusion.2 = f32[2048,512]{1,0:T(8,128)} fusion(bf16[1,640,2048]{2,1,0:T(8,128)(2,1)S(1)} %copy-done, bf16[1,640,512]{2,1,0:T(8,128)(2,1)} %param.11), kind=kOutput, calls=%fused_computation.8 | convolution fusion | flops 1342177280 | bytes 7471104 | tf_op jit(solution)/shard_map/dot_general | solution.py:36
  13.2 0.0 reduce-scatter.2.cloned.1.call-update
  13.2 0.0 all-gather.10.cloned.1.call-start
  13.2 52.8 %reduce-scatter.2.cloned.1.call-done = f32[256,512]{1,0:T(8,128)} async-done(((f32[2048,512]{1,0:T(8,128)}), f32[256,512]{1,0:T(8,128)}) %reduce-scatter.2.cloned.1.call-update) | async-done | bytes 524304 | tf_op jit(solution)/shard_map/reduce_scatter | solution.py:35
  66.0 0.0 all-gather.10.cloned.1.call-update
  66.1 0.0 all-gather.8.cloned.1.call-start
  66.1 0.0 copy-done.2
  66.1 8.0 %all-gather.3 = f32[4,1,512]{2,1,0:T(1,128)S(1)} all-gather(f32[1,1,512]{2,1,0:T(1,128)S(1)} %bitcast.66), channel_id=1, replica_groups=mesh['layer'=4,'dp'=8] {'layer'}, dimensions={0}, use_global_device_ids=true | all-gather | bytes 10240 | tf_op jit(solution)/shard_map/all_gather | solution.py:9
  74.2 0.0 copy-done.1
  74.2 8.0 %all-gather.2 = f32[4,1,256]{2,1,0:T(1,128)S(1)} all-gather(f32[1,1,256]{2,1,0:T(1,128)S(1)} %bitcast.63), channel_id=1, replica_groups=mesh['layer'=4,'dp'=8] {'layer'}, dimensions={0}, use_global_device_ids=true | all-gather | bytes 5120 | tf_op jit(solution)/shard_map/all_gather | solution.py:9
  82.2 19.2 %all-gather.10.cloned.1.call-done = f32[1024,512]{1,0:T(8,128)} async-done(((f32[256,512]{1,0:T(8,128)}), f32[1024,512]{1,0:T(8,128)}) %all-gather.10.cloned.1.call-update) | async-done | bytes 2097168 | tf_op jit(solution)/shard_map/all_gather | solution.py:9
  101.4 5.0 %while.30 = (s32[]{:T(128)}, f32[256,512]{1,0:T(8,128)S(1)}, s32[]{:T(128)}, f32[4,256,512]{2,1,0:T(8,128)}, f32[4,256]{1,0:T(4,128)S(1)}, /*index=5*/f32[4,512]...) while((s32[]{:T(128)}, f32[256,512]{1,0:T(8,128)S(1)}, s32[]{:T(128)}, ...), condition=%wide.region_2.3_spmd.clone, body=%wide.region_1.2_spmd.clone.sunk | while | flops 655368 | bytes 1582259 | solution.py:22
  101.4 1.2 fusion.16
  102.7 1.2 fusion.16
  103.9 1.2 fusion.16
  105.2 1.2 fusion.16
  106.4 2.3 %convolution_convert_fusion = bf16[256,512]{1,0:T(8,128)(2,1)} fusion(bf16[1,512,512]{2,1,0:T(8,128)(2,1)} %param.13, f32[256,512]{1,0:T(8,128)} %reduce-scatter.2.cloned.1.call-done, f32[256,512]{1,0:T(8,128)S(1)} %get-tuple-element.268, f32[512]{0:T(512)S(1)} %bitcast.67, f32[256]{0:T(256)S(1)} %bitcast.64), kind=kOutput, calls=%fused_computation.11 | convolution fusion | flops 134873088 | bytes 1838080 | tf_op jit(solution)/shard_map/dot_general | solution.py:47
  108.7 0.0 all-gather.8.cloned.1.call-update
  108.7 0.0 all-gather.12.cloned.1.call-start
  108.7 29.2 %all-gather.8.cloned.1.call-done = bf16[2048,512]{1,0:T(8,128)(2,1)} async-done(((bf16[256,512]{1,0:T(8,128)(2,1)}), bf16[2048,512]{1,0:T(8,128)(2,1)}) %all-gather.8.cloned.1.call-update) | async-done | bytes 2097168 | tf_op jit(solution)/shard_map/all_gather | solution.py:54
  137.9 3.6 %multiply_multiply_fusion = (f32[256,512]{1,0:T(8,128)}, f32[256,512]{1,0:T(8,128)}) fusion(f32[512]{0:T(512)S(1)} %bitcast.68, f32[256]{0:T(256)S(1)} %bitcast.65, bf16[2048,512]{1,0:T(8,128)(2,1)} %all-gather.8.cloned.1.call-done, bf16[1,256,2048]{2,1,0:T(8,128)(2,1)} %param.12), kind=kOutput, calls=%fused_computation.13 | convolution fusion | flops 537133056 | bytes 4197376 | tf_op jit(solution)/shard_map/dot_general | solution.py:52
  141.5 0.0 all-gather.12.cloned.1.call-update
  141.6 35.0 %all-gather.12.cloned.1.call-done = f32[1024,512]{1,0:T(8,128)} async-done(((f32[256,512]{1,0:T(8,128)}), f32[1024,512]{1,0:T(8,128)}) %all-gather.12.cloned.1.call-update) | async-done | bytes 2097168 | tf_op jit(solution)/shard_map/all_gather | solution.py:9
  176.5 5.0 %while.31 = (s32[]{:T(128)}, f32[256,512]{1,0:T(8,128)S(1)}, s32[]{:T(128)}, f32[4,256,512]{2,1,0:T(8,128)}, f32[4,256]{1,0:T(4,128)S(1)}, /*index=5*/f32[4,512]{1,0:T(4,128)S(1)}, s32[]{:T(128)}, s32[]{:T(128)}) while((s32[]{:T(128)}, f32[256,512]{1,0:T(8,128)S(1)}, s32[]{:T(128)}, f32[4,256,512]{2,1,0:T(8,128)}, ...), condition=%wide.region_4.5_spmd.clone, body=%wide.region_3.4_spmd.clone.sunk | while | flops 655364 | bytes 1582197 | solution.py:22
  176.5 1.2 fusion.17
  177.8 1.2 fusion.17
  179.0 1.2 fusion.17
  180.3 1.2 fusion.17
  181.5 1.8 fusion.9
  (22 shorter events, 0.1 us)
Async XLA Ops:
  6.5 1.7 copy-start
  6.5 59.5 %reduce-scatter.2.cloned.1.call-start = ((), (), s32[]{:S(2)}) async-start(), calls=%async_computation.1 | async-start | bytes 4718592 | tf_op jit(solution)/shard_map/reduce_scatter | solution.py:35
  13.2 53.0 %copy-start.2 = (f32[1,512]{1,0:T(1,128)S(1)}, f32[1,512]{1,0:T(1,128)}, u32[]{:S(2)}) copy-start(f32[1,512]{1,0:T(1,128)} %param.15) | copy-start | bytes 6148
  13.2 61.0 %copy-start.1 = (f32[1,256]{1,0:T(1,128)S(1)}, f32[1,256]{1,0:T(1,128)}, u32[]{:S(2)}) copy-start(f32[1,256]{1,0:T(1,128)} %param.14) | copy-start | bytes 3076
  13.2 88.2 %all-gather.10.cloned.1.call-start = ((), (), s32[]{:S(2)}) async-start(), calls=%async_computation.3 | async-start | bytes 2621440 | tf_op jit(solution)/shard_map/all_gather | solution.py:9
  66.1 71.9 %all-gather.8.cloned.1.call-start = ((), (), s32[]{:S(2)}) async-start(), calls=%async_computation.2 | async-start | bytes 2359296 | tf_op jit(solution)/shard_map/all_gather | solution.py:54
  108.7 67.8 %all-gather.12.cloned.1.call-start = ((), (), s32[]{:S(2)}) async-start(), calls=%async_computation.4 | async-start | bytes 2621440 | tf_op jit(solution)/shard_map/all_gather | solution.py:9
Sparse Core Ops, SparseCore 0:
  13.3 52.6 reduce-scatter.1
  67.9 33.4 all-gather.9
  108.8 29.0 all-gather.7
  141.7 34.7 all-gather.11
where the time goes:
time: 191 us; the launch traced here: 190 us
  waiting for transfers between devices  136 us (71%)
  blocking collectives  16.1 us (8%)
  between operations  13.2 us (7%)
  other arithmetic  11.4 us (6%)
  matrix products  10.7 us (6%)
    all_gather x2, waiting for transfers between devices, prefix(): everything = jax.tree.map(lambda part: lax.all_gather(part, axis), shard)  54.1 us
    reduce_scatter x1, waiting for transfers between devices, shards(): lax.psum_scatter(lax.dot_general(window_cols, grads_here, contract, prefe...  52.8 us
    all_gather x1, waiting for transfers between devices, shards(): lax.all_gather(s_applied, 'dp', axis=0, tiled=True)  29.2 us
    all_gather x2, blocking collectives, prefix(): everything = jax.tree.map(lambda part: lax.all_gather(part, axis), shard)  16.1 us
    select_n x8, other arithmetic, turn(): return jax.tree.map(lambda a, b: jnp.where(reached, a, b), new, before)  9.54 us
    dot_general x1, matrix products, shards(): lax.dot_general(window_cols, grads_here, contract, preferred_element_type...  4.88 us
  transfers between devices with their start and end apart: 4, of which 4 were waited for; matrix products, arithmetic and copies ran while one was open for 0% of the time, Pallas kernels for 0%

commit v1 on v0

v1 whole, which is shorter than its diff:
```python
import jax
import jax.numpy as jnp
from jax import lax
from jax.sharding import PartitionSpec as P

MARGIN = 16


def exchange(x, axis, flip):
    return lax.ppermute(x, axis, [(i, i ^ flip) for i in range(lax.axis_size(axis))])


def pack(x):
    top = jnp.maximum(jnp.max(jnp.abs(x)), 1e-30)
    power = jnp.floor(jnp.log2(top))
    body = (x * jnp.exp2(13.0 - power)).astype(jnp.float16)
    tail = jnp.full((MARGIN, x.shape[1]), power.astype(jnp.float16))
    return jnp.concatenate([body, tail], axis=0)


def unpack(message):
    power = message[-1, 0].astype(jnp.float32)
    return message[:-MARGIN].astype(jnp.float32) * jnp.exp2(power - 13.0)


def outer(pair):
    return pair[0][:, None] * pair[1][None, :]


def shards(activations, out_grads, a_inverse, s_inverse, in_decay, out_decay):
    layers, peers = lax.axis_size("layer"), lax.axis_size("dp")
    layer, here = lax.axis_index("layer"), lax.axis_index("dp")
    core, chip = here % 2, here // 2
    rows = a_inverse.shape[1]
    width = out_grads.shape[2]
    tokens = activations.shape[1]
    chips = peers // 2

    rates = (in_decay[0], out_decay[0])
    steps = []
    own = rates
    below = rates
    above = (jnp.ones_like(rates[0]), jnp.ones_like(rates[1]))
    flip = 1
    while flip < layers:
        other = tuple(exchange(r, "layer", flip) for r in own)
        steps.append((flip, own, other, below, above))
        high = (layer & flip) != 0
        above = tuple(jnp.where(high, a * o, a) for a, o in zip(above, other))
        below = tuple(jnp.where(high, b, b * o) for b, o in zip(below, other))
        own = tuple(a * b for a, b in zip(own, other))
        flip *= 2

    window = activations[0].reshape(tokens, chips, 2, rows)
    contract = (((0,), (0,)), ((), ()))

    def partial(of):
        take = lax.dynamic_index_in_dim(window, of, 2, keepdims=False).reshape(tokens, chips * rows)
        return lax.dot_general(take, out_grads[0], contract, preferred_element_type=jnp.float32)

    theirs = unpack(exchange(pack(partial(1 - core)), "dp", 1))
    summed = (partial(core) + theirs).reshape(chips, rows, width)

    def block(at):
        return lax.dynamic_index_in_dim(summed, at, 0, keepdims=False)

    grad = block(chip)
    for flip in range(1, chips):
        grad = grad + unpack(exchange(pack(block(chip ^ flip)), "dp", 2 * flip))

    upper, total = grad, grad
    for flip, mine, other, below, above in steps:
        got = unpack(exchange(pack(total), "layer", flip))
        high = (layer & flip) != 0
        upper = jnp.where(high, upper, upper + outer(below) * got)
        total = jnp.where(high, got + outer(other) * total, total + outer(mine) * got)

    s_applied = jnp.dot(
        upper.astype(jnp.bfloat16), s_inverse[0], preferred_element_type=jnp.float32
    ).astype(jnp.bfloat16)

    parts = [s_applied] + [exchange(s_applied, "dp", 2 * f) for f in range(1, chips)]
    a_rows = a_inverse[0].reshape(rows, chips, 2, rows)
    solved = jnp.zeros((rows, width), jnp.float32)
    for flip, part in enumerate(parts):
        other = exchange(part, "dp", 1)
        for of, operand in ((core, part), (1 - core, other)):
            columns = lax.dynamic_slice(a_rows, (0, chip ^ flip, of, 0), (rows, 1, 1, rows)).reshape(rows, rows)
            solved = solved + jnp.dot(columns, operand, preferred_element_type=jnp.float32)

    lower, total = solved, outer(rates) * solved
    for flip, mine, other, below, above in steps:
        got = unpack(exchange(pack(total), "layer", flip))
        high = (layer & flip) != 0
        lower = jnp.where(high, lower + outer(above) * got, lower)
        total = jnp.where(high, total + outer(mine) * got, got + outer(other) * total)
    return lower.astype(jnp.bfloat16)[None]


def solution(mesh):
    placed = (
        P("layer", "dp", None),
        P("layer", "dp", None),
        P("layer", "dp", None),
        P("layer", None, None),
        P("layer", "dp"),
        P("layer", None),
    )
    return jax.shard_map(
        shards, mesh=mesh, in_specs=placed, out_specs=P("layer", "dp", None), check_vma=False
    )
```

time: 191 us -> 121 us (0.63)
  waiting for transfers between devices: 136 us -> 57.7 us
  starting transfers between devices: 0.12 us -> 22.5 us
  blocking collectives: 16.1 us -> 0 us
  local copies, waits for them, and re-layouts: 1.89 us -> 14.2 us
  other arithmetic: 11.4 us -> 6.25 us
  matrix products: 10.7 us -> 8.36 us
    all_gather x3 -> x0, waiting for transfers between devices: 83.3 us -> none  [the longest x2 54.1 us: prefix(): everything = jax.tree.map(lambda part: lax.all_gather(part, axis), shard)]
    ppermute x0 -> x17, waiting for transfers between devices: none -> 57.7 us  [exchange(): lax.ppermute(x, axis, [(i, i ^ flip) for i in range(lax.axis_size(axis))])]
    reduce_scatter x1 -> x0, waiting for transfers between devices: 52.8 us -> none  [shards(): lax.psum_scatter(lax.dot_general(window_cols, grads_here, contract, prefe...]
    ppermute x0 -> x17, starting transfers between devices: none -> 22.5 us  [exchange(): lax.ppermute(x, axis, [(i, i ^ flip) for i in range(lax.axis_size(axis))])]
    all_gather x2 -> x0, blocking collectives: 16.1 us -> none  [prefix(): everything = jax.tree.map(lambda part: lax.all_gather(part, axis), shard)]
    select_n x8 -> x2, other arithmetic: 9.54 us -> 0.01 us  [shards(): above = tuple((jnp.where(high, a * o, a) for a, o in zip(above, other)))]
    slice x0 -> x8, local copies, waits for them, and re-layouts: none -> 6.19 us  [unpack(): power = message[-1, 0].astype(jnp.float32)]
    reduce_max x0 -> x4, other arithmetic: none -> 4.54 us  [pack(): top = jnp.maximum(jnp.max(jnp.abs(x)), 1e-30)]
  transfers between devices with their start and end apart: 4 -> 17, of which waited for: 4 -> 10; matrix products, arithmetic and copies ran while one was open for 0% -> 6% of each run, Pallas kernels for 0% -> 0%
where the time goes in v1:
time: 121 us
  waiting for transfers between devices  57.7 us (48%)
  starting transfers between devices  22.5 us (19%)
  local copies, waits for them, and re-layouts  14.2 us (12%)
  between operations  11.6 us (10%)
  matrix products  8.36 us (7%)
  other arithmetic  6.25 us (5%)
    ppermute x17, waiting for transfers between devices, exchange(): lax.ppermute(x, axis, [(i, i ^ flip) for i in range(lax.axis_size(axis))])  57.7 us
    ppermute x17, starting transfers between devices, exchange(): lax.ppermute(x, axis, [(i, i ^ flip) for i in range(lax.axis_size(axis))])  22.5 us
    slice x8, local copies, waits for them, and re-layouts, unpack(): power = message[-1, 0].astype(jnp.float32)  6.19 us
    unnamed x10, local copies, waits for them, and re-layouts  4.69 us
    reduce_max x4, other arithmetic, pack(): top = jnp.maximum(jnp.max(jnp.abs(x)), 1e-30)  4.54 us
    dot_general x2, matrix products, partial(): lax.dot_general(take, out_grads[0], contract, preferred_element_type=jnp....  4.24 us
    dot_general x8, matrix products, shards(): jnp.dot(columns, operand, preferred_element_type=jnp.float32)  2.64 us
  transfers between devices with their start and end apart: 17, of which 10 were waited for; matrix products, arithmetic and copies ran while one was open for 6% of the time, Pallas kernels for 0%

profile of v1, /device:TPU:0, one launch (start us, length us, event | category | flops | bytes accessed | tf_op | source)
XLA Modules:
  0.0 120.6 jit_solution(4331765989460695752)
XLA Ops:
  0.0 3.2 %copy.9 = bf16[1,640,2048]{1,2,0:T(8,128)(2,1)S(1)} copy(bf16[1,640,2048]{2,1,0:T(8,128)(2,1)} %param.6) | data formatting | bytes 5242880 | tf_op args[0]
  3.2 1.3 %constant_dynamic-slice_fusion.1 = (bf16[640,4,1,256]{0,3,2,1:T(8,128)(2,1)}, bf16[640,4,1,256]{0,3,2,1:T(8,128)(2,1)S(1)}) fusion(bf16[640,4,2,256]{0,3,2,1:T(8,128)(2,1)S(1)} %bitcast.86, s32[]{:T(128)S(6)} %select_n.106, s32[]{:T(128)S(6)} %select_n.107), kind=kLoop, calls=%fused_computation.93 | loop fusion | bytes 5242888 | tf_op jit(solution)/shard_map/jit(dynamic_index_in_dim)/dynamic_slice | solution.py:58
  4.5 1.7 %abs_reduce_fusion = (f32[]{:T(128)}, f32[1024,512]{1,0:T(8,128)S(1)}) fusion(bf16[640,1024]{0,1:T(8,128)(2,1)S(1)} %bitcast.99, bf16[1,640,512]{2,1,0:T(8,128)(2,1)S(1)} %copy-done), kind=kOutput, calls=%fused_computation.2 | convolution fusion | flops 672137216 | bytes 4063236 | tf_op jit(solution)/shard_map/dot_general | solution.py:59
  8.0 2.3 %collective-permute-done = f16[1040,512]{1,0:T(8,128)(2,1)S(1)} collective-permute-done((f16[1040,512]{1,0:T(8,128)(2,1)S(1)}, f16[1040,512]{1,0:T(8,128)(2,1)S(1)}, u32[]{:S(2)}, u32[]{:S(2)}) %collective-permute-start) | collective-permute-done | bytes 1064992 | tf_op jit(solution)/shard_map/ppermute | solution.py:10
  11.5 2.6 %multiply_add_fusion = f32[1024,512]{1,0:T(8,128)S(1)} fusion(f16[1040,512]{1,0:T(8,128)(2,1)} %copy-done.3, f32[]{:T(128)} %bitcast.6, bf16[640,1024]{0,1:T(8,128)(2,1)} %bitcast.98, bf16[1,640,512]{2,1,0:T(8,128)(2,1)S(1)} %copy-done), kind=kOutput, calls=%fused_computation | convolution fusion | flops 672661504 | bytes 5111812 | tf_op jit(solution)/shard_map/dot_general | solution.py:59
  18.1 2.9 %collective-permute-start.1 = (f16[272,512]{1,0:T(8,128)(2,1)}, f16[272,512]{1,0:T(8,128)(2,1)}, u32[]{:S(2)}, u32[]{:S(2)}) collective-permute-start(f16[272,512]{1,0:T(8,128)(2,1)} %concatenate.25), channel_id=1, source_target_pairs={{0,2},{1,3},{2,0},{3,1},{4,6},{5,7},{6,4},{7,5},{8,10},{9,11},{10,... | collective-permute-start | bytes 835592 | tf_op jit(solution)/shard_map/ppermute | solution.py:10
  21.8 2.6 %collective-permute-start.2 = (f16[272,512]{1,0:T(8,128)(2,1)}, f16[272,512]{1,0:T(8,128)(2,1)}, u32[]{:S(2)}, u32[]{:S(2)}) collective-permute-start(f16[272,512]{1,0:T(8,128)(2,1)} %concatenate.26), channel_id=1, source_target_pairs={{0,4},{1,5},{2,6},{3,7},{4,0},{5,1},{6,2},{7,3},{8,12},{9,13},{10,... | collective-permute-start | bytes 835592 | tf_op jit(solution)/shard_map/ppermute | solution.py:10
  24.5 8.8 %collective-permute-done.1 = f16[272,512]{1,0:T(8,128)(2,1)} collective-permute-done((f16[272,512]{1,0:T(8,128)(2,1)}, f16[272,512]{1,0:T(8,128)(2,1)}, u32[]{:S(2)}, u32[]{:S(2)}) %collective-permute-start.1) | collective-permute-done | bytes 278560 | tf_op jit(solution)/shard_map/ppermute | solution.py:10
  33.3 1.2 slice.67
  35.2 9.3 %collective-permute-done.2 = f16[272,512]{1,0:T(8,128)(2,1)} collective-permute-done((f16[272,512]{1,0:T(8,128)(2,1)}, f16[272,512]{1,0:T(8,128)(2,1)}, u32[]{:S(2)}, u32[]{:S(2)}) %collective-permute-start.2) | collective-permute-done | bytes 278560 | tf_op jit(solution)/shard_map/ppermute | solution.py:10
  44.5 1.2 slice.69
  46.4 1.2 slice.71
  48.3 2.0 %abs_reduce_fusion.4 = (f32[]{:T(128)}, f32[256,512]{1,0:T(8,128)S(1)}) fusion(f32[]{:T(128)} %bitcast.14, f16[272,512]{1,0:T(8,128)(2,1)} %collective-permute-done.3, f32[]{:T(128)} %bitcast.12, f16[272,512]{1,0:T(8,128)(2,1)} %collective-permute-done.2, f32[]{:T(128)} %bitcast.10, f16[272,512]{1,0:T(8,128)(2,1)} %collective-permute-done.1, ...), kind=kLoop, calls=%fused_computation.45 | loop fusion | flops 1441791 | bytes 1835028 | tf_op jit(solution)/shard_map/reduce_max | solution.py:14
  51.2 1.6 %collective-permute-start.4 = (f16[272,512]{1,0:T(8,128)(2,1)S(1)}, f16[272,512]{1,0:T(8,128)(2,1)S(1)}, u32[]{:S(2)}, u32[]{:S(2)}) collective-permute-start(f16[272,512]{1,0:T(8,128)(2,1)S(1)} %concatenate.28), channel_id=1, source_target_pairs={{0,8},{8,0},{16,24},{24,16},{1,9},{9,1},{17,25},{25,17},{2,10},{10... | collective-permute-start | bytes 835592 | tf_op jit(solution)/shard_map/ppermute | solution.py:10
  53.3 1.5 %collective-permute-start.5 = (f32[256]{0:T(256)S(1)}, f32[256]{0:T(256)S(1)}, u32[]{:S(2)}, u32[]{:S(2)}) collective-permute-start(f32[256]{0:T(256)S(1)} %bitcast.107), channel_id=1, source_target_pairs={{0,8},{8,0},{16,24},{24,16},{1,9},{9,1},{17,25},{25,17},{2,10},{10... | collective-permute-start | bytes 3080 | tf_op jit(solution)/shard_map/ppermute | solution.py:10
  54.8 3.0 %collective-permute-done.4 = f16[272,512]{1,0:T(8,128)(2,1)S(1)} collective-permute-done((f16[272,512]{1,0:T(8,128)(2,1)S(1)}, f16[272,512]{1,0:T(8,128)(2,1)S(1)}, u32[]{:S(2)}, u32[]{:S(2)}) %collective-permute-start.4) | collective-permute-done | bytes 278560 | tf_op jit(solution)/shard_map/ppermute | solution.py:10
  59.0 0.9 abs_reduce_fusion.3
  60.7 1.6 %collective-permute-start.7 = (f16[272,512]{1,0:T(8,128)(2,1)S(1)}, f16[272,512]{1,0:T(8,128)(2,1)S(1)}, u32[]{:S(2)}, u32[]{:S(2)}) collective-permute-start(f16[272,512]{1,0:T(8,128)(2,1)S(1)} %concatenate.29), channel_id=1, source_target_pairs={{0,16},{8,24},{16,0},{24,8},{1,17},{9,25},{17,1},{25,9},{2,18},{10... | collective-permute-start | bytes 835592 | tf_op jit(solution)/shard_map/ppermute | solution.py:10
  62.3 5.0 %collective-permute-done.7 = f16[272,512]{1,0:T(8,128)(2,1)S(1)} collective-permute-done((f16[272,512]{1,0:T(8,128)(2,1)S(1)}, f16[272,512]{1,0:T(8,128)(2,1)S(1)}, u32[]{:S(2)}, u32[]{:S(2)}) %collective-permute-start.7) | collective-permute-done | bytes 278560 | tf_op jit(solution)/shard_map/ppermute | solution.py:10
  68.4 1.5 %convolution_convert_fusion = bf16[256,512]{1,0:T(8,128)(2,1)S(1)} fusion(bf16[1,512,512]{2,1,0:T(8,128)(2,1)} %param.9, f32[256,512]{1,0:T(8,128)S(1)} %get-tuple-element.13, f16[272,512]{1,0:T(8,128)(2,1)S(1)} %collective-permute-done.7, f32[]{:T(128)} %bitcast.18, f32[512]{0:T(512)S(1)} %get-tuple-element.20, f32[256]{0:T(256)S(1)} %get-tuple-element.22, ...), kind=kOutput, calls=%fused_computation.10 | convolution fusion | flops 136052736 | bytes 1841162 | tf_op jit(solution)/shard_map/dot_general | solution.py:78
  69.9 5.8 %collective-permute-start.11 = (bf16[256,512]{1,0:T(8,128)(2,1)S(1)}, bf16[256,512]{1,0:T(8,128)(2,1)S(1)}, u32[]{:S(2)}, u32[]{:S(2)}) collective-permute-start(bf16[256,512]{1,0:T(8,128)(2,1)S(1)} %convolution_convert_fusion), channel_id=1, source_target_pairs={{0,4},{1,5},{2,6},{3,7},{4,0},{5,1},{6,2},{7,3},{8,12},{9,13},{10,... | collective-permute-start | bytes 786440 | tf_op jit(solution)/shard_map/ppermute | solution.py:10
  75.7 1.5 %copy.7 = bf16[1,256,2048]{1,2,0:T(8,128)(2,1)S(1)} copy(bf16[1,256,2048]{2,1,0:T(8,128)(2,1)} %param.8) | data formatting | bytes 2097152 | tf_op args[2]
  77.4 1.5 %collective-permute-start.13 = (bf16[256,512]{1,0:T(8,128)(2,1)S(1)}, bf16[256,512]{1,0:T(8,128)(2,1)S(1)}, u32[]{:S(2)}, u32[]{:S(2)}) collective-permute-start(bf16[256,512]{1,0:T(8,128)(2,1)S(1)} %convolution_convert_fusion), channel_id=1, source_target_pairs={{0,6},{1,7},{2,4},{3,5},{4,2},{5,3},{6,0},{7,1},{8,14},{9,15},{10,... | collective-permute-start | bytes 786440 | tf_op jit(solution)/shard_map/ppermute | solution.py:10
  79.1 7.7 %collective-permute-done.11 = bf16[256,512]{1,0:T(8,128)(2,1)S(1)} collective-permute-done((bf16[256,512]{1,0:T(8,128)(2,1)S(1)}, bf16[256,512]{1,0:T(8,128)(2,1)S(1)}, u32[]{:S(2)}, u32[]{:S(2)}) %collective-permute-start.11) | collective-permute-done | bytes 262176 | tf_op jit(solution)/shard_map/ppermute | solution.py:10
  87.1 7.9 %collective-permute-done.9 = bf16[256,512]{1,0:T(8,128)(2,1)S(1)} collective-permute-done((bf16[256,512]{1,0:T(8,128)(2,1)S(1)}, bf16[256,512]{1,0:T(8,128)(2,1)S(1)}, u32[]{:S(2)}, u32[]{:S(2)}) %collective-permute-start.9) | collective-permute-done | bytes 262176 | tf_op jit(solution)/shard_map/ppermute | solution.py:10
  97.0 0.9 abs_reduce_fusion.2
  98.9 1.6 %collective-permute-start.15 = (f16[272,512]{1,0:T(8,128)(2,1)S(1)}, f16[272,512]{1,0:T(8,128)(2,1)S(1)}, u32[]{:S(2)}, u32[]{:S(2)}) collective-permute-start(f16[272,512]{1,0:T(8,128)(2,1)S(1)} %concatenate.30), channel_id=1, source_target_pairs={{0,8},{8,0},{16,24},{24,16},{1,9},{9,1},{17,25},{25,17},{2,10},{10... | collective-permute-start | bytes 835592 | tf_op jit(solution)/shard_map/ppermute | solution.py:10
  100.4 7.2 %collective-permute-done.15 = f16[272,512]{1,0:T(8,128)(2,1)S(1)} collective-permute-done((f16[272,512]{1,0:T(8,128)(2,1)S(1)}, f16[272,512]{1,0:T(8,128)(2,1)S(1)}, u32[]{:S(2)}, u32[]{:S(2)}) %collective-permute-start.15) | collective-permute-done | bytes 278560 | tf_op jit(solution)/shard_map/ppermute | solution.py:10
  108.8 0.9 abs_reduce_fusion.1
  110.6 1.6 %collective-permute-start.16 = (f16[272,512]{1,0:T(8,128)(2,1)S(1)}, f16[272,512]{1,0:T(8,128)(2,1)S(1)}, u32[]{:S(2)}, u32[]{:S(2)}) collective-permute-start(f16[272,512]{1,0:T(8,128)(2,1)S(1)} %concatenate.31), channel_id=1, source_target_pairs={{0,16},{8,24},{16,0},{24,8},{1,17},{9,25},{17,1},{25,9},{2,18},{10... | collective-permute-start | bytes 835592 | tf_op jit(solution)/shard_map/ppermute | solution.py:10
  112.1 6.4 %collective-permute-done.16 = f16[272,512]{1,0:T(8,128)(2,1)S(1)} collective-permute-done((f16[272,512]{1,0:T(8,128)(2,1)S(1)}, f16[272,512]{1,0:T(8,128)(2,1)S(1)}, u32[]{:S(2)}, u32[]{:S(2)}) %collective-permute-start.16) | collective-permute-done | bytes 278560 | tf_op jit(solution)/shard_map/ppermute | solution.py:10
  119.7 0.9 fusion.23
  (53 shorter events, 10.1 us)
Async XLA Ops:
  0.0 4.5 %copy-start = (bf16[1,640,512]{2,1,0:T(8,128)(2,1)S(1)}, bf16[1,640,512]{2,1,0:T(8,128)(2,1)}, u32[]{:S(2)}) copy-start(bf16[1,640,512]{2,1,0:T(8,128)(2,1)} %param.7) | copy-start | bytes 1966084
  7.5 2.8 %collective-permute-start = (f16[1040,512]{1,0:T(8,128)(2,1)S(1)}, f16[1040,512]{1,0:T(8,128)(2,1)S(1)}, u32[]{:S(2)}, u32[]{:S(2)}) collective-permute-start(f16[1040,512]{1,0:T(8,128)(2,1)S(1)} %concatenate.24), channel_id=1, source_target_pairs={{0,1},{1,0},{2,3},{3,2},{4,5},{5,4},{6,7},{7,6},{8,9},{9,8},{10,11... | collective-permute-start | bytes 3194888 | tf_op jit(solution)/shard_map/ppermute | solution.py:10
  10.3 1.3 %copy-start.3 = (f16[1040,512]{1,0:T(8,128)(2,1)}, f16[1040,512]{1,0:T(8,128)(2,1)S(1)}, u32[]{:S(2)}) copy-start(f16[1040,512]{1,0:T(8,128)(2,1)S(1)} %collective-permute-done) | copy-start | bytes 3194884
  18.1 15.2 %collective-permute-start.1 = (f16[272,512]{1,0:T(8,128)(2,1)}, f16[272,512]{1,0:T(8,128)(2,1)}, u32[]{:S(2)}, u32[]{:S(2)}) collective-permute-start(f16[272,512]{1,0:T(8,128)(2,1)} %concatenate.25), channel_id=1, source_target_pairs={{0,2},{1,3},{2,0},{3,1},{4,6},{5,7},{6,4},{7,5},{8,10},{9,11},{10,... | collective-permute-start | bytes 835592 | tf_op jit(solution)/shard_map/ppermute | solution.py:10
  21.0 31.7 %copy-start.1 = (f32[1,512]{1,0:T(1,128)S(1)}, f32[1,512]{1,0:T(1,128)}, u32[]{:S(2)}) copy-start(f32[1,512]{1,0:T(1,128)} %param.11) | copy-start | bytes 6148
  21.0 32.2 %copy-start.2 = (f32[1,256]{1,0:T(1,128)S(1)}, f32[1,256]{1,0:T(1,128)}, u32[]{:S(2)}) copy-start(f32[1,256]{1,0:T(1,128)} %param.10) | copy-start | bytes 3076
  21.8 22.7 %collective-permute-start.2 = (f16[272,512]{1,0:T(8,128)(2,1)}, f16[272,512]{1,0:T(8,128)(2,1)}, u32[]{:S(2)}, u32[]{:S(2)}) collective-permute-start(f16[272,512]{1,0:T(8,128)(2,1)} %concatenate.26), channel_id=1, source_target_pairs={{0,4},{1,5},{2,6},{3,7},{4,0},{5,1},{6,2},{7,3},{8,12},{9,13},{10,... | collective-permute-start | bytes 835592 | tf_op jit(solution)/shard_map/ppermute | solution.py:10
  24.4 21.9 %collective-permute-start.3 = (f16[272,512]{1,0:T(8,128)(2,1)S(1)}, f16[272,512]{1,0:T(8,128)(2,1)}, u32[]{:S(2)}, u32[]{:S(2)}) collective-permute-start(f16[272,512]{1,0:T(8,128)(2,1)S(1)} %concatenate.27), channel_id=1, source_target_pairs={{0,6},{1,7},{2,4},{3,5},{4,2},{5,3},{6,0},{7,1},{8,14},{9,15},{10,... | collective-permute-start | bytes 835592 | tf_op jit(solution)/shard_map/ppermute | solution.py:10
  51.2 6.6 %collective-permute-start.4 = (f16[272,512]{1,0:T(8,128)(2,1)S(1)}, f16[272,512]{1,0:T(8,128)(2,1)S(1)}, u32[]{:S(2)}, u32[]{:S(2)}) collective-permute-start(f16[272,512]{1,0:T(8,128)(2,1)S(1)} %concatenate.28), channel_id=1, source_target_pairs={{0,8},{8,0},{16,24},{24,16},{1,9},{9,1},{17,25},{25,17},{2,10},{10... | collective-permute-start | bytes 835592 | tf_op jit(solution)/shard_map/ppermute | solution.py:10
  52.7 6.3 %collective-permute-start.6 = (f32[512]{0:T(512)S(1)}, f32[512]{0:T(512)S(1)}, u32[]{:S(2)}, u32[]{:S(2)}) collective-permute-start(f32[512]{0:T(512)S(1)} %bitcast.100), channel_id=1, source_target_pairs={{0,8},{8,0},{16,24},{24,16},{1,9},{9,1},{17,25},{25,17},{2,10},{10... | collective-permute-start | bytes 6152 | tf_op jit(solution)/shard_map/ppermute | solution.py:10
  53.3 5.7 %collective-permute-start.5 = (f32[256]{0:T(256)S(1)}, f32[256]{0:T(256)S(1)}, u32[]{:S(2)}, u32[]{:S(2)}) collective-permute-start(f32[256]{0:T(256)S(1)} %bitcast.107), channel_id=1, source_target_pairs={{0,8},{8,0},{16,24},{24,16},{1,9},{9,1},{17,25},{25,17},{2,10},{10... | collective-permute-start | bytes 3080 | tf_op jit(solution)/shard_map/ppermute | solution.py:10
  60.7 6.6 %collective-permute-start.7 = (f16[272,512]{1,0:T(8,128)(2,1)S(1)}, f16[272,512]{1,0:T(8,128)(2,1)S(1)}, u32[]{:S(2)}, u32[]{:S(2)}) collective-permute-start(f16[272,512]{1,0:T(8,128)(2,1)S(1)} %concatenate.29), channel_id=1, source_target_pairs={{0,16},{8,24},{16,0},{24,8},{1,17},{9,25},{17,1},{25,9},{2,18},{10... | collective-permute-start | bytes 835592 | tf_op jit(solution)/shard_map/ppermute | solution.py:10
  69.9 16.9 %collective-permute-start.11 = (bf16[256,512]{1,0:T(8,128)(2,1)S(1)}, bf16[256,512]{1,0:T(8,128)(2,1)S(1)}, u32[]{:S(2)}, u32[]{:S(2)}) collective-permute-start(bf16[256,512]{1,0:T(8,128)(2,1)S(1)} %convolution_convert_fusion), channel_id=1, source_target_pairs={{0,4},{1,5},{2,6},{3,7},{4,0},{5,1},{6,2},{7,3},{8,12},{9,13},{10,... | collective-permute-start | bytes 786440 | tf_op jit(solution)/shard_map/ppermute | solution.py:10
  77.2 18.5 %collective-permute-start.8 = (bf16[256,512]{1,0:T(8,128)(2,1)S(1)}, bf16[256,512]{1,0:T(8,128)(2,1)S(1)}, u32[]{:S(2)}, u32[]{:S(2)}) collective-permute-start(bf16[256,512]{1,0:T(8,128)(2,1)S(1)} %convolution_convert_fusion), channel_id=1, source_target_pairs={{0,1},{1,0},{2,3},{3,2},{4,5},{5,4},{6,7},{7,6},{8,9},{9,8},{10,11... | collective-permute-start | bytes 786440 | tf_op jit(solution)/shard_map/ppermute | solution.py:10
  77.3 17.7 %collective-permute-start.9 = (bf16[256,512]{1,0:T(8,128)(2,1)S(1)}, bf16[256,512]{1,0:T(8,128)(2,1)S(1)}, u32[]{:S(2)}, u32[]{:S(2)}) collective-permute-start(bf16[256,512]{1,0:T(8,128)(2,1)S(1)} %convolution_convert_fusion), channel_id=1, source_target_pairs={{0,2},{1,3},{2,0},{3,1},{4,6},{5,7},{6,4},{7,5},{8,10},{9,11},{10,... | collective-permute-start | bytes 786440 | tf_op jit(solution)/shard_map/ppermute | solution.py:10
  77.4 17.6 %collective-permute-start.13 = (bf16[256,512]{1,0:T(8,128)(2,1)S(1)}, bf16[256,512]{1,0:T(8,128)(2,1)S(1)}, u32[]{:S(2)}, u32[]{:S(2)}) collective-permute-start(bf16[256,512]{1,0:T(8,128)(2,1)S(1)} %convolution_convert_fusion), channel_id=1, source_target_pairs={{0,6},{1,7},{2,4},{3,5},{4,2},{5,3},{6,0},{7,1},{8,14},{9,15},{10,... | collective-permute-start | bytes 786440 | tf_op jit(solution)/shard_map/ppermute | solution.py:10
  87.0 9.8 %collective-permute-start.12 = (bf16[256,512]{1,0:T(8,128)(2,1)S(1)}, bf16[256,512]{1,0:T(8,128)(2,1)S(1)}, u32[]{:S(2)}, u32[]{:S(2)}) collective-permute-start(bf16[256,512]{1,0:T(8,128)(2,1)S(1)} %collective-permute-done.11), channel_id=1, source_target_pairs={{0,1},{1,0},{2,3},{3,2},{4,5},{5,4},{6,7},{7,6},{8,9},{9,8},{10,11... | collective-permute-start | bytes 786440 | tf_op jit(solution)/shard_map/ppermute | solution.py:10
  94.9 1.5 %collective-permute-start.10 = (bf16[256,512]{1,0:T(8,128)(2,1)S(1)}, bf16[256,512]{1,0:T(8,128)(2,1)S(1)}, u32[]{:S(2)}, u32[]{:S(2)}) collective-permute-start(bf16[256,512]{1,0:T(8,128)(2,1)S(1)} %collective-permute-done.9), channel_id=1, source_target_pairs={{0,1},{1,0},{2,3},{3,2},{4,5},{5,4},{6,7},{7,6},{8,9},{9,8},{10,11... | collective-permute-start | bytes 786440 | tf_op jit(solution)/shard_map/ppermute | solution.py:10
  95.0 2.1 %collective-permute-start.14 = (bf16[256,512]{1,0:T(8,128)(2,1)S(1)}, bf16[256,512]{1,0:T(8,128)(2,1)S(1)}, u32[]{:S(2)}, u32[]{:S(2)}) collective-permute-start(bf16[256,512]{1,0:T(8,128)(2,1)S(1)} %collective-permute-done.13), channel_id=1, source_target_pairs={{0,1},{1,0},{2,3},{3,2},{4,5},{5,4},{6,7},{7,6},{8,9},{9,8},{10,11... | collective-permute-start | bytes 786440 | tf_op jit(solution)/shard_map/ppermute | solution.py:10
  98.9 8.8 %collective-permute-start.15 = (f16[272,512]{1,0:T(8,128)(2,1)S(1)}, f16[272,512]{1,0:T(8,128)(2,1)S(1)}, u32[]{:S(2)}, u32[]{:S(2)}) collective-permute-start(f16[272,512]{1,0:T(8,128)(2,1)S(1)} %concatenate.30), channel_id=1, source_target_pairs={{0,8},{8,0},{16,24},{24,16},{1,9},{9,1},{17,25},{25,17},{2,10},{10... | collective-permute-start | bytes 835592 | tf_op jit(solution)/shard_map/ppermute | solution.py:10
  110.6 7.9 %collective-permute-start.16 = (f16[272,512]{1,0:T(8,128)(2,1)S(1)}, f16[272,512]{1,0:T(8,128)(2,1)S(1)}, u32[]{:S(2)}, u32[]{:S(2)}) collective-permute-start(f16[272,512]{1,0:T(8,128)(2,1)S(1)} %concatenate.31), channel_id=1, source_target_pairs={{0,16},{8,24},{16,0},{24,8},{1,17},{9,25},{17,1},{25,9},{2,18},{10... | collective-permute-start | bytes 835592 | tf_op jit(solution)/shard_map/ppermute | solution.py:10

commit v2 on v0

v2 whole, which is shorter than its diff:
```python
import functools

import jax
import jax.numpy as jnp
from jax import lax
from jax.experimental import pallas as pl
from jax.experimental.pallas import tpu as pltpu
from jax.sharding import PartitionSpec as P

TAIL = 16
LIFT = 2.0**15
TINY = 1e-30
F32, BF16 = jnp.float32, jnp.bfloat16
VMEM = pl.BlockSpec(memory_space=pltpu.VMEM)
SMEM = pl.BlockSpec(memory_space=pltpu.SMEM)


def exchange(x, axis, flip):
    return lax.ppermute(x, axis, [(i, i ^ flip) for i in range(lax.axis_size(axis))])


def put(ref, value):
    rows = value.shape[0]
    top = jnp.max(jnp.max(jnp.abs(value), axis=0, keepdims=True), axis=1, keepdims=True)
    top = jnp.maximum(jnp.broadcast_to(top, (1, value.shape[1])), TINY).astype(BF16).astype(F32)
    ref[rows:, :] = jnp.broadcast_to(top, (TAIL, value.shape[1])).astype(BF16)
    z = value * (LIFT / top)
    z2 = z * z
    z4 = z2 * z2
    z8 = z4 * z4
    ref[:rows, :] = jnp.where(z < 0, -z8, z8).astype(BF16)


def get(ref):
    rows = ref.shape[0] - TAIL
    top = ref[rows:, :][:1, :].astype(F32) * (1.0 / LIFT)
    y = ref[:rows, :].astype(F32)
    square = lax.rsqrt(lax.rsqrt(jnp.abs(y) + 1e-37))
    size = square * lax.rsqrt(square)
    return jnp.where(y < 0, -size, size) * top


def partial_kernel(pick_ref, grads_ref, inputs_ref, out_ref, turned_ref):
    @pl.when(pl.program_id(0) == 0)
    def _():
        turned_ref[...] = grads_ref[0].T

    put(out_ref.at[0], jnp.dot(turned_ref[...], inputs_ref[0], preferred_element_type=F32))


def own_kernel(pick_ref, turned_ref, inputs_ref, out_ref):
    out_ref[0] = jnp.dot(turned_ref[...], inputs_ref[0], preferred_element_type=F32)


def pair_sum_kernel(send, at_ref, own_ref, message_ref, out_ref):
    at = at_ref[0]
    total = own_ref[at] + get(message_ref.at[at])
    if send:
        put(out_ref, total)
    else:
        out_ref[...] = total


def chip_sum_kernel(*refs):
    grad_ref, messages, out_ref, sent_ref = refs[0], refs[1:-2], refs[-2], refs[-1]
    total = grad_ref[...]
    for message in messages:
        total = total + get(message)
    out_ref[...] = total
    put(sent_ref, total)


def step_kernel(value_ref, total_ref, message_ref, a0, a1, b0, b1, c0, c1, value_out, total_out, sent_ref):
    got = get(message_ref)
    value_out[...] = value_ref[...] + (c0[...] * c1[...]) * got
    total = (a0[...] * a1[...]) * total_ref[...] + (b0[...] * b1[...]) * got
    total_out[...] = total
    put(sent_ref, total)


def side_s_kernel(value_ref, message_ref, c0, c1, s_ref, out_ref):
    upper = value_ref[...] + (c0[...] * c1[...]) * get(message_ref)
    out_ref[...] = jnp.dot(s_ref[...], upper.astype(BF16), preferred_element_type=F32).astype(BF16)


def side_a_kernel(*refs):
    at_ref, a_ref, parts = refs[0], refs[1], refs[2:-5]
    r0, r1, solved_ref, total_ref, sent_ref = refs[-5:]
    rows = a_ref.shape[0]
    solved = None
    for i, part in enumerate(parts):
        columns = a_ref[:, pl.ds(pl.multiple_of(at_ref[i] * rows, rows), rows)]
        term = lax.dot_general(part[...], columns, (((1,), (1,)), ((), ())), preferred_element_type=F32)
        solved = term if solved is None else solved + term
    solved_ref[...] = solved
    total = (r0[...] * r1[...]) * solved
    total_ref[...] = total
    put(sent_ref, total)


def last_kernel(value_ref, message_ref, c0, c1, out_ref):
    lower = value_ref[...] + (c0[...] * c1[...]) * get(message_ref)
    out_ref[0] = lower.T.astype(BF16)


def shards(activations, out_grads, a_inverse, s_inverse, in_decay, out_decay):
    layers, peers = lax.axis_size("layer"), lax.axis_size("dp")
    layer, here = lax.axis_index("layer"), lax.axis_index("dp")
    core, chip = here % 2, here // 2
    chips = peers // 2
    rows = a_inverse.shape[1]
    width = out_grads.shape[2]
    tokens = activations.shape[1]
    params = pltpu.CompilerParams(vmem_limit_bytes=32 * 2**20)
    grid_shape = jax.ShapeDtypeStruct((width, rows), F32)
    low_shape = jax.ShapeDtypeStruct((width, rows), BF16)
    sent_shape = jax.ShapeDtypeStruct((width + TAIL, rows), BF16)

    def call(kernel, out_shape, *operands, scalars=0, name=None):
        several = isinstance(out_shape, (list, tuple))
        return pl.pallas_call(
            kernel,
            out_shape=out_shape,
            in_specs=[SMEM] * scalars + [VMEM] * (len(operands) - scalars),
            out_specs=[VMEM] * len(out_shape) if several else VMEM,
            compiler_params=params,
            name=name,
        )(*operands)

    rates = jnp.concatenate([out_decay[0], in_decay[0]])
    ones, zeros = jnp.ones_like(rates), jnp.zeros_like(rates)

    def factors(r):
        return r[:width].reshape(width, 1), r[width:].reshape(1, rows)

    steps = []
    own, below, above = rates, rates, ones
    flip = 1
    while flip < layers:
        other = exchange(own, "layer", flip)
        high = (layer & flip) != 0
        up = (jnp.where(high, other, ones), jnp.where(high, ones, own), jnp.where(high, zeros, below))
        down = (jnp.where(high, ones, other), jnp.where(high, own, ones), jnp.where(high, above, zeros))
        steps.append((flip, [f for r in up for f in factors(r)], [f for r in down for f in factors(r)]))
        above = jnp.where(high, above * other, above)
        below = jnp.where(high, below, below * other)
        own = own * other
        flip *= 2

    def blocks(kernel, of, lead, lead_spec, out_shape, out_specs):
        return pl.pallas_call(
            kernel,
            grid_spec=pltpu.PrefetchScalarGridSpec(
                num_scalar_prefetch=1,
                grid=(chips,),
                in_specs=[lead_spec, pl.BlockSpec((1, tokens, rows), lambda i, pick: (0, 0, 2 * i + pick[0]))],
                out_specs=out_specs,
            ),
            out_shape=out_shape,
            compiler_params=params,
        )(of.reshape(1).astype(jnp.int32), lead, activations)

    message, turned = blocks(
        partial_kernel,
        1 - core,
        out_grads,
        pl.BlockSpec((1, tokens, width), lambda i, pick: (0, 0, 0)),
        [jax.ShapeDtypeStruct((chips, width + TAIL, rows), BF16), jax.ShapeDtypeStruct((width, tokens), BF16)],
        [
            pl.BlockSpec((1, width + TAIL, rows), lambda i, pick: (i, 0, 0)),
            pl.BlockSpec((width, tokens), lambda i, pick: (0, 0)),
        ],
    )
    theirs = exchange(message, "dp", 1)
    mine = blocks(
        own_kernel,
        core,
        turned,
        pl.BlockSpec((width, tokens), lambda i, pick: (0, 0)),
        jax.ShapeDtypeStruct((chips, width, rows), F32),
        pl.BlockSpec((1, width, rows), lambda i, pick: (i, 0, 0)),
    )

    def pair_sum(flip):
        at = (chip ^ flip).reshape(1).astype(jnp.int32)
        kernel = functools.partial(pair_sum_kernel, flip != 0)
        return call(kernel, sent_shape if flip else grid_shape, at, mine, theirs, scalars=1)

    arrived = [exchange(pair_sum(flip), "dp", 2 * flip) for flip in range(1, chips)]
    value, sent = call(chip_sum_kernel, [grid_shape, sent_shape], pair_sum(0), *arrived)

    total = value
    for flip, up, _ in steps[:-1]:
        value, total, sent = call(
            step_kernel, [grid_shape, grid_shape, sent_shape], value, total, exchange(sent, "layer", flip), *up
        )
    flip, up, _ = steps[-1]
    s_applied = call(side_s_kernel, low_shape, value, exchange(sent, "layer", flip), *up[4:], s_inverse[0].T)

    parts, places = [], []
    for flip in range(chips):
        part = exchange(s_applied, "dp", 2 * flip) if flip else s_applied
        parts += [part, exchange(part, "dp", 1)]
        places += [2 * (chip ^ flip) + core, 2 * (chip ^ flip) + 1 - core]
    value, total, sent = call(
        side_a_kernel,
        [grid_shape, grid_shape, sent_shape],
        jnp.stack(places).astype(jnp.int32),
        a_inverse[0],
        *parts,
        *factors(rates),
        scalars=1,
    )

    for flip, _, down in steps[:-1]:
        value, total, sent = call(
            step_kernel, [grid_shape, grid_shape, sent_shape], value, total, exchange(sent, "layer", flip), *down
        )
    flip, _, down = steps[-1]
    return call(
        last_kernel, jax.ShapeDtypeStruct((1, rows, width), BF16), value, exchange(sent, "layer", flip), *down[4:]
    )


def solution(mesh):
    placed = (
        P("layer", "dp", None),
        P("layer", "dp", None),
        P("layer", "dp", None),
        P("layer", None, None),
        P("layer", "dp"),
        P("layer", None),
    )
    return jax.shard_map(
        shards, mesh=mesh, in_specs=placed, out_specs=P("layer", "dp", None), check_vma=False
    )
```

time: 191 us -> 108 us (0.57)
  waiting for transfers between devices: 136 us -> 62.2 us
  starting transfers between devices: 0.12 us -> 16.6 us
  blocking collectives: 16.1 us -> 0 us
  Pallas kernels: 0 us -> 14.5 us
  between operations: 13.2 us -> 0.29 us
  other arithmetic: 11.4 us -> 0.02 us
  local copies, waits for them, and re-layouts: 1.89 us -> 12.7 us
  matrix products: 10.7 us -> 0 us
    all_gather x3 -> x0, waiting for transfers between devices: 83.3 us -> none  [the longest x2 54.1 us: prefix(): everything = jax.tree.map(lambda part: lax.all_gather(part, axis), shard)]
    ppermute x0 -> x16, waiting for transfers between devices: none -> 62.2 us  [exchange(): lax.ppermute(x, axis, [(i, i ^ flip) for i in range(lax.axis_size(axis))])]
    reduce_scatter x1 -> x0, waiting for transfers between devices: 52.8 us -> none  [shards(): lax.psum_scatter(lax.dot_general(window_cols, grads_here, contract, prefe...]
    ppermute x0 -> x16, starting transfers between devices: none -> 16.6 us  [exchange(): lax.ppermute(x, axis, [(i, i ^ flip) for i in range(lax.axis_size(axis))])]
    all_gather x2 -> x0, blocking collectives: 16.1 us -> none  [prefix(): everything = jax.tree.map(lambda part: lax.all_gather(part, axis), shard)]
    pallas_call x0 -> x12, Pallas kernels: none -> 14.5 us  [the longest x10 9.59 us: call(): pl.pallas_call(kernel, out_shape=out_shape, in_specs=[SMEM] * scalars + [...]
    dot_general x3 -> x0, matrix products: 10.7 us -> none  [the longest x1 4.88 us: shards(): lax.dot_general(window_cols, grads_here, contract, preferred_element_type...]
    unnamed x8 -> x31, local copies, waits for them, and re-layouts: 1.75 us -> 11.4 us
  transfers between devices with their start and end apart: 4 -> 16, of which waited for: 4 -> 8; matrix products, arithmetic and copies ran while one was open for 0% -> 1% of each run, Pallas kernels for 0% -> 3%
where the time goes in v2:
time: 108 us; the launch traced here: 106 us
  waiting for transfers between devices  62.2 us (58%)
  starting transfers between devices  16.6 us (15%)
  Pallas kernels  14.5 us (13%)
  local copies, waits for them, and re-layouts  12.7 us (12%)
    ppermute x16, waiting for transfers between devices, exchange(): lax.ppermute(x, axis, [(i, i ^ flip) for i in range(lax.axis_size(axis))])  62.2 us
    ppermute x16, starting transfers between devices, exchange(): lax.ppermute(x, axis, [(i, i ^ flip) for i in range(lax.axis_size(axis))])  16.6 us
    unnamed x31, local copies, waits for them, and re-layouts  11.4 us
    pallas_call x10, Pallas kernels, call(): pl.pallas_call(kernel, out_shape=out_shape, in_specs=[SMEM] * scalars + [...  9.59 us
    pallas_call x2, Pallas kernels, blocks(): pl.pallas_call(kernel, grid_spec=pltpu.PrefetchScalarGridSpec(num_scalar_...  4.93 us
  transfers between devices with their start and end apart: 16, of which 8 were waited for; matrix products, arithmetic and copies ran while one was open for 1% of the time, Pallas kernels for 3%

profile of v2, /device:TPU:0, one launch (start us, length us, event | category | flops | bytes accessed | tf_op | source)
XLA Modules:
  0.0 106.4 jit_solution(6980098261765479108)
XLA Ops:
  0.0 1.7 %copy-done = bf16[1,640,2048]{2,1,0:T(8,128)(2,1)S(1)} copy-done((bf16[1,640,2048]{2,1,0:T(8,128)(2,1)S(1)}, bf16[1,640,2048]{2,1,0:T(8,128)(2,1)}, u32[]{:S(2)}) %copy-start) | copy-done | bytes 2621464
  1.7 1.1 %copy-done.3 = bf16[1,640,512]{2,1,0:T(8,128)(2,1)S(1)} copy-done((bf16[1,640,512]{2,1,0:T(8,128)(2,1)S(1)}, bf16[1,640,512]{2,1,0:T(8,128)(2,1)}, u32[]{:S(2)}) %copy-start.3) | copy-done | bytes 655384
  2.8 3.2 %shard_map.64 = (bf16[4,528,256]{2,1,0:T(8,128)(2,1)S(1)}, bf16[512,640]{1,0:T(8,128)(2,1)S(1)}) custom-call(s32[1]{0:T(128)} %bitcast.11.pick_ref, bf16[1,640,512]{2,1,0:T(8,128)(2,1)S(1)} %copy-done.3, bf16[1,640,2048]{2,1,0:T(8,128)(2,1)S(1)} %copy-done), custom_call_target="tpu_custom_call" | custom-call | tf_op jit(solution)/shard_map/pallas_call | solution.py:151
  6.5 1.7 %copy-done.1 = bf16[1,640,2048]{2,1,0:T(8,128)(2,1)S(1)} copy-done((bf16[1,640,2048]{2,1,0:T(8,128)(2,1)S(1)}, bf16[1,640,2048]{2,1,0:T(8,128)(2,1)}, u32[]{:S(2)}) %copy-start.1) | copy-done | bytes 2621464
  8.3 1.8 %shard_map.65.own_ref = f32[4,512,256]{2,1,0:T(8,128)S(1)} custom-call(s32[1]{0:T(128)} %bitcast.10.pick_ref, bf16[512,640]{1,0:T(8,128)(2,1)S(1)} %get-tuple-element.16.turned_ref, bf16[1,640,2048]{2,1,0:T(8,128)(2,1)S(1)} %copy-done.1), custom_call_target="tpu_custom_call" | custom-call | tf_op jit(solution)/shard_map/pallas_call | solution.py:151
  10.6 4.7 %collective-permute-start.3 = (bf16[528,256]{1,0:T(8,128)(2,1)S(1)}, bf16[528,256]{1,0:T(8,128)(2,1)S(1)}, u32[]{:S(2)}, u32[]{:S(2)}) collective-permute-start(bf16[528,256]{1,0:T(8,128)(2,1)S(1)} %shard_map.69), channel_id=1, source_target_pairs={{0,6},{1,7},{2,4},{3,5},{4,2},{5,3},{6,0},{7,1},{8,14},{9,15},{10,... | collective-permute-start | bytes 811016 | tf_op jit(solution)/shard_map/ppermute | solution.py:19
  17.4 5.4 %collective-permute-done.3.refs_3_ = bf16[528,256]{1,0:T(8,128)(2,1)S(1)} collective-permute-done((bf16[528,256]{1,0:T(8,128)(2,1)S(1)}, bf16[528,256]{1,0:T(8,128)(2,1)S(1)}, u32[]{:S(2)}, u32[]{:S(2)}) %collective-permute-start.3) | collective-permute-done | bytes 270368 | tf_op jit(solution)/shard_map/ppermute | solution.py:19
  22.8 16.2 %collective-permute-done.2.refs_2_ = bf16[528,256]{1,0:T(8,128)(2,1)S(1)} collective-permute-done((bf16[528,256]{1,0:T(8,128)(2,1)S(1)}, bf16[528,256]{1,0:T(8,128)(2,1)S(1)}, u32[]{:S(2)}, u32[]{:S(2)}) %collective-permute-start.2) | collective-permute-done | bytes 270368 | tf_op jit(solution)/shard_map/ppermute | solution.py:19
  38.9 1.3 %shard_map.70 = (f32[512,256]{1,0:T(8,128)S(1)}, bf16[528,256]{1,0:T(8,128)(2,1)S(1)}) custom-call(f32[512,256]{1,0:T(8,128)S(1)} %shard_map.66.refs_0_, bf16[528,256]{1,0:T(8,128)(2,1)S(1)} %collective-permute-done.1.refs_1_, bf16[528,256]{1,0:T(8,128)(2,1)S(1)} %collective-permute-done.2.refs_2_, bf16[528,256]{1,0:T(8,128)(2,1)S(1)} %collective-permute-done.3.refs_3_), custom_call_target="tpu_custom_call" | custom-call | tf_op jit(solution)/shard_map/pallas_call | solution.py:121
  40.3 1.6 %collective-permute-start.4 = (bf16[528,256]{1,0:T(8,128)(2,1)S(1)}, bf16[528,256]{1,0:T(8,128)(2,1)S(1)}, u32[]{:S(2)}, u32[]{:S(2)}) collective-permute-start(bf16[528,256]{1,0:T(8,128)(2,1)S(1)} %get-tuple-element.19), channel_id=1, source_target_pairs={{0,8},{8,0},{16,24},{24,16},{1,9},{9,1},{17,25},{25,17},{2,10},{10... | collective-permute-start | bytes 811016 | tf_op jit(solution)/shard_map/ppermute | solution.py:19
  42.5 6.1 %collective-permute-done.5 = f32[768]{0:T(1024)S(1)} collective-permute-done((f32[768]{0:T(1024)S(1)}, f32[768]{0:T(1024)S(1)}, u32[]{:S(2)}, u32[]{:S(2)}) %collective-permute-start.5) | collective-permute-done | bytes 3104 | tf_op jit(solution)/shard_map/ppermute | solution.py:19
  49.1 1.2 %shard_map.71 = (f32[512,256]{1,0:T(8,128)S(1)}, f32[512,256]{1,0:T(8,128)}, bf16[528,256]{1,0:T(8,128)(2,1)S(1)}) custom-call(f32[512,256]{1,0:T(8,128)S(1)} %get-tuple-element.18.value_ref.total_ref, f32[512,256]{1,0:T(8,128)S(1)} %get-tuple-element.18.value_ref.total_ref, bf16[528,256]{1,0:T(8,128)(2,1)S(1)} %collective-permute-done.4.message_ref, ...), custom_call_target="tpu_custom_call" | custom-call | tf_op jit(solution)/shard_map/pallas_call | solution.py:121
  50.3 1.5 %collective-permute-start.6 = (bf16[528,256]{1,0:T(8,128)(2,1)S(1)}, bf16[528,256]{1,0:T(8,128)(2,1)S(1)}, u32[]{:S(2)}, u32[]{:S(2)}) collective-permute-start(bf16[528,256]{1,0:T(8,128)(2,1)S(1)} %get-tuple-element.21), channel_id=1, source_target_pairs={{0,16},{8,24},{16,0},{24,8},{1,17},{9,25},{17,1},{25,9},{2,18},{10... | collective-permute-start | bytes 811016 | tf_op jit(solution)/shard_map/ppermute | solution.py:19
  52.2 5.3 %collective-permute-done.6.message_ref = bf16[528,256]{1,0:T(8,128)(2,1)S(1)} collective-permute-done((bf16[528,256]{1,0:T(8,128)(2,1)S(1)}, bf16[528,256]{1,0:T(8,128)(2,1)S(1)}, u32[]{:S(2)}, u32[]{:S(2)}) %collective-permute-start.6) | collective-permute-done | bytes 270368 | tf_op jit(solution)/shard_map/ppermute | solution.py:19
  58.1 2.5 %collective-permute-start.12 = (bf16[512,256]{1,0:T(8,128)(2,1)S(1)}, bf16[512,256]{1,0:T(8,128)(2,1)S(1)}, u32[]{:S(2)}, u32[]{:S(2)}) collective-permute-start(bf16[512,256]{1,0:T(8,128)(2,1)S(1)} %shard_map.72.refs_2_), channel_id=1, source_target_pairs={{0,6},{1,7},{2,4},{3,5},{4,2},{5,3},{6,0},{7,1},{8,14},{9,15},{10,... | collective-permute-start | bytes 786440 | tf_op jit(solution)/shard_map/ppermute | solution.py:19
  60.7 0.9 collective-permute-start.8
  61.6 14.7 %collective-permute-done.10.refs_6_ = bf16[512,256]{1,0:T(8,128)(2,1)S(1)} collective-permute-done((bf16[512,256]{1,0:T(8,128)(2,1)S(1)}, bf16[512,256]{1,0:T(8,128)(2,1)S(1)}, u32[]{:S(2)}, u32[]{:S(2)}) %collective-permute-start.10) | collective-permute-done | bytes 262176 | tf_op jit(solution)/shard_map/ppermute | solution.py:19
  76.8 0.8 collective-permute-done.8.refs_4_
  77.9 0.7 copy-done.4
  78.6 0.7 copy-done.6
  79.3 0.7 copy-done.8
  80.7 0.9 copy-done.5
  81.6 0.9 copy-done.7
  82.6 0.9 copy-done.9
  83.5 0.9 copy-done.11
  84.5 2.3 %shard_map.73 = (f32[512,256]{1,0:T(8,128)S(1)}, f32[512,256]{1,0:T(8,128)S(1)}, bf16[528,256]{1,0:T(8,128)(2,1)}) custom-call(s32[8]{0:T(128)S(1)} %stack.35.refs_0_, bf16[256,2048]{1,0:T(8,128)(2,1)S(1)} %bitcast.36, bf16[512,256]{1,0:T(8,128)(2,1)S(1)} %shard_map.72.refs_2_, bf16[512,256]{1,0:T(8,128)(2,1)S(1)} %copy-done.5, ...), custom_call_target="tpu_custom_call" | custom-call | tf_op jit(solution)/shard_map/pallas_call | solution.py:121
  86.8 1.5 %collective-permute-start.14 = (bf16[528,256]{1,0:T(8,128)(2,1)}, bf16[528,256]{1,0:T(8,128)(2,1)S(1)}, u32[]{:S(2)}, u32[]{:S(2)}) collective-permute-start(bf16[528,256]{1,0:T(8,128)(2,1)} %get-tuple-element.24), channel_id=1, source_target_pairs={{0,8},{8,0},{16,24},{24,16},{1,9},{9,1},{17,25},{25,17},{2,10},{10... | collective-permute-start | bytes 811016 | tf_op jit(solution)/shard_map/ppermute | solution.py:19
  88.6 7.3 %collective-permute-done.14.message_ref = bf16[528,256]{1,0:T(8,128)(2,1)S(1)} collective-permute-done((bf16[528,256]{1,0:T(8,128)(2,1)}, bf16[528,256]{1,0:T(8,128)(2,1)S(1)}, u32[]{:S(2)}, u32[]{:S(2)}) %collective-permute-start.14) | collective-permute-done | bytes 270368 | tf_op jit(solution)/shard_map/ppermute | solution.py:19
  95.9 1.2 %shard_map.74 = (f32[512,256]{1,0:T(8,128)S(1)}, f32[512,256]{1,0:T(8,128)}, bf16[528,256]{1,0:T(8,128)(2,1)S(1)}) custom-call(f32[512,256]{1,0:T(8,128)S(1)} %get-tuple-element.22.value_ref, f32[512,256]{1,0:T(8,128)S(1)} %get-tuple-element.23.total_ref, bf16[528,256]{1,0:T(8,128)(2,1)S(1)} %collective-permute-done.14.message_ref, f32[512,1]{1,0:T(8,128)S(1)} %copy.14.a0, ...), custom_call_target="tpu_custom_call" | custom-call | tf_op jit(solution)/shard_map/pallas_call | solution.py:121
  97.2 1.5 %collective-permute-start.15 = (bf16[528,256]{1,0:T(8,128)(2,1)S(1)}, bf16[528,256]{1,0:T(8,128)(2,1)S(1)}, u32[]{:S(2)}, u32[]{:S(2)}) collective-permute-start(bf16[528,256]{1,0:T(8,128)(2,1)S(1)} %get-tuple-element.26), channel_id=1, source_target_pairs={{0,16},{8,24},{16,0},{24,8},{1,17},{9,25},{17,1},{25,9},{2,18},{10... | collective-permute-start | bytes 811016 | tf_op jit(solution)/shard_map/ppermute | solution.py:19
  98.8 6.4 %collective-permute-done.15.message_ref = bf16[528,256]{1,0:T(8,128)(2,1)S(1)} collective-permute-done((bf16[528,256]{1,0:T(8,128)(2,1)S(1)}, bf16[528,256]{1,0:T(8,128)(2,1)S(1)}, u32[]{:S(2)}, u32[]{:S(2)}) %collective-permute-start.15) | collective-permute-done | bytes 270368 | tf_op jit(solution)/shard_map/ppermute | solution.py:19
  105.3 1.1 %shard_map.75 = bf16[1,256,512]{2,1,0:T(8,128)(2,1)} custom-call(f32[512,256]{1,0:T(8,128)S(1)} %get-tuple-element.25.value_ref, bf16[528,256]{1,0:T(8,128)(2,1)S(1)} %collective-permute-done.15.message_ref, f32[512,1]{1,0:T(8,128)S(1)} %copy.16.c0, f32[1,256]{1,0:T(1,128)S(1)} %bitcast.45), custom_call_target="tpu_custom_call" | custom-call | tf_op jit(solution)/shard_map/pallas_call | solution.py:121
  (70 shorter events, 7.1 us)
Async XLA Ops:
  0.0 1.7 %copy-start = (bf16[1,640,2048]{2,1,0:T(8,128)(2,1)S(1)}, bf16[1,640,2048]{2,1,0:T(8,128)(2,1)}, u32[]{:S(2)}) copy-start(bf16[1,640,2048]{2,1,0:T(8,128)(2,1)} %inputs_ref.3) | copy-start | bytes 7864324
  1.7 1.1 %copy-start.3 = (bf16[1,640,512]{2,1,0:T(8,128)(2,1)S(1)}, bf16[1,640,512]{2,1,0:T(8,128)(2,1)}, u32[]{:S(2)}) copy-start(bf16[1,640,512]{2,1,0:T(8,128)(2,1)} %grads_ref.1) | copy-start | bytes 1966084
  6.0 4.0 %collective-permute-start = (bf16[4,528,256]{2,1,0:T(8,128)(2,1)S(1)}, bf16[4,528,256]{2,1,0:T(8,128)(2,1)S(1)}, u32[]{:S(2)}, u32[]{:S(2)}) collective-permute-start(bf16[4,528,256]{2,1,0:T(8,128)(2,1)S(1)} %get-tuple-element.17), channel_id=1, source_target_pairs={{0,1},{1,0},{2,3},{3,2},{4,5},{5,4},{6,7},{7,6},{8,9},{9,8},{10,11... | collective-permute-start | bytes 3244040 | tf_op jit(solution)/shard_map/ppermute | solution.py:19
  6.5 1.7 %copy-start.1 = (bf16[1,640,2048]{2,1,0:T(8,128)(2,1)S(1)}, bf16[1,640,2048]{2,1,0:T(8,128)(2,1)}, u32[]{:S(2)}) copy-start(bf16[1,640,2048]{2,1,0:T(8,128)(2,1)} %inputs_ref.3) | copy-start | bytes 7864324
  10.6 12.2 %collective-permute-start.3 = (bf16[528,256]{1,0:T(8,128)(2,1)S(1)}, bf16[528,256]{1,0:T(8,128)(2,1)S(1)}, u32[]{:S(2)}, u32[]{:S(2)}) collective-permute-start(bf16[528,256]{1,0:T(8,128)(2,1)S(1)} %shard_map.69), channel_id=1, source_target_pairs={{0,6},{1,7},{2,4},{3,5},{4,2},{5,3},{6,0},{7,1},{8,14},{9,15},{10,... | collective-permute-start | bytes 811016 | tf_op jit(solution)/shard_map/ppermute | solution.py:19
  15.8 23.1 %collective-permute-start.2 = (bf16[528,256]{1,0:T(8,128)(2,1)S(1)}, bf16[528,256]{1,0:T(8,128)(2,1)S(1)}, u32[]{:S(2)}, u32[]{:S(2)}) collective-permute-start(bf16[528,256]{1,0:T(8,128)(2,1)S(1)} %shard_map.68), channel_id=1, source_target_pairs={{0,4},{1,5},{2,6},{3,7},{4,0},{5,1},{6,2},{7,3},{8,12},{9,13},{10,... | collective-permute-start | bytes 811016 | tf_op jit(solution)/shard_map/ppermute | solution.py:19
  16.5 22.5 %collective-permute-start.1 = (bf16[528,256]{1,0:T(8,128)(2,1)S(1)}, bf16[528,256]{1,0:T(8,128)(2,1)S(1)}, u32[]{:S(2)}, u32[]{:S(2)}) collective-permute-start(bf16[528,256]{1,0:T(8,128)(2,1)S(1)} %shard_map.67), channel_id=1, source_target_pairs={{0,2},{1,3},{2,0},{3,1},{4,6},{5,7},{6,4},{7,5},{8,10},{9,11},{10,... | collective-permute-start | bytes 811016 | tf_op jit(solution)/shard_map/ppermute | solution.py:19
  17.1 24.7 %copy-start.12 = (f32[1,256]{1,0:T(1,128)S(1)}, f32[1,256]{1,0:T(1,128)}, u32[]{:S(2)}) copy-start(f32[1,256]{1,0:T(1,128)} %refs_11_.1) | copy-start | bytes 3076
  17.1 24.7 %copy-start.14 = (f32[1,512]{1,0:T(1,128)S(1)}, f32[1,512]{1,0:T(1,128)}, u32[]{:S(2)}) copy-start(f32[1,512]{1,0:T(1,128)} %param.11) | copy-start | bytes 6148
  17.4 34.5 %copy-start.13 = (bf16[1,512,512]{2,1,0:T(8,128)(2,1)S(1)}, bf16[1,512,512]{2,1,0:T(8,128)(2,1)}, u32[]{:S(2)}) copy-start(bf16[1,512,512]{2,1,0:T(8,128)(2,1)} %param.9) | copy-start | bytes 1572868
  40.3 8.8 %collective-permute-start.4 = (bf16[528,256]{1,0:T(8,128)(2,1)S(1)}, bf16[528,256]{1,0:T(8,128)(2,1)S(1)}, u32[]{:S(2)}, u32[]{:S(2)}) collective-permute-start(bf16[528,256]{1,0:T(8,128)(2,1)S(1)} %get-tuple-element.19), channel_id=1, source_target_pairs={{0,8},{8,0},{16,24},{24,16},{1,9},{9,1},{17,25},{25,17},{2,10},{10... | collective-permute-start | bytes 811016 | tf_op jit(solution)/shard_map/ppermute | solution.py:19
  41.9 6.7 %collective-permute-start.5 = (f32[768]{0:T(1024)S(1)}, f32[768]{0:T(1024)S(1)}, u32[]{:S(2)}, u32[]{:S(2)}) collective-permute-start(f32[768]{0:T(1024)S(1)} %pad_maximum_fusion), channel_id=1, source_target_pairs={{0,8},{8,0},{16,24},{24,16},{1,9},{9,1},{17,25},{25,17},{2,10},{10... | collective-permute-start | bytes 9224 | tf_op jit(solution)/shard_map/ppermute | solution.py:19
  50.3 30.4 %copy-start.2 = (bf16[1,256,2048]{2,1,0:T(8,128)(2,1)S(1)}, bf16[1,256,2048]{2,1,0:T(8,128)(2,1)}, u32[]{:S(2)}) copy-start(bf16[1,256,2048]{2,1,0:T(8,128)(2,1)} %param.8) | copy-start | bytes 3145732
  50.3 7.2 %collective-permute-start.6 = (bf16[528,256]{1,0:T(8,128)(2,1)S(1)}, bf16[528,256]{1,0:T(8,128)(2,1)S(1)}, u32[]{:S(2)}, u32[]{:S(2)}) collective-permute-start(bf16[528,256]{1,0:T(8,128)(2,1)S(1)} %get-tuple-element.21), channel_id=1, source_target_pairs={{0,16},{8,24},{16,0},{24,8},{1,17},{9,25},{17,1},{25,9},{2,18},{10... | collective-permute-start | bytes 811016 | tf_op jit(solution)/shard_map/ppermute | solution.py:19
  58.0 18.2 %collective-permute-start.10 = (bf16[512,256]{1,0:T(8,128)(2,1)S(1)}, bf16[512,256]{1,0:T(8,128)(2,1)S(1)}, u32[]{:S(2)}, u32[]{:S(2)}) collective-permute-start(bf16[512,256]{1,0:T(8,128)(2,1)S(1)} %shard_map.72.refs_2_), channel_id=1, source_target_pairs={{0,4},{1,5},{2,6},{3,7},{4,0},{5,1},{6,2},{7,3},{8,12},{9,13},{10,... | collective-permute-start | bytes 786440 | tf_op jit(solution)/shard_map/ppermute | solution.py:19
  58.1 18.2 %collective-permute-start.12 = (bf16[512,256]{1,0:T(8,128)(2,1)S(1)}, bf16[512,256]{1,0:T(8,128)(2,1)S(1)}, u32[]{:S(2)}, u32[]{:S(2)}) collective-permute-start(bf16[512,256]{1,0:T(8,128)(2,1)S(1)} %shard_map.72.refs_2_), channel_id=1, source_target_pairs={{0,6},{1,7},{2,4},{3,5},{4,2},{5,3},{6,0},{7,1},{8,14},{9,15},{10,... | collective-permute-start | bytes 786440 | tf_op jit(solution)/shard_map/ppermute | solution.py:19
  60.7 17.0 %collective-permute-start.8 = (bf16[512,256]{1,0:T(8,128)(2,1)S(1)}, bf16[512,256]{1,0:T(8,128)(2,1)S(1)}, u32[]{:S(2)}, u32[]{:S(2)}) collective-permute-start(bf16[512,256]{1,0:T(8,128)(2,1)S(1)} %shard_map.72.refs_2_), channel_id=1, source_target_pairs={{0,2},{1,3},{2,0},{3,1},{4,6},{5,7},{6,4},{7,5},{8,10},{9,11},{10,... | collective-permute-start | bytes 786440 | tf_op jit(solution)/shard_map/ppermute | solution.py:19
  61.6 16.3 %collective-permute-start.7 = (bf16[512,256]{1,0:T(8,128)(2,1)S(1)}, bf16[512,256]{1,0:T(8,128)(2,1)S(1)}, u32[]{:S(2)}, u32[]{:S(2)}) collective-permute-start(bf16[512,256]{1,0:T(8,128)(2,1)S(1)} %shard_map.72.refs_2_), channel_id=1, source_target_pairs={{0,1},{1,0},{2,3},{3,2},{4,5},{5,4},{6,7},{7,6},{8,9},{9,8},{10,11... | collective-permute-start | bytes 786440 | tf_op jit(solution)/shard_map/ppermute | solution.py:19
  76.3 2.3 %collective-permute-start.11 = (bf16[512,256]{1,0:T(8,128)(2,1)S(1)}, bf16[512,256]{1,0:T(8,128)(2,1)S(1)}, u32[]{:S(2)}, u32[]{:S(2)}) collective-permute-start(bf16[512,256]{1,0:T(8,128)(2,1)S(1)} %collective-permute-done.10.refs_6_), channel_id=1, source_target_pairs={{0,1},{1,0},{2,3},{3,2},{4,5},{5,4},{6,7},{7,6},{8,9},{9,8},{10,11... | collective-permute-start | bytes 786440 | tf_op jit(solution)/shard_map/ppermute | solution.py:19
  76.3 3.0 %collective-permute-start.13 = (bf16[512,256]{1,0:T(8,128)(2,1)S(1)}, bf16[512,256]{1,0:T(8,128)(2,1)S(1)}, u32[]{:S(2)}, u32[]{:S(2)}) collective-permute-start(bf16[512,256]{1,0:T(8,128)(2,1)S(1)} %collective-permute-done.12.refs_8_), channel_id=1, source_target_pairs={{0,1},{1,0},{2,3},{3,2},{4,5},{5,4},{6,7},{7,6},{8,9},{9,8},{10,11... | collective-permute-start | bytes 786440 | tf_op jit(solution)/shard_map/ppermute | solution.py:19
  77.6 2.4 %collective-permute-start.9 = (bf16[512,256]{1,0:T(8,128)(2,1)S(1)}, bf16[512,256]{1,0:T(8,128)(2,1)S(1)}, u32[]{:S(2)}, u32[]{:S(2)}) collective-permute-start(bf16[512,256]{1,0:T(8,128)(2,1)S(1)} %collective-permute-done.8.refs_4_), channel_id=1, source_target_pairs={{0,1},{1,0},{2,3},{3,2},{4,5},{5,4},{6,7},{7,6},{8,9},{9,8},{10,11... | collective-permute-start | bytes 786440 | tf_op jit(solution)/shard_map/ppermute | solution.py:19
  77.9 0.7 copy-start.4
  78.6 0.7 copy-start.6
  79.3 0.7 copy-start.8
  80.0 0.7 copy-start.10
  80.7 1.0 copy-start.5
  81.6 0.9 copy-start.7
  82.6 0.9 copy-start.9
  83.5 0.9 copy-start.11
  86.8 9.1 %collective-permute-start.14 = (bf16[528,256]{1,0:T(8,128)(2,1)}, bf16[528,256]{1,0:T(8,128)(2,1)S(1)}, u32[]{:S(2)}, u32[]{:S(2)}) collective-permute-start(bf16[528,256]{1,0:T(8,128)(2,1)} %get-tuple-element.24), channel_id=1, source_target_pairs={{0,8},{8,0},{16,24},{24,16},{1,9},{9,1},{17,25},{25,17},{2,10},{10... | collective-permute-start | bytes 811016 | tf_op jit(solution)/shard_map/ppermute | solution.py:19
  97.2 8.1 %collective-permute-start.15 = (bf16[528,256]{1,0:T(8,128)(2,1)S(1)}, bf16[528,256]{1,0:T(8,128)(2,1)S(1)}, u32[]{:S(2)}, u32[]{:S(2)}) collective-permute-start(bf16[528,256]{1,0:T(8,128)(2,1)S(1)} %get-tuple-element.26), channel_id=1, source_target_pairs={{0,16},{8,24},{16,0},{24,8},{1,17},{9,25},{17,1},{25,9},{2,18},{10... | collective-permute-start | bytes 811016 | tf_op jit(solution)/shard_map/ppermute | solution.py:19

commit v3 on v0

v3 whole, which is shorter than its diff:
```python
import functools

import jax
import jax.numpy as jnp
from jax import lax
from jax.experimental import pallas as pl
from jax.experimental.pallas import tpu as pltpu
from jax.sharding import PartitionSpec as P

TAIL = 16
LIFT = 2.0**15
TINY = 1e-30
F32, BF16 = jnp.float32, jnp.bfloat16
VMEM = pl.BlockSpec(memory_space=pltpu.VMEM)
SMEM = pl.BlockSpec(memory_space=pltpu.SMEM)
HBM = pl.BlockSpec(memory_space=pltpu.HBM)
FIRST_GRANT = 8
SPLIT = 2


def exchange(x, axis, flip):
    return lax.ppermute(x, axis, [(i, i ^ flip) for i in range(lax.axis_size(axis))])


def put(ref, value):
    rows = value.shape[0]
    top = jnp.max(jnp.max(jnp.abs(value), axis=0, keepdims=True), axis=1, keepdims=True)
    top = jnp.maximum(jnp.broadcast_to(top, (1, value.shape[1])), TINY).astype(BF16).astype(F32)
    ref[rows:, :] = jnp.broadcast_to(top, (TAIL, value.shape[1])).astype(BF16)
    z = value * (LIFT / top)
    z2 = z * z
    z4 = z2 * z2
    z8 = z4 * z4
    ref[:rows, :] = jnp.where(z < 0, -z8, z8).astype(BF16)


def get(ref):
    rows = ref.shape[0] - TAIL
    top = ref[rows:, :][:1, :].astype(F32) * (1.0 / LIFT)
    y = ref[:rows, :].astype(F32)
    square = lax.rsqrt(lax.rsqrt(jnp.abs(y) + 1e-37))
    size = square * lax.rsqrt(square)
    return jnp.where(y < 0, -size, size) * top


def first_kernel(
    core_ref, grads_hbm, inputs_hbm, out_decay, in_decay, out_ref, turned_ref, own_ref, rates_ref, grads_ref, inputs_ref, sems
):
    core = core_ref[0]
    width = out_decay.shape[1]
    rates_ref[:, :width] = out_decay[...]
    rates_ref[:, width:] = in_decay[...]
    chips, _, rows = inputs_ref.shape
    lead = pltpu.make_async_copy(grads_hbm.at[0], grads_ref, sems.at[2 * chips])
    lead.start()

    def load(i, of, into, sem):
        start = pl.multiple_of((2 * i + of) * rows, rows)
        return pltpu.make_async_copy(inputs_hbm.at[0, :, pl.ds(start, rows)], into.at[i], sem)

    theirs = [load(i, 1 - core, inputs_ref, sems.at[i]) for i in range(chips)]
    mine = [load(i, core, own_ref, sems.at[chips + i]) for i in range(chips)]
    for copy in theirs + mine:
        copy.start()
    lead.wait()
    turned_ref[...] = grads_ref[...].T
    for i in range(chips):
        theirs[i].wait()
        put(out_ref.at[i], jnp.dot(turned_ref[...], inputs_ref[i], preferred_element_type=F32))
    for copy in mine:
        copy.wait()


def sum_kernel(part, n, passes, *refs):
    at_ref, turned_ref, own_ref, theirs_ref = refs[:4]
    messages, rest = refs[4 : 4 + n], refs[4 + n :]
    outs = rest[passes:]
    lanes = outs[0].shape[1]
    columns = pl.ds(part * lanes, lanes)
    at = at_ref[0]
    total = jnp.dot(turned_ref[...], own_ref[at, :, columns], preferred_element_type=F32)
    total = total + get(theirs_ref.at[at, :, columns])
    for message in messages:
        total = total + get(message)
    put(outs[0], total)
    if passes:
        for i in range(passes):
            outs[1][i : i + 1, :] = rest[i][...]
    elif len(outs) > 1:
        outs[1][...] = total


def turn_kernel(core_ref, a_ref, s_ref, own_ref, send_ref, s_out):
    core = core_ref[0]
    rows = a_ref.shape[1]
    for i in range(own_ref.shape[0] // rows):
        for of, out in ((core, own_ref), (1 - core, send_ref)):
            columns = pl.ds(pl.multiple_of((2 * i + of) * rows, rows), rows)
            out[i * rows : (i + 1) * rows, :] = a_ref[0, :, columns].T
    s_out[...] = s_ref[0].T


def weight(cols_ref, rows_ref, j):
    return cols_ref[:, j : j + 1] * rows_ref[j : j + 1, :]


def weighed(places, cols_ref, rows_ref, messages, value):
    for j, message in zip(places, messages):
        value = value + weight(cols_ref, rows_ref, j) * get(message)
    return value


def step_kernel(into_value, into_total, more, *refs):
    n = len(into_value)
    value_ref, total_ref, cols_ref, rows_ref = refs[:4]
    messages, outs = refs[4 : 4 + n], refs[4 + n :]
    outs[0][...] = weighed(into_value, cols_ref, rows_ref, messages, value_ref[...])
    total = weight(cols_ref, rows_ref, into_total[0]) * total_ref[...]
    total = weighed(into_total[1:], cols_ref, rows_ref, messages, total)
    put(outs[1], total)
    if more:
        outs[2][...] = total


def cross_kernel(places, part, value_ref, total_ref, cols_ref, rows_ref, message_ref, value_out, sent_ref):
    into_value, mix_own, mix_got = places
    lanes = sent_ref.shape[1]
    columns = slice(part * lanes, (part + 1) * lanes)
    at = rows_ref.at[:, columns]
    got = get(message_ref)
    value_out[...] = value_ref[:, columns] + weight(cols_ref, at, into_value) * got
    put(sent_ref, weight(cols_ref, at, mix_own) * total_ref[:, columns] + weight(cols_ref, at, mix_got) * got)


def side_s_kernel(places, value_ref, s_ref, cols_ref, rows_ref, *refs):
    upper = weighed(places, cols_ref, rows_ref, refs[: len(places)], value_ref[...])
    refs[-1][...] = jnp.dot(s_ref[...], upper.astype(BF16), preferred_element_type=F32).astype(BF16)


def side_a_kernel(n, has_before, start, *refs):
    refs = list(refs)
    at_ref, a_ref = refs.pop(0), refs.pop(0)
    solved = refs.pop(0)[...] if has_before else None
    for i in range(n):
        lanes = refs[i].shape[1]
        features = pl.ds(pl.multiple_of(at_ref[start + i], lanes), lanes)
        term = jnp.dot(refs[i][...], a_ref[features, :], preferred_element_type=F32)
        solved = term if solved is None else solved + term
    if refs[-1].dtype == F32:
        refs[-1][...] = solved
    else:
        put(refs[-1], solved)


def joint_kernel(j, own_ref, theirs_ref, cols_ref, rows_ref, value_ref, total_ref, *sent_refs):
    value = own_ref[...] + get(theirs_ref)
    value_ref[...] = value
    total_ref[...] = weight(cols_ref, rows_ref, j) * value
    for i, sent in enumerate(sent_refs):
        lanes = sent.shape[1]
        put(sent, total_ref[:, i * lanes : (i + 1) * lanes])


def last_kernel(places, *refs):
    cols_ref, rows_ref, out_ref = refs[0], refs[1], refs[-1]
    start, refs = 0, list(refs[2:-1])
    while refs:
        value_ref = refs.pop(0)
        lanes = value_ref.shape[1]
        at = rows_ref.at[:, start : start + lanes]
        lower = weighed(places, cols_ref, at, [refs.pop(0) for _ in places], value_ref[...])
        out_ref[0, start : start + lanes, :] = lower.T.astype(BF16)
        start += lanes


def digits(layers):
    step, out = 1, []
    while step < layers:
        size = min(4, layers // step)
        out.append((step, size))
        step *= size
    return out


def weights_kernel(size, last, n, me_ref, *refs):
    groups, (below_ref, above_ref) = refs[:n], refs[n : n + 2]
    cols_ref, rows_ref, state_ref = refs[n + 2 :]
    group = [ref[i : i + 1, :] for ref in groups for i in range(ref.shape[0])]
    below, above = below_ref[...], above_ref[...]
    me = me_ref[0]
    ones, zeros = jnp.ones_like(below), jnp.zeros_like(below)

    def product(holds):
        out = ones
        for flip, vector in enumerate(group):
            out = out * jnp.where(holds(me ^ flip), vector, ones)
        return out

    def carry(up, source, target):
        if up:
            return jnp.where(source > target, product(lambda q: (q > target) & (q < source)), zeros)
        return jnp.where(source < target, product(lambda q: (q < target) & (q > source)), zeros)

    stack = [group[0]]
    for up, factor in ((True, below), (False, above)):
        if not last:
            stack += [factor * carry(up, me ^ flip, me) for flip in range(1, size)]
            for flip in range(size):
                stack.append(product((lambda q: q < me ^ flip) if up else (lambda q: q > me ^ flip)))
        elif size == 4:
            for first, second in ((1, 2), (2, 1)):
                its, target = me ^ first, me ^ second
                stack += [factor * carry(up, its, me), carry(up, me, target), carry(up, its, target)]
            stack.append(factor)
        else:
            stack.append(factor * carry(up, me ^ 1, me))
    width = cols_ref.shape[0]
    stack += [zeros] * (cols_ref.shape[1] - len(stack))
    table = jnp.concatenate(stack, axis=0)
    cols_ref[...] = table[:, :width].T
    rows_ref[...] = table[: rows_ref.shape[0], width:]
    before = product(lambda q: q < me)
    state_ref[...] = jnp.concatenate([product(lambda q: q >= 0), below * before, above * before], axis=0)


def weight_places(size, last):
    if not last:
        n = 2 * size - 1
        return [(list(range(1 + i * n, i * n + size)), list(range(i * n + size, 1 + i * n + n))) for i in range(2)]
    if size == 4:
        orders = [((1, 2), (0, 1, 2)), ((2, 1), (3, 4, 5))]
        return [([(flips, tuple(1 + 7 * i + j for j in at)) for flips, at in orders], [7 + 7 * i]) for i in range(2)]
    return [(None, [1 + i]) for i in range(2)]


def shards(activations, out_grads, a_inverse, s_inverse, in_decay, out_decay):
    layers, peers = lax.axis_size("layer"), lax.axis_size("dp")
    layer, here = lax.axis_index("layer"), lax.axis_index("dp")
    core, chip = here % 2, here // 2
    chips = peers // 2
    rows = a_inverse.shape[1]
    width = out_grads.shape[2]
    tokens = activations.shape[1]
    split = SPLIT if rows % (128 * SPLIT) == 0 else 1
    lanes = rows // split

    def shape(*dims, dtype=F32):
        return jax.ShapeDtypeStruct(dims, dtype)

    def message(n):
        return shape(width + TAIL, n, dtype=BF16)

    def call(kernel, out_shape, *operands, scalars=0, grant=4 * 2**20, hbm=0, scratch=(), after=()):
        several = isinstance(out_shape, (list, tuple))
        if after:
            inner, count = kernel, len(operands)

            def kernel(*refs):
                inner(*refs[:count], *refs[count + len(after) :])

        return pl.pallas_call(
            kernel,
            out_shape=out_shape,
            in_specs=[SMEM] * scalars
            + [HBM] * hbm
            + [VMEM] * (len(operands) - scalars - hbm)
            + [pl.BlockSpec(memory_space=pl.ANY)] * len(after),
            out_specs=[VMEM] * len(out_shape) if several else VMEM,
            scratch_shapes=scratch,
            compiler_params=pltpu.CompilerParams(vmem_limit_bytes=grant),
            cost_estimate=pl.CostEstimate(flops=10**9, bytes_accessed=10**8, transcendentals=0),
        )(*operands, *after)

    def scalar(x):
        return x.reshape(1).astype(jnp.int32)

    sent, turned, inputs, rates = call(
        first_kernel,
        [
            shape(chips, width + TAIL, rows, dtype=BF16),
            shape(width, tokens, dtype=BF16),
            shape(chips, tokens, rows, dtype=BF16),
            shape(1, width + rows),
        ],
        scalar(core),
        pltpu.with_memory_space_constraint(out_grads, pltpu.HBM),
        pltpu.with_memory_space_constraint(activations, pltpu.HBM),
        out_decay,
        in_decay,
        scalars=1,
        hbm=2,
        grant=FIRST_GRANT * 2**20,
        scratch=[
            pltpu.VMEM((tokens, width), BF16),
            pltpu.VMEM((chips, tokens, rows), BF16),
            pltpu.SemaphoreType.DMA((2 * chips + 1,)),
        ],
    )
    theirs = exchange(sent, "dp", 1)

    levels = [1 << b for b in range(chips.bit_length() - 1)]
    received = [{o: [] for o in range(chips)} for _ in range(split)]
    latest = []

    def block(part, o, *more, passed=(), after=()):
        got = received[part][o]
        outs = call(
            functools.partial(sum_kernel, part, len(got), len(passed)),
            [message(lanes), *more],
            scalar(chip ^ o),
            turned,
            inputs,
            theirs,
            *got,
            *passed,
            scalars=1,
            after=[*latest[-1:], *after],
        )
        latest.append(outs[0])
        return outs

    order = []
    for level in levels:
        sends = list(reversed(range(level, chips, 2 * level)))
        early, late = (sends[:-1], sends[-1:]) if level < levels[-1] else (sends, [])
        order += [(level, o, part) for o in early for part in range(split)]
        order += [(level, o, 0) for o in late]
    order += [(level, level, part) for level in levels[:-1] for part in range(1, split)]

    size = digits(layers)[0][1]
    group = [exchange(rates, "layer", 1)]
    pair_at = min(1, len(order) - 1)
    wait_at = min(3, len(order) - 1)
    for i, (level, o, part) in enumerate(order):
        if i == pair_at:
            sent, pair = block(part, o, shape(2, width + rows), passed=(rates, *group))
            group = [pair] if size < 4 else [pair, exchange(pair, "layer", 2)]
        else:
            [sent] = block(part, o, after=group[1:] if i == wait_at else ())
        received[part][o ^ level].append(exchange(sent, "dp", 2 * level))

    ups, downs = [], []
    below, above = rates, jnp.ones_like(rates)
    for step, size in digits(layers):
        last = step * size == layers
        if step > 1:
            group = [own]
            for bit in (1, 2)[: size.bit_length() - 1]:
                group.append(exchange(jnp.concatenate(group, axis=0), "layer", bit * step))
        cols, in_rows, state = call(
            functools.partial(weights_kernel, size, last, len(group)),
            [shape(width, 128), shape(16, rows), shape(3, width + rows)],
            scalar(layer // step % size),
            *group,
            below,
            above,
            scalars=1,
        )
        own, below, above = state[:1], state[1:2], state[2:]
        for solve, places in zip((ups, downs), weight_places(size, last)):
            solve.append((step, size, cols, in_rows, *places))
    a_own, a_theirs, s_turned = call(
        turn_kernel,
        [shape(chips * rows, rows, dtype=BF16)] * 2 + [shape(width, width, dtype=BF16)],
        scalar(core),
        a_inverse,
        s_inverse,
        scalars=1,
        after=latest[-1:],
    )
    a_theirs = exchange(a_theirs, "dp", 1)

    def steps(solve, value, total, sent, part=0):
        n = value.shape[1]
        for i, (step, size, cols, in_rows, into_value, into_total) in enumerate(solve[:-1]):
            more = i + 1 < len(solve)
            outs = [shape(width, n), message(n)] + [shape(width, n)] * more
            kernel = functools.partial(step_kernel, into_value, into_total, more)
            others = [exchange(sent, "layer", flip * step) for flip in range(1, size)]
            value, sent, total = call(kernel, outs, value, total, cols, in_rows[:, part * n : (part + 1) * n], *others)
        return value, total, sent

    def cross(solve, part, value, total, sent):
        step, size, cols, in_rows, orders, _ = solve[-1]
        n = sent.shape[1]
        if orders is None:
            return value, exchange(sent, "layer", step)
        (first, second), places = orders[part % 2]
        kernel = functools.partial(cross_kernel, places, part if value.shape[1] > n else 0)
        got = exchange(sent, "layer", first * step)
        at = in_rows if value.shape[1] > n or n == rows else in_rows[:, part * n : (part + 1) * n]
        value, sent = call(kernel, [shape(width, n), message(n)], value, total, cols, at, got)
        return value, exchange(sent, "layer", second * step)

    def upper_solve(part, after):
        sent, value = block(part, 0, shape(width, lanes))
        value, total, sent = steps(ups, value, value, sent, part)
        value, got = cross(ups, part, value, total, sent)
        _, _, cols, in_rows, _, places = ups[-1]
        at = in_rows[:, part * lanes : (part + 1) * lanes]
        kernel = functools.partial(side_s_kernel, places)
        return call(kernel, shape(width, lanes, dtype=BF16), value, s_turned, cols, at, got, after=after)

    applied = []
    for part in range(split):
        applied.append(upper_solve(part, applied[-1:]))
    own, others = None, None
    for part in range(split):
        have = {0: applied[part]}
        for level in reversed(levels):
            for o in list(have):
                have[o ^ level] = exchange(have[o], "dp", 2 * level)
        places = jnp.stack([(chip ^ o) * rows + part * lanes for o in have]).astype(jnp.int32)

        def product(a, before, out_shape, after=()):
            before = [] if before is None else [before]
            kernel = functools.partial(side_a_kernel, chips, bool(before), 0)
            return call(kernel, out_shape, places, a, *before, *have.values(), scalars=1, after=after)

        last = part + 1 == split
        others = product(
            a_theirs, others, message(rows) if last else shape(width, rows), [own] if last and own is not None else []
        )
        own = product(a_own, own, shape(width, rows))
    others = exchange(others, "dp", 1)

    pieces = split if len(downs) == 1 and downs[-1][1] == 4 else 1
    outs = [shape(width, rows)] * 2 + [message(rows // pieces)] * pieces
    _, _, cols, in_rows, *_ = downs[0]
    value, total, *sent = call(functools.partial(joint_kernel, 0), outs, own, others, cols, in_rows)
    if pieces == 1:
        value, total, sent[0] = steps(downs, value, total, sent[0])
    operands = [x for part in range(pieces) for x in cross(downs, part, value, total, sent[part])]
    _, _, cols, in_rows, _, places = downs[-1]
    return call(functools.partial(last_kernel, places), shape(1, rows, width, dtype=BF16), cols, in_rows, *operands)


def solution(mesh):
    placed = (
        P("layer", "dp", None),
        P("layer", "dp", None),
        P("layer", "dp", None),
        P("layer", None, None),
        P("layer", "dp"),
        P("layer", None),
    )
    return jax.shard_map(
        shards, mesh=mesh, in_specs=placed, out_specs=P("layer", "dp", None), check_vma=False
    )
```

time: 191 us -> 85.3 us (0.45)
  waiting for transfers between devices: 136 us -> 27.3 us
  starting transfers between devices: 0.12 us -> 34.2 us
  Pallas kernels: 0 us -> 18.9 us
  blocking collectives: 16.1 us -> 0 us
  between operations: 13.2 us -> 0.26 us
  other arithmetic: 11.4 us -> 0.15 us
  matrix products: 10.7 us -> 0 us
  local copies, waits for them, and re-layouts: 1.89 us -> 4.24 us
    all_gather x3 -> x0, waiting for transfers between devices: 83.3 us -> none  [the longest x2 54.1 us: prefix(): everything = jax.tree.map(lambda part: lax.all_gather(part, axis), shard)]
    reduce_scatter x1 -> x0, waiting for transfers between devices: 52.8 us -> none  [shards(): lax.psum_scatter(lax.dot_general(window_cols, grads_here, contract, prefe...]
    ppermute x0 -> x25, starting transfers between devices: none -> 34.2 us  [exchange(): lax.ppermute(x, axis, [(i, i ^ flip) for i in range(lax.axis_size(axis))])]
    ppermute x0 -> x25, waiting for transfers between devices: none -> 27.3 us  [exchange(): lax.ppermute(x, axis, [(i, i ^ flip) for i in range(lax.axis_size(axis))])]
    pallas_call x0 -> x23, Pallas kernels: none -> 18.9 us  [call(): pl.pallas_call(kernel, out_shape=out_shape, in_specs=[SMEM] * scalars + [...]
    all_gather x2 -> x0, blocking collectives: 16.1 us -> none  [prefix(): everything = jax.tree.map(lambda part: lax.all_gather(part, axis), shard)]
    dot_general x3 -> x0, matrix products: 10.7 us -> none  [the longest x1 4.88 us: shards(): lax.dot_general(window_cols, grads_here, contract, preferred_element_type...]
    select_n x8 -> x0, other arithmetic: 9.54 us -> none  [turn(): return jax.tree.map(lambda a, b: jnp.where(reached, a, b), new, before)]
  transfers between devices with their start and end apart: 4 -> 25, of which waited for: 4 -> 13; matrix products, arithmetic and copies ran while one was open for 0% -> 0% of each run, Pallas kernels for 0% -> 13%
where the time goes in v3:
time: 85.3 us; the launch traced here: 85.1 us
  starting transfers between devices  34.2 us (40%)
  waiting for transfers between devices  27.3 us (32%)
  Pallas kernels  18.9 us (22%)
  local copies, waits for them, and re-layouts  4.24 us (5%)
    ppermute x25, starting transfers between devices, exchange(): lax.ppermute(x, axis, [(i, i ^ flip) for i in range(lax.axis_size(axis))])  34.2 us
    ppermute x25, waiting for transfers between devices, exchange(): lax.ppermute(x, axis, [(i, i ^ flip) for i in range(lax.axis_size(axis))])  27.3 us
    pallas_call x23, Pallas kernels, call(): pl.pallas_call(kernel, out_shape=out_shape, in_specs=[SMEM] * scalars + [...  18.9 us
    unnamed x18, local copies, waits for them, and re-layouts  4.24 us
  transfers between devices with their start and end apart: 25, of which 13 were waited for; matrix products, arithmetic and copies ran while one was open for 0% of the time, Pallas kernels for 13%

profile of v3, /device:TPU:0, one launch (start us, length us, event | category | flops | bytes accessed | tf_op | source)
XLA Modules:
  0.0 85.1 jit_solution(11931755064845643169)
XLA Ops:
  1.4 4.8 %shard_map.64 = (bf16[4,528,256]{2,1,0:T(8,128)(2,1)S(1)}, bf16[512,640]{1,0:T(8,128)(2,1)S(1)}, bf16[4,640,256]{2,1,0:T(8,128)(2,1)S(1)}, f32[1,768]{1,0:T(1,128)S(1)}) custom-call(s32[1]{0:T(128)} %bitcast.2.core_ref.refs_0_, bf16[1,640,512]{2,1,0:T(8,128)(2,1)} %grads_hbm.1, bf16[1,640,2048]{2,1,0:T(8,128)(2,1)} %inputs_hbm.1, f32[1,512]{1,0:T(1,128)S(1)} %copy-done.2, ...), custom_call_target="tpu_custom_call" | custom-call | flops 1000000000 | bytes 100000000 | tf_op jit(solution)/shard_map/pallas_call | solution.py:261
  7.5 2.5 %collective-permute-start.1 = (f32[1,768]{1,0:T(1,128)S(1)}, f32[1,768]{1,0:T(1,128)S(1)}, u32[]{:S(2)}, u32[]{:S(2)}) collective-permute-start(f32[1,768]{1,0:T(1,128)S(1)} %get-tuple-element.35.refs_4_.refs_2_), channel_id=1, source_target_pairs={{0,8},{8,0},{16,24},{24,16},{1,9},{9,1},{17,25},{25,17},{2,10},{10... | collective-permute-start | bytes 9224 | tf_op jit(solution)/shard_map/ppermute | solution.py:22
  10.0 1.1 %copy-done.5 = bf16[512,640]{1,0:T(8,128)(2,1)S(1)} copy-done((bf16[512,640]{1,0:T(8,128)(2,1)S(1)}, bf16[512,640]{1,0:T(8,128)(2,1)}, u32[]{:S(2)}) %copy-start.5) | copy-done | bytes 655384
  11.6 2.9 %collective-permute-start.4 = (bf16[528,128]{1,0:T(8,128)(2,1)S(1)}, bf16[528,128]{1,0:T(8,128)(2,1)S(1)}, u32[]{:S(2)}, u32[]{:S(2)}) collective-permute-start(bf16[528,128]{1,0:T(8,128)(2,1)S(1)} %shard_map.65.refs_6_), channel_id=1, source_target_pairs={{0,2},{1,3},{2,0},{3,1},{4,6},{5,7},{6,4},{7,5},{8,10},{9,11},{10,... | collective-permute-start | bytes 405512 | tf_op jit(solution)/shard_map/ppermute | solution.py:22
  15.0 1.6 %collective-permute-start.2 = (f32[2,768]{1,0:T(2,128)S(1)}, f32[2,768]{1,0:T(2,128)S(1)}, u32[]{:S(2)}, u32[]{:S(2)}) collective-permute-start(f32[2,768]{1,0:T(2,128)S(1)} %get-tuple-element.36.refs_0_), channel_id=1, source_target_pairs={{0,16},{8,24},{16,0},{24,8},{1,17},{9,25},{17,1},{25,9},{2,18},{10... | collective-permute-start | bytes 18440 | tf_op jit(solution)/shard_map/ppermute | solution.py:22
  17.5 1.6 %collective-permute-start.5 = (bf16[528,128]{1,0:T(8,128)(2,1)S(1)}, bf16[528,128]{1,0:T(8,128)(2,1)S(1)}, u32[]{:S(2)}, u32[]{:S(2)}) collective-permute-start(bf16[528,128]{1,0:T(8,128)(2,1)S(1)} %shard_map.68.refs_5_), channel_id=1, source_target_pairs={{0,2},{1,3},{2,0},{3,1},{4,6},{5,7},{6,4},{7,5},{8,10},{9,11},{10,... | collective-permute-start | bytes 405512 | tf_op jit(solution)/shard_map/ppermute | solution.py:22
  19.7 2.7 %collective-permute-start.6 = (bf16[528,128]{1,0:T(8,128)(2,1)S(1)}, bf16[528,128]{1,0:T(8,128)(2,1)S(1)}, u32[]{:S(2)}, u32[]{:S(2)}) collective-permute-start(bf16[528,128]{1,0:T(8,128)(2,1)S(1)} %shard_map.69.refs_5_), channel_id=1, source_target_pairs={{0,4},{1,5},{2,6},{3,7},{4,0},{5,1},{6,2},{7,3},{8,12},{9,13},{10,... | collective-permute-start | bytes 405512 | tf_op jit(solution)/shard_map/ppermute | solution.py:22
  22.4 3.2 %collective-permute-done.3.refs_4_ = bf16[528,128]{1,0:T(8,128)(2,1)S(1)} collective-permute-done((bf16[528,128]{1,0:T(8,128)(2,1)S(1)}, bf16[528,128]{1,0:T(8,128)(2,1)S(1)}, u32[]{:S(2)}, u32[]{:S(2)}) %collective-permute-start.3) | collective-permute-done | bytes 135200 | tf_op jit(solution)/shard_map/ppermute | solution.py:22
  26.8 2.2 %collective-permute-start.13 = (bf16[528,128]{1,0:T(8,128)(2,1)S(1)}, bf16[528,128]{1,0:T(8,128)(2,1)S(1)}, u32[]{:S(2)}, u32[]{:S(2)}) collective-permute-start(bf16[528,128]{1,0:T(8,128)(2,1)S(1)} %shard_map.71.refs_3_.refs_6_), channel_id=1, source_target_pairs={{0,2},{1,3},{2,0},{3,1},{4,6},{5,7},{6,4},{7,5},{8,10},{9,11},{10,... | collective-permute-start | bytes 405512 | tf_op jit(solution)/shard_map/ppermute | solution.py:22
  30.4 1.6 %collective-permute-start.7 = (bf16[528,128]{1,0:T(8,128)(2,1)S(1)}, bf16[528,128]{1,0:T(8,128)(2,1)S(1)}, u32[]{:S(2)}, u32[]{:S(2)}) collective-permute-start(bf16[528,128]{1,0:T(8,128)(2,1)S(1)} %get-tuple-element.42.refs_6_), channel_id=1, source_target_pairs={{0,8},{8,0},{16,24},{24,16},{1,9},{9,1},{17,25},{25,17},{2,10},{10... | collective-permute-start | bytes 405512 | tf_op jit(solution)/shard_map/ppermute | solution.py:22
  31.9 1.1 %collective-permute-done.13.refs_5_ = bf16[528,128]{1,0:T(8,128)(2,1)S(1)} collective-permute-done((bf16[528,128]{1,0:T(8,128)(2,1)S(1)}, bf16[528,128]{1,0:T(8,128)(2,1)S(1)}, u32[]{:S(2)}, u32[]{:S(2)}) %collective-permute-start.13) | collective-permute-done | bytes 135200 | tf_op jit(solution)/shard_map/ppermute | solution.py:22
  33.0 1.4 %collective-permute-done.12.refs_4_ = bf16[528,128]{1,0:T(8,128)(2,1)S(1)} collective-permute-done((bf16[528,128]{1,0:T(8,128)(2,1)S(1)}, bf16[528,128]{1,0:T(8,128)(2,1)S(1)}, u32[]{:S(2)}, u32[]{:S(2)}) %collective-permute-start.12) | collective-permute-done | bytes 135200 | tf_op jit(solution)/shard_map/ppermute | solution.py:22
  35.1 1.7 %collective-permute-start.14 = (bf16[528,128]{1,0:T(8,128)(2,1)S(1)}, bf16[528,128]{1,0:T(8,128)(2,1)S(1)}, u32[]{:S(2)}, u32[]{:S(2)}) collective-permute-start(bf16[528,128]{1,0:T(8,128)(2,1)S(1)} %get-tuple-element.47), channel_id=1, source_target_pairs={{0,16},{8,24},{16,0},{24,8},{1,17},{9,25},{17,1},{25,9},{2,18},{10... | collective-permute-start | bytes 405512 | tf_op jit(solution)/shard_map/ppermute | solution.py:22
  37.3 2.8 %collective-permute-start.8 = (bf16[528,128]{1,0:T(8,128)(2,1)S(1)}, bf16[528,128]{1,0:T(8,128)(2,1)S(1)}, u32[]{:S(2)}, u32[]{:S(2)}) collective-permute-start(bf16[528,128]{1,0:T(8,128)(2,1)S(1)} %get-tuple-element.45), channel_id=1, source_target_pairs={{0,16},{8,24},{16,0},{24,8},{1,17},{9,25},{17,1},{25,9},{2,18},{10... | collective-permute-start | bytes 405512 | tf_op jit(solution)/shard_map/ppermute | solution.py:22
  40.1 1.4 %collective-permute-done.14.message_ref = bf16[528,128]{1,0:T(8,128)(2,1)S(1)} collective-permute-done((bf16[528,128]{1,0:T(8,128)(2,1)S(1)}, bf16[528,128]{1,0:T(8,128)(2,1)S(1)}, u32[]{:S(2)}, u32[]{:S(2)}) %collective-permute-start.14) | collective-permute-done | bytes 135200 | tf_op jit(solution)/shard_map/ppermute | solution.py:22
  42.0 1.6 %collective-permute-start.15 = (bf16[528,128]{1,0:T(8,128)(2,1)S(1)}, bf16[528,128]{1,0:T(8,128)(2,1)S(1)}, u32[]{:S(2)}, u32[]{:S(2)}) collective-permute-start(bf16[528,128]{1,0:T(8,128)(2,1)S(1)} %get-tuple-element.49), channel_id=1, source_target_pairs={{0,8},{8,0},{16,24},{24,16},{1,9},{9,1},{17,25},{25,17},{2,10},{10... | collective-permute-start | bytes 405512 | tf_op jit(solution)/shard_map/ppermute | solution.py:22
  44.6 1.5 %collective-permute-start.9 = (bf16[512,128]{1,0:T(8,128)(2,1)S(1)}, bf16[512,128]{1,0:T(8,128)(2,1)S(1)}, u32[]{:S(2)}, u32[]{:S(2)}) collective-permute-start(bf16[512,128]{1,0:T(8,128)(2,1)S(1)} %shard_map.75.refs_2_.refs_5_), channel_id=1, source_target_pairs={{0,4},{1,5},{2,6},{3,7},{4,0},{5,1},{6,2},{7,3},{8,12},{9,13},{10,... | collective-permute-start | bytes 393224 | tf_op jit(solution)/shard_map/ppermute | solution.py:22
  46.1 2.3 %collective-permute-start.10 = (bf16[512,128]{1,0:T(8,128)(2,1)S(1)}, bf16[512,128]{1,0:T(8,128)(2,1)S(1)}, u32[]{:S(2)}, u32[]{:S(2)}) collective-permute-start(bf16[512,128]{1,0:T(8,128)(2,1)S(1)} %shard_map.75.refs_2_.refs_5_), channel_id=1, source_target_pairs={{0,2},{1,3},{2,0},{3,1},{4,6},{5,7},{6,4},{7,5},{8,10},{9,11},{10,... | collective-permute-start | bytes 393224 | tf_op jit(solution)/shard_map/ppermute | solution.py:22
  50.0 5.0 %collective-permute-done.9.refs_3_ = bf16[512,128]{1,0:T(8,128)(2,1)S(1)} collective-permute-done((bf16[512,128]{1,0:T(8,128)(2,1)S(1)}, bf16[512,128]{1,0:T(8,128)(2,1)S(1)}, u32[]{:S(2)}, u32[]{:S(2)}) %collective-permute-start.9) | collective-permute-done | bytes 131104 | tf_op jit(solution)/shard_map/ppermute | solution.py:22
  55.1 2.0 %collective-permute-start.17 = (bf16[512,128]{1,0:T(8,128)(2,1)S(1)}, bf16[512,128]{1,0:T(8,128)(2,1)S(1)}, u32[]{:S(2)}, u32[]{:S(2)}) collective-permute-start(bf16[512,128]{1,0:T(8,128)(2,1)S(1)} %shard_map.79.refs_3_), channel_id=1, source_target_pairs={{0,2},{1,3},{2,0},{3,1},{4,6},{5,7},{6,4},{7,5},{8,10},{9,11},{10,... | collective-permute-start | bytes 393224 | tf_op jit(solution)/shard_map/ppermute | solution.py:22
  57.1 2.9 %collective-permute-done.16.refs_4_ = bf16[512,128]{1,0:T(8,128)(2,1)S(1)} collective-permute-done((bf16[512,128]{1,0:T(8,128)(2,1)S(1)}, bf16[512,128]{1,0:T(8,128)(2,1)S(1)}, u32[]{:S(2)}, u32[]{:S(2)}) %collective-permute-start.16) | collective-permute-done | bytes 131104 | tf_op jit(solution)/shard_map/ppermute | solution.py:22
  60.0 2.9 %collective-permute-done.11.refs_5_ = bf16[512,128]{1,0:T(8,128)(2,1)S(1)} collective-permute-done((bf16[512,128]{1,0:T(8,128)(2,1)S(1)}, bf16[512,128]{1,0:T(8,128)(2,1)S(1)}, u32[]{:S(2)}, u32[]{:S(2)}) %collective-permute-start.11) | collective-permute-done | bytes 131104 | tf_op jit(solution)/shard_map/ppermute | solution.py:22
  65.7 1.9 %collective-permute-done.18.refs_6_ = bf16[512,128]{1,0:T(8,128)(2,1)S(1)} collective-permute-done((bf16[512,128]{1,0:T(8,128)(2,1)S(1)}, bf16[512,128]{1,0:T(8,128)(2,1)S(1)}, u32[]{:S(2)}, u32[]{:S(2)}) %collective-permute-start.18) | collective-permute-done | bytes 131104 | tf_op jit(solution)/shard_map/ppermute | solution.py:22
  67.6 1.3 %shard_map.82 = bf16[528,256]{1,0:T(8,128)(2,1)S(1)} custom-call(s32[4]{0:T(128)S(1)} %pad_add_fusion.refs_0_, bf16[1024,256]{1,0:T(8,128)(2,1)S(1)} %collective-permute-done.19.refs_1_, f32[512,256]{1,0:T(8,128)S(1)} %shard_map.81.refs_2_, bf16[512,128]{1,0:T(8,128)(2,1)S(1)} %shard_map.79.refs_3_, bf16[512,128]{1,0:T(8,128)(2,1)S(1)} %collective-permute-done.16.refs_4_, ...), custom_call_target="tpu_custom_call" | custom-call | flops 1000000000 | bytes 100000000 | tf_op jit(solution)/shard_map/pallas_call | solution.py:261
  71.0 1.8 %collective-permute-start.23 = (bf16[528,128]{1,0:T(8,128)(2,1)S(1)}, bf16[528,128]{1,0:T(8,128)(2,1)S(1)}, u32[]{:S(2)}, u32[]{:S(2)}) collective-permute-start(bf16[528,128]{1,0:T(8,128)(2,1)S(1)} %get-tuple-element.56), channel_id=1, source_target_pairs={{0,16},{8,24},{16,0},{24,8},{1,17},{9,25},{17,1},{25,9},{2,18},{10... | collective-permute-start | bytes 405512 | tf_op jit(solution)/shard_map/ppermute | solution.py:22
  72.8 1.1 %collective-permute-start.21 = (bf16[528,128]{1,0:T(8,128)(2,1)S(1)}, bf16[528,128]{1,0:T(8,128)(2,1)S(1)}, u32[]{:S(2)}, u32[]{:S(2)}) collective-permute-start(bf16[528,128]{1,0:T(8,128)(2,1)S(1)} %get-tuple-element.53), channel_id=1, source_target_pairs={{0,8},{8,0},{16,24},{24,16},{1,9},{9,1},{17,25},{25,17},{2,10},{10... | collective-permute-start | bytes 405512 | tf_op jit(solution)/shard_map/ppermute | solution.py:22
  73.9 2.8 %collective-permute-done.23.message_ref = bf16[528,128]{1,0:T(8,128)(2,1)S(1)} collective-permute-done((bf16[528,128]{1,0:T(8,128)(2,1)S(1)}, bf16[528,128]{1,0:T(8,128)(2,1)S(1)}, u32[]{:S(2)}, u32[]{:S(2)}) %collective-permute-start.23) | collective-permute-done | bytes 135200 | tf_op jit(solution)/shard_map/ppermute | solution.py:22
  77.2 1.3 %collective-permute-start.24 = (bf16[528,128]{1,0:T(8,128)(2,1)S(1)}, bf16[528,128]{1,0:T(8,128)(2,1)S(1)}, u32[]{:S(2)}, u32[]{:S(2)}) collective-permute-start(bf16[528,128]{1,0:T(8,128)(2,1)S(1)} %get-tuple-element.58), channel_id=1, source_target_pairs={{0,8},{8,0},{16,24},{24,16},{1,9},{9,1},{17,25},{25,17},{2,10},{10... | collective-permute-start | bytes 405512 | tf_op jit(solution)/shard_map/ppermute | solution.py:22
  78.9 1.7 %collective-permute-start.22 = (bf16[528,128]{1,0:T(8,128)(2,1)S(1)}, bf16[528,128]{1,0:T(8,128)(2,1)S(1)}, u32[]{:S(2)}, u32[]{:S(2)}) collective-permute-start(bf16[528,128]{1,0:T(8,128)(2,1)S(1)} %get-tuple-element.55), channel_id=1, source_target_pairs={{0,16},{8,24},{16,0},{24,8},{1,17},{9,25},{17,1},{25,9},{2,18},{10... | collective-permute-start | bytes 405512 | tf_op jit(solution)/shard_map/ppermute | solution.py:22
  80.6 1.6 %collective-permute-done.24.refs_5_ = bf16[528,128]{1,0:T(8,128)(2,1)S(1)} collective-permute-done((bf16[528,128]{1,0:T(8,128)(2,1)S(1)}, bf16[528,128]{1,0:T(8,128)(2,1)S(1)}, u32[]{:S(2)}, u32[]{:S(2)}) %collective-permute-start.24) | collective-permute-done | bytes 135200 | tf_op jit(solution)/shard_map/ppermute | solution.py:22
  82.2 1.8 %collective-permute-done.22.refs_3_ = bf16[528,128]{1,0:T(8,128)(2,1)S(1)} collective-permute-done((bf16[528,128]{1,0:T(8,128)(2,1)S(1)}, bf16[528,128]{1,0:T(8,128)(2,1)S(1)}, u32[]{:S(2)}, u32[]{:S(2)}) %collective-permute-start.22) | collective-permute-done | bytes 135200 | tf_op jit(solution)/shard_map/ppermute | solution.py:22
  84.0 1.1 %shard_map.86 = bf16[1,256,512]{2,1,0:T(8,128)(2,1)} custom-call(f32[512,128]{1,0:T(8,128)S(1)} %copy-done.8, f32[16,256]{1,0:T(8,128)S(1)} %get-tuple-element.38.rows_ref.refs_1_, f32[512,128]{1,0:T(8,128)S(1)} %get-tuple-element.54.refs_2_, bf16[528,128]{1,0:T(8,128)(2,1)S(1)} %collective-permute-done.22.refs_3_, ...), custom_call_target="tpu_custom_call" | custom-call | flops 1000000000 | bytes 100000000 | tf_op jit(solution)/shard_map/pallas_call | solution.py:261
  (63 shorter events, 17.9 us)
Async XLA Ops:
  6.2 0.8 copy-start.4
  7.0 2.9 %collective-permute-start = (bf16[4,528,256]{2,1,0:T(8,128)(2,1)S(1)}, bf16[4,528,256]{2,1,0:T(8,128)(2,1)S(1)}, u32[]{:S(2)}, u32[]{:S(2)}) collective-permute-start(bf16[4,528,256]{2,1,0:T(8,128)(2,1)S(1)} %get-tuple-element.34), channel_id=1, source_target_pairs={{0,1},{1,0},{2,3},{3,2},{4,5},{5,4},{6,7},{7,6},{8,9},{9,8},{10,11... | collective-permute-start | bytes 3244040 | tf_op jit(solution)/shard_map/ppermute | solution.py:22
  7.5 7.0 %collective-permute-start.1 = (f32[1,768]{1,0:T(1,128)S(1)}, f32[1,768]{1,0:T(1,128)S(1)}, u32[]{:S(2)}, u32[]{:S(2)}) collective-permute-start(f32[1,768]{1,0:T(1,128)S(1)} %get-tuple-element.35.refs_4_.refs_2_), channel_id=1, source_target_pairs={{0,8},{8,0},{16,24},{24,16},{1,9},{9,1},{17,25},{25,17},{2,10},{10... | collective-permute-start | bytes 9224 | tf_op jit(solution)/shard_map/ppermute | solution.py:22
  10.0 1.1 %copy-start.5 = (bf16[512,640]{1,0:T(8,128)(2,1)S(1)}, bf16[512,640]{1,0:T(8,128)(2,1)}, u32[]{:S(2)}) copy-start(bf16[512,640]{1,0:T(8,128)(2,1)} %copy-done.4) | copy-start | bytes 1966084
  11.6 7.6 %collective-permute-start.4 = (bf16[528,128]{1,0:T(8,128)(2,1)S(1)}, bf16[528,128]{1,0:T(8,128)(2,1)S(1)}, u32[]{:S(2)}, u32[]{:S(2)}) collective-permute-start(bf16[528,128]{1,0:T(8,128)(2,1)S(1)} %shard_map.65.refs_6_), channel_id=1, source_target_pairs={{0,2},{1,3},{2,0},{3,1},{4,6},{5,7},{6,4},{7,5},{8,10},{9,11},{10,... | collective-permute-start | bytes 405512 | tf_op jit(solution)/shard_map/ppermute | solution.py:22
  15.0 4.2 %collective-permute-start.2 = (f32[2,768]{1,0:T(2,128)S(1)}, f32[2,768]{1,0:T(2,128)S(1)}, u32[]{:S(2)}, u32[]{:S(2)}) collective-permute-start(f32[2,768]{1,0:T(2,128)S(1)} %get-tuple-element.36.refs_0_), channel_id=1, source_target_pairs={{0,16},{8,24},{16,0},{24,8},{1,17},{9,25},{17,1},{25,9},{2,18},{10... | collective-permute-start | bytes 18440 | tf_op jit(solution)/shard_map/ppermute | solution.py:22
  16.5 9.0 %collective-permute-start.3 = (bf16[528,128]{1,0:T(8,128)(2,1)S(1)}, bf16[528,128]{1,0:T(8,128)(2,1)S(1)}, u32[]{:S(2)}, u32[]{:S(2)}) collective-permute-start(bf16[528,128]{1,0:T(8,128)(2,1)S(1)} %get-tuple-element.39.refs_4_), channel_id=1, source_target_pairs={{0,2},{1,3},{2,0},{3,1},{4,6},{5,7},{6,4},{7,5},{8,10},{9,11},{10,... | collective-permute-start | bytes 405512 | tf_op jit(solution)/shard_map/ppermute | solution.py:22
  17.5 12.2 %collective-permute-start.5 = (bf16[528,128]{1,0:T(8,128)(2,1)S(1)}, bf16[528,128]{1,0:T(8,128)(2,1)S(1)}, u32[]{:S(2)}, u32[]{:S(2)}) collective-permute-start(bf16[528,128]{1,0:T(8,128)(2,1)S(1)} %shard_map.68.refs_5_), channel_id=1, source_target_pairs={{0,2},{1,3},{2,0},{3,1},{4,6},{5,7},{6,4},{7,5},{8,10},{9,11},{10,... | collective-permute-start | bytes 405512 | tf_op jit(solution)/shard_map/ppermute | solution.py:22
  19.7 10.0 %collective-permute-start.6 = (bf16[528,128]{1,0:T(8,128)(2,1)S(1)}, bf16[528,128]{1,0:T(8,128)(2,1)S(1)}, u32[]{:S(2)}, u32[]{:S(2)}) collective-permute-start(bf16[528,128]{1,0:T(8,128)(2,1)S(1)} %shard_map.69.refs_5_), channel_id=1, source_target_pairs={{0,4},{1,5},{2,6},{3,7},{4,0},{5,1},{6,2},{7,3},{8,12},{9,13},{10,... | collective-permute-start | bytes 405512 | tf_op jit(solution)/shard_map/ppermute | solution.py:22
  26.1 8.3 %collective-permute-start.12 = (bf16[528,128]{1,0:T(8,128)(2,1)S(1)}, bf16[528,128]{1,0:T(8,128)(2,1)S(1)}, u32[]{:S(2)}, u32[]{:S(2)}) collective-permute-start(bf16[528,128]{1,0:T(8,128)(2,1)S(1)} %shard_map.70.refs_4_), channel_id=1, source_target_pairs={{0,4},{1,5},{2,6},{3,7},{4,0},{5,1},{6,2},{7,3},{8,12},{9,13},{10,... | collective-permute-start | bytes 405512 | tf_op jit(solution)/shard_map/ppermute | solution.py:22
  26.8 6.2 %collective-permute-start.13 = (bf16[528,128]{1,0:T(8,128)(2,1)S(1)}, bf16[528,128]{1,0:T(8,128)(2,1)S(1)}, u32[]{:S(2)}, u32[]{:S(2)}) collective-permute-start(bf16[528,128]{1,0:T(8,128)(2,1)S(1)} %shard_map.71.refs_3_.refs_6_), channel_id=1, source_target_pairs={{0,2},{1,3},{2,0},{3,1},{4,6},{5,7},{6,4},{7,5},{8,10},{9,11},{10,... | collective-permute-start | bytes 405512 | tf_op jit(solution)/shard_map/ppermute | solution.py:22
  29.7 14.4 %copy-start.6 = (f32[512,128]{1,0:T(8,128)}, f32[512,128]{1,0:T(8,128)S(1)}, u32[]{:S(2)}) copy-start(f32[512,128]{1,0:T(8,128)S(1)} %get-tuple-element.37.cols_ref.refs_2_.refs_0_) | copy-start | bytes 786436
  30.4 6.4 %collective-permute-start.7 = (bf16[528,128]{1,0:T(8,128)(2,1)S(1)}, bf16[528,128]{1,0:T(8,128)(2,1)S(1)}, u32[]{:S(2)}, u32[]{:S(2)}) collective-permute-start(bf16[528,128]{1,0:T(8,128)(2,1)S(1)} %get-tuple-element.42.refs_6_), channel_id=1, source_target_pairs={{0,8},{8,0},{16,24},{24,16},{1,9},{9,1},{17,25},{25,17},{2,10},{10... | collective-permute-start | bytes 405512 | tf_op jit(solution)/shard_map/ppermute | solution.py:22
  35.1 6.5 %collective-permute-start.14 = (bf16[528,128]{1,0:T(8,128)(2,1)S(1)}, bf16[528,128]{1,0:T(8,128)(2,1)S(1)}, u32[]{:S(2)}, u32[]{:S(2)}) collective-permute-start(bf16[528,128]{1,0:T(8,128)(2,1)S(1)} %get-tuple-element.47), channel_id=1, source_target_pairs={{0,16},{8,24},{16,0},{24,8},{1,17},{9,25},{17,1},{25,9},{2,18},{10... | collective-permute-start | bytes 405512 | tf_op jit(solution)/shard_map/ppermute | solution.py:22
  37.3 6.9 %collective-permute-start.8 = (bf16[528,128]{1,0:T(8,128)(2,1)S(1)}, bf16[528,128]{1,0:T(8,128)(2,1)S(1)}, u32[]{:S(2)}, u32[]{:S(2)}) collective-permute-start(bf16[528,128]{1,0:T(8,128)(2,1)S(1)} %get-tuple-element.45), channel_id=1, source_target_pairs={{0,16},{8,24},{16,0},{24,8},{1,17},{9,25},{17,1},{25,9},{2,18},{10... | collective-permute-start | bytes 405512 | tf_op jit(solution)/shard_map/ppermute | solution.py:22
  41.5 2.0 %copy-start = (bf16[1,256,2048]{2,1,0:T(8,128)(2,1)S(1)}, bf16[1,256,2048]{2,1,0:T(8,128)(2,1)}, u32[]{:S(2)}) copy-start(bf16[1,256,2048]{2,1,0:T(8,128)(2,1)} %refs_1_.1) | copy-start | bytes 3145732
  41.5 2.0 %copy-start.1 = (bf16[1,512,512]{2,1,0:T(8,128)(2,1)S(1)}, bf16[1,512,512]{2,1,0:T(8,128)(2,1)}, u32[]{:S(2)}) copy-start(bf16[1,512,512]{2,1,0:T(8,128)(2,1)} %refs_2_.1) | copy-start | bytes 1572868
  42.0 6.4 %collective-permute-start.15 = (bf16[528,128]{1,0:T(8,128)(2,1)S(1)}, bf16[528,128]{1,0:T(8,128)(2,1)S(1)}, u32[]{:S(2)}, u32[]{:S(2)}) collective-permute-start(bf16[528,128]{1,0:T(8,128)(2,1)S(1)} %get-tuple-element.49), channel_id=1, source_target_pairs={{0,8},{8,0},{16,24},{24,16},{1,9},{9,1},{17,25},{25,17},{2,10},{10... | collective-permute-start | bytes 405512 | tf_op jit(solution)/shard_map/ppermute | solution.py:22
  44.0 19.8 %collective-permute-start.19 = (bf16[1024,256]{1,0:T(8,128)(2,1)S(1)}, bf16[1024,256]{1,0:T(8,128)(2,1)S(1)}, u32[]{:S(2)}, u32[]{:S(2)}) collective-permute-start(bf16[1024,256]{1,0:T(8,128)(2,1)S(1)} %get-tuple-element.50), channel_id=1, source_target_pairs={{0,1},{1,0},{2,3},{3,2},{4,5},{5,4},{6,7},{7,6},{8,9},{9,8},{10,11... | collective-permute-start | bytes 1572872 | tf_op jit(solution)/shard_map/ppermute | solution.py:22
  44.6 10.4 %collective-permute-start.9 = (bf16[512,128]{1,0:T(8,128)(2,1)S(1)}, bf16[512,128]{1,0:T(8,128)(2,1)S(1)}, u32[]{:S(2)}, u32[]{:S(2)}) collective-permute-start(bf16[512,128]{1,0:T(8,128)(2,1)S(1)} %shard_map.75.refs_2_.refs_5_), channel_id=1, source_target_pairs={{0,4},{1,5},{2,6},{3,7},{4,0},{5,1},{6,2},{7,3},{8,12},{9,13},{10,... | collective-permute-start | bytes 393224 | tf_op jit(solution)/shard_map/ppermute | solution.py:22
  46.1 13.9 %collective-permute-start.10 = (bf16[512,128]{1,0:T(8,128)(2,1)S(1)}, bf16[512,128]{1,0:T(8,128)(2,1)S(1)}, u32[]{:S(2)}, u32[]{:S(2)}) collective-permute-start(bf16[512,128]{1,0:T(8,128)(2,1)S(1)} %shard_map.75.refs_2_.refs_5_), channel_id=1, source_target_pairs={{0,2},{1,3},{2,0},{3,1},{4,6},{5,7},{6,4},{7,5},{8,10},{9,11},{10,... | collective-permute-start | bytes 393224 | tf_op jit(solution)/shard_map/ppermute | solution.py:22
  48.4 1.0 %copy-start.7 = (f32[512,128]{1,0:T(8,128)S(1)}, f32[512,128]{1,0:T(8,128)}, u32[]{:S(2)}) copy-start(f32[512,128]{1,0:T(8,128)} %copy-done.6) | copy-start | bytes 786436
  49.7 10.3 %collective-permute-start.16 = (bf16[512,128]{1,0:T(8,128)(2,1)S(1)}, bf16[512,128]{1,0:T(8,128)(2,1)S(1)}, u32[]{:S(2)}, u32[]{:S(2)}) collective-permute-start(bf16[512,128]{1,0:T(8,128)(2,1)S(1)} %shard_map.79.refs_3_), channel_id=1, source_target_pairs={{0,4},{1,5},{2,6},{3,7},{4,0},{5,1},{6,2},{7,3},{8,12},{9,13},{10,... | collective-permute-start | bytes 393224 | tf_op jit(solution)/shard_map/ppermute | solution.py:22
  54.9 7.9 %collective-permute-start.11 = (bf16[512,128]{1,0:T(8,128)(2,1)S(1)}, bf16[512,128]{1,0:T(8,128)(2,1)S(1)}, u32[]{:S(2)}, u32[]{:S(2)}) collective-permute-start(bf16[512,128]{1,0:T(8,128)(2,1)S(1)} %collective-permute-done.9.refs_3_), channel_id=1, source_target_pairs={{0,2},{1,3},{2,0},{3,1},{4,6},{5,7},{6,4},{7,5},{8,10},{9,11},{10,... | collective-permute-start | bytes 393224 | tf_op jit(solution)/shard_map/ppermute | solution.py:22
  55.1 10.6 %collective-permute-start.17 = (bf16[512,128]{1,0:T(8,128)(2,1)S(1)}, bf16[512,128]{1,0:T(8,128)(2,1)S(1)}, u32[]{:S(2)}, u32[]{:S(2)}) collective-permute-start(bf16[512,128]{1,0:T(8,128)(2,1)S(1)} %shard_map.79.refs_3_), channel_id=1, source_target_pairs={{0,2},{1,3},{2,0},{3,1},{4,6},{5,7},{6,4},{7,5},{8,10},{9,11},{10,... | collective-permute-start | bytes 393224 | tf_op jit(solution)/shard_map/ppermute | solution.py:22
  60.0 7.6 %collective-permute-start.18 = (bf16[512,128]{1,0:T(8,128)(2,1)S(1)}, bf16[512,128]{1,0:T(8,128)(2,1)S(1)}, u32[]{:S(2)}, u32[]{:S(2)}) collective-permute-start(bf16[512,128]{1,0:T(8,128)(2,1)S(1)} %collective-permute-done.16.refs_4_), channel_id=1, source_target_pairs={{0,2},{1,3},{2,0},{3,1},{4,6},{5,7},{6,4},{7,5},{8,10},{9,11},{10,... | collective-permute-start | bytes 393224 | tf_op jit(solution)/shard_map/ppermute | solution.py:22
  68.8 1.6 %copy-start.8 = (f32[512,128]{1,0:T(8,128)S(1)}, f32[512,128]{1,0:T(8,128)}, u32[]{:S(2)}) copy-start(f32[512,128]{1,0:T(8,128)} %copy-done.6) | copy-start | bytes 786436
  68.8 1.6 %collective-permute-start.20 = (bf16[528,256]{1,0:T(8,128)(2,1)S(1)}, bf16[528,256]{1,0:T(8,128)(2,1)S(1)}, u32[]{:S(2)}, u32[]{:S(2)}) collective-permute-start(bf16[528,256]{1,0:T(8,128)(2,1)S(1)} %shard_map.82), channel_id=1, source_target_pairs={{0,1},{1,0},{2,3},{3,2},{4,5},{5,4},{6,7},{7,6},{8,9},{9,8},{10,11... | collective-permute-start | bytes 811016 | tf_op jit(solution)/shard_map/ppermute | solution.py:22
  71.0 5.7 %collective-permute-start.23 = (bf16[528,128]{1,0:T(8,128)(2,1)S(1)}, bf16[528,128]{1,0:T(8,128)(2,1)S(1)}, u32[]{:S(2)}, u32[]{:S(2)}) collective-permute-start(bf16[528,128]{1,0:T(8,128)(2,1)S(1)} %get-tuple-element.56), channel_id=1, source_target_pairs={{0,16},{8,24},{16,0},{24,8},{1,17},{9,25},{17,1},{25,9},{2,18},{10... | collective-permute-start | bytes 405512 | tf_op jit(solution)/shard_map/ppermute | solution.py:22
  72.8 5.7 %collective-permute-start.21 = (bf16[528,128]{1,0:T(8,128)(2,1)S(1)}, bf16[528,128]{1,0:T(8,128)(2,1)S(1)}, u32[]{:S(2)}, u32[]{:S(2)}) collective-permute-start(bf16[528,128]{1,0:T(8,128)(2,1)S(1)} %get-tuple-element.53), channel_id=1, source_target_pairs={{0,8},{8,0},{16,24},{24,16},{1,9},{9,1},{17,25},{25,17},{2,10},{10... | collective-permute-start | bytes 405512 | tf_op jit(solution)/shard_map/ppermute | solution.py:22
  77.2 5.1 %collective-permute-start.24 = (bf16[528,128]{1,0:T(8,128)(2,1)S(1)}, bf16[528,128]{1,0:T(8,128)(2,1)S(1)}, u32[]{:S(2)}, u32[]{:S(2)}) collective-permute-start(bf16[528,128]{1,0:T(8,128)(2,1)S(1)} %get-tuple-element.58), channel_id=1, source_target_pairs={{0,8},{8,0},{16,24},{24,16},{1,9},{9,1},{17,25},{25,17},{2,10},{10... | collective-permute-start | bytes 405512 | tf_op jit(solution)/shard_map/ppermute | solution.py:22
  78.9 5.1 %collective-permute-start.22 = (bf16[528,128]{1,0:T(8,128)(2,1)S(1)}, bf16[528,128]{1,0:T(8,128)(2,1)S(1)}, u32[]{:S(2)}, u32[]{:S(2)}) collective-permute-start(bf16[528,128]{1,0:T(8,128)(2,1)S(1)} %get-tuple-element.55), channel_id=1, source_target_pairs={{0,16},{8,24},{16,0},{24,8},{1,17},{9,25},{17,1},{25,9},{2,18},{10... | collective-permute-start | bytes 405512 | tf_op jit(solution)/shard_map/ppermute | solution.py:22
  (2 other events, 1.4 us)

commit v4 on v3

v4 whole, which is shorter than its diff:
```python
import functools

import jax
import jax.numpy as jnp
from jax import lax
from jax.experimental import pallas as pl
from jax.experimental.pallas import tpu as pltpu
from jax.sharding import PartitionSpec as P

TAIL = 16
LIFT = 2.0**15
TINY = 1e-30
F32, BF16 = jnp.float32, jnp.bfloat16
VMEM = pl.BlockSpec(memory_space=pltpu.VMEM)
SMEM = pl.BlockSpec(memory_space=pltpu.SMEM)
HBM = pl.BlockSpec(memory_space=pltpu.HBM)
FIRST_GRANT = 8
SPLIT = 2


def exchange(x, axis, flip):
    return lax.ppermute(x, axis, [(i, i ^ flip) for i in range(lax.axis_size(axis))])


def put(ref, value):
    rows = value.shape[0]
    top = jnp.maximum(jnp.max(jnp.abs(value), axis=0, keepdims=True), TINY).astype(BF16).astype(F32)
    ref[rows:, :] = jnp.broadcast_to(top, (TAIL, value.shape[1])).astype(BF16)
    z = value * (LIFT / top)
    z2 = z * z
    z4 = z2 * z2
    z8 = z4 * z4
    ref[:rows, :] = jnp.where(z < 0, -z8, z8).astype(BF16)


def get(ref):
    rows = ref.shape[0] - TAIL
    top = ref[rows:, :][:1, :].astype(F32) * (1.0 / LIFT)
    y = ref[:rows, :].astype(F32)
    square = lax.rsqrt(lax.rsqrt(jnp.abs(y) + 1e-37))
    size = square * lax.rsqrt(square)
    return jnp.where(y < 0, -size, size) * top


def first_kernel(
    here_ref, grads_hbm, inputs_hbm, out_decay, in_decay, sent_ref, turned_ref, rest_ref, own_ref, rates_ref, *scratch
):
    grads_ref, inputs_ref, sems = scratch
    core, chip = here_ref[0], here_ref[1]
    width = out_decay.shape[1]
    chips, _, rows = own_ref.shape
    sem = iter(range(sems.shape[0]))

    def copy(source, into):
        out = pltpu.make_async_copy(source, into, sems.at[next(sem)])
        out.start()
        return out

    def load(o, of, into):
        start = pl.multiple_of((2 * (chip ^ o) + of) * rows, rows)
        return copy(inputs_hbm.at[0, :, pl.ds(start, rows)], into)

    lead = copy(grads_hbm.at[0], grads_ref)
    theirs = [load(o, 1 - core, inputs_ref.at[i]) for i, o in enumerate(range(1, chips, 2))]
    others = [load(o, 1 - core, rest_ref.at[i]) for i, o in enumerate(range(0, chips, 2))]
    others += [load(o, core, own_ref.at[o]) for o in range(chips)]
    others.append(copy(out_decay, rates_ref.at[:, pl.ds(0, width)]))
    others.append(copy(in_decay, rates_ref.at[:, pl.ds(width, rows)]))
    lead.wait()
    turned_ref[...] = grads_ref[...].T
    for i, arrival in enumerate(theirs):
        arrival.wait()
        put(sent_ref.at[i], jnp.dot(turned_ref[...], inputs_ref[i], preferred_element_type=F32))
    for arrival in others:
        arrival.wait()


def rest_kernel(turned_ref, inputs_ref, sent_ref):
    for i in range(inputs_ref.shape[0]):
        put(sent_ref.at[i], jnp.dot(turned_ref[...], inputs_ref[i], preferred_element_type=F32))


def sum_kernel(part, offsets, picks, n, weighs, turned_ref, own_ref, theirs_ref, *refs):
    messages, outs = refs[:n], refs[n + (2 if weighs else 0) :]
    lanes = outs[0].shape[-1]
    columns = pl.ds(part * lanes, lanes)
    for i, o in enumerate(offsets):
        total = jnp.dot(turned_ref[...], own_ref[o, :, columns], preferred_element_type=F32)
        total = total + get(theirs_ref.at[o // 2, :, columns])
        for array, j in picks[i]:
            total = total + get(messages[array].at[j])
        if len(outs) > 1:
            outs[1][...] = total
        if weighs:
            cols_ref, rows_ref = refs[n : n + 2]
            total = weight(cols_ref, rows_ref.at[:, columns], weighs) * total
        put(outs[0].at[i] if len(outs[0].shape) == 3 else outs[0], total)


def turn_kernel(core_ref, a_ref, s_ref, own_ref, send_ref, s_out):
    core = core_ref[0]
    rows = a_ref.shape[1]
    for i in range(own_ref.shape[0] // rows):
        for of, out in ((core, own_ref), (1 - core, send_ref)):
            columns = pl.ds(pl.multiple_of((2 * i + of) * rows, rows), rows)
            out[i * rows : (i + 1) * rows, :] = a_ref[0, :, columns].T
    s_out[...] = s_ref[0].T


def weight(cols_ref, rows_ref, j):
    return cols_ref[:, j : j + 1] * rows_ref[j : j + 1, :]


def weighed(places, cols_ref, rows_ref, messages, value):
    for j, message in zip(places, messages):
        value = value + weight(cols_ref, rows_ref, j) * get(message)
    return value


def step_kernel(into_value, into_total, more, *refs):
    n = len(into_value)
    value_ref, total_ref, cols_ref, rows_ref = refs[:4]
    messages, outs = refs[4 : 4 + n], refs[4 + n :]
    outs[0][...] = weighed(into_value, cols_ref, rows_ref, messages, value_ref[...])
    total = weight(cols_ref, rows_ref, into_total[0]) * total_ref[...]
    total = weighed(into_total[1:], cols_ref, rows_ref, messages, total)
    put(outs[1], total)
    if more:
        outs[2][...] = total


def cross_kernel(places, part, value_ref, total_ref, cols_ref, rows_ref, message_ref, value_out, sent_ref):
    into_value, mix_own, mix_got = places
    lanes = sent_ref.shape[1]
    columns = slice(part * lanes, (part + 1) * lanes)
    at = rows_ref.at[:, columns]
    got = get(message_ref)
    value_out[...] = value_ref[:, columns] + weight(cols_ref, at, into_value) * got
    put(sent_ref, weight(cols_ref, at, mix_own) * total_ref[:, columns] + weight(cols_ref, at, mix_got) * got)


def side_s_kernel(places, value_ref, s_ref, cols_ref, rows_ref, *refs):
    upper = weighed(places, cols_ref, rows_ref, refs[: len(places)], value_ref[...])
    refs[-1][...] = jnp.dot(s_ref[...], upper.astype(BF16), preferred_element_type=F32).astype(BF16)


def stack_kernel(*refs):
    for i, ref in enumerate(refs[:-1]):
        refs[-1][i] = ref[...]


def side_a_kernel(picks, has_before, *refs):
    refs = list(refs)
    at_ref, a_ref = refs.pop(0), refs.pop(0)
    solved = refs.pop(0)[...] if has_before else None
    for array, block, place in picks:
        operand = refs[array][...] if block is None else refs[array][block]
        lanes = operand.shape[1]
        features = pl.ds(pl.multiple_of(at_ref[place], lanes), lanes)
        term = jnp.dot(operand, a_ref[features, :], preferred_element_type=F32)
        solved = term if solved is None else solved + term
    if refs[-1].dtype == F32:
        refs[-1][...] = solved
    else:
        put(refs[-1], solved)


def joint_kernel(total_at, sent_at, own_ref, theirs_ref, cols_ref, rows_ref, value_ref, total_ref, *sent_refs):
    value = own_ref[...] + get(theirs_ref)
    value_ref[...] = value
    total_ref[...] = weight(cols_ref, rows_ref, total_at) * value
    for i, sent in enumerate(sent_refs):
        lanes = sent.shape[1]
        columns = slice(i * lanes, (i + 1) * lanes)
        total = total_ref[:, columns]
        if sent_at[i] is not None:
            total = weight(cols_ref, rows_ref.at[:, columns], sent_at[i]) * total
        put(sent, total)


def last_kernel(places, cols_ref, rows_ref, *refs):
    out_ref = refs[-1]
    for i, place in enumerate(places):
        value_ref, message_ref = refs[2 * i : 2 * i + 2]
        lanes = value_ref.shape[1]
        columns = slice(i * lanes, (i + 1) * lanes)
        lower = weighed([place], cols_ref, rows_ref.at[:, columns], [message_ref], value_ref[...])
        out_ref[0, columns, :] = lower.T.astype(BF16)


def digits(layers):
    step, out = 1, []
    while step < layers:
        size = min(4, layers // step)
        out.append((step, size))
        step *= size
    return out


def weights_kernel(size, last, n, me_ref, *refs):
    groups, (below_ref, above_ref) = refs[:n], refs[n : n + 2]
    cols_ref, rows_ref, *state_ref = refs[n + 2 :]
    group = [ref[i : i + 1, :] for ref in groups for i in range(ref.shape[0])]
    below, above = below_ref[...], above_ref[...]
    ones, zeros = jnp.ones_like(below), jnp.zeros_like(below)

    def product(holds):
        out = ones
        for flip, vector in enumerate(group):
            out = out * jnp.where(holds(me ^ flip), vector, ones)
        return out

    def pick(*cases):
        out = zeros
        for at, vector in cases:
            out = jnp.where(me == at, vector, out)
        return out

    stack = [group[0]]
    for me, factor in ((me_ref[0], below), (size - 1 - me_ref[0], above)):
        if not last:
            for flip in range(1, size):
                peer = me ^ flip
                between = product(lambda q: (q > me) & (q < peer))
                stack.append(jnp.where(peer > me, factor * between, zeros))
            for flip in range(size):
                stack.append(product(lambda q: q < me ^ flip))
        elif size == 4:
            rates, beside = group[:2]
            far = factor * beside
            stack.append(pick((0, factor), (2, factor)))
            stack.append(pick((2, ones), (3, beside)))
            stack.append(pick((2, rates), (3, ones)))
            stack.append(pick((0, far), (1, factor)))
            stack.append(pick((0, far), (1, factor)))
            stack.append(pick((1, ones), (3, ones)))
            stack.append(pick((0, ones), (1, rates)))
            stack.append(pick((0, factor), (1, factor), (2, factor)))
            stack.append(pick((0, ones), (1, ones), (2, ones), (3, beside)))
        else:
            stack.append(pick((0, factor)))
    width = cols_ref.shape[0]
    stack += [zeros] * (cols_ref.shape[1] - len(stack))
    table = jnp.concatenate(stack, axis=0)
    cols_ref[...] = table[:, :width].T
    rows_ref[...] = table[: rows_ref.shape[0], width:]
    if not last:
        me = me_ref[0]
        before = product(lambda q: q < me)
        state_ref[0][...] = jnp.concatenate([product(lambda q: q >= 0), below * before, above * before], axis=0)


def weight_places(size, last):
    out = []
    for i in range(2):
        if not last:
            n = 2 * size - 1
            out.append((list(range(1 + i * n, i * n + size)), list(range(i * n + size, 1 + i * n + n))))
        elif size == 4:
            b = 1 + 9 * i
            out.append(([((1, 2), None, (b, b + 1, b + 2), b + 3), ((2, 1), b + 8, (b + 4, b + 5, b + 6), b + 7)], None))
        else:
            out.append((None, 1 + i))
    return out


def shards(activations, out_grads, a_inverse, s_inverse, in_decay, out_decay):
    layers, peers = lax.axis_size("layer"), lax.axis_size("dp")
    layer, here = lax.axis_index("layer"), lax.axis_index("dp")
    core, chip = here % 2, here // 2
    chips = peers // 2
    rows = a_inverse.shape[1]
    width = out_grads.shape[2]
    tokens = activations.shape[1]
    split = SPLIT if rows % (128 * SPLIT) == 0 else 1
    lanes = rows // split

    def shape(*dims, dtype=F32):
        return jax.ShapeDtypeStruct(dims, dtype)

    def message(n):
        return shape(width + TAIL, n, dtype=BF16)

    def call(kernel, out_shape, *operands, scalars=0, grant=4 * 2**20, hbm=0, scratch=(), after=()):
        several = isinstance(out_shape, (list, tuple))
        if after:
            inner, count = kernel, len(operands)

            def kernel(*refs):
                inner(*refs[:count], *refs[count + len(after) :])

        return pl.pallas_call(
            kernel,
            out_shape=out_shape,
            in_specs=[SMEM] * scalars
            + [HBM] * hbm
            + [VMEM] * (len(operands) - scalars - hbm)
            + [pl.BlockSpec(memory_space=pl.ANY)] * len(after),
            out_specs=[VMEM] * len(out_shape) if several else VMEM,
            scratch_shapes=scratch,
            compiler_params=pltpu.CompilerParams(vmem_limit_bytes=grant),
            cost_estimate=pl.CostEstimate(flops=10**9, bytes_accessed=10**8, transcendentals=0),
        )(*operands, *after)

    def scalar(x):
        return x.reshape(1).astype(jnp.int32)

    odd, even = list(range(1, chips, 2)), list(range(0, chips, 2))
    sent, turned, rest, inputs, rates = call(
        first_kernel,
        [
            shape(len(odd), width + TAIL, rows, dtype=BF16),
            shape(width, tokens, dtype=BF16),
            shape(len(even), tokens, rows, dtype=BF16),
            shape(chips, tokens, rows, dtype=BF16),
            shape(1, width + rows),
        ],
        jnp.stack([core, chip]).astype(jnp.int32),
        *(pltpu.with_memory_space_constraint(x, pltpu.HBM) for x in (out_grads, activations, out_decay, in_decay)),
        scalars=1,
        hbm=4,
        grant=FIRST_GRANT * 2**20,
        scratch=[
            pltpu.VMEM((tokens, width), BF16),
            pltpu.VMEM((len(odd), tokens, rows), BF16),
            pltpu.SemaphoreType.DMA((2 * chips + 3,)),
        ],
    )
    theirs = {1: exchange(sent, "dp", 1)}
    sent = call(rest_kernel, shape(len(even), width + TAIL, rows, dtype=BF16), turned, rest, after=(sent,))
    theirs[0] = exchange(sent, "dp", 1)
    group = [rates, exchange(rates, "layer", 1)]

    levels = [1 << b for b in range(chips.bit_length() - 1)]
    received = [{} for _ in range(split)]
    latest = []

    def blocks(part, offsets, outs, weighs=None, weights=()):
        heard = [[(got, j) for got, j in received[part].get(o, [])] for o in offsets]
        arrays = list({id(got): got for some in heard for got, _ in some}.values())
        picks = [[([id(x) for x in arrays].index(id(got)), j) for got, j in some] for some in heard]
        outs = call(
            functools.partial(sum_kernel, part, offsets, picks, len(arrays), weighs),
            outs,
            turned,
            inputs,
            theirs[offsets[0] % 2],
            *arrays,
            *(weights if weighs else ()),
            after=latest[-1:],
        )
        latest.append(outs[0])
        return outs

    held = []
    for i, level in enumerate(levels):
        offsets = list(range(level, chips, 2 * level))
        soon, held_next = (offsets, []) if level == levels[-1] else (offsets[1:], offsets[:1])
        for part in range(split):
            for at, some in [(level, soon)] + held:
                outs = [shape(len(some), width + TAIL, lanes, dtype=BF16)]
                [sent] = blocks(part, some, outs)
                got = exchange(sent, "dp", 2 * at)
                received[part].update({o ^ at: received[part].get(o ^ at, []) + [(got, j)] for j, o in enumerate(some)})
        held = [(level, held_next)] if held_next else []

    ups, downs = [], []
    below, above = rates, jnp.ones_like(rates)
    for step, size in digits(layers):
        last = step * size == layers
        if step > 1:
            group = [own, exchange(own, "layer", step)]
        if size == 4 and not last:
            group = [jnp.concatenate(group, axis=0)]
            group.append(exchange(group[0], "layer", 2 * step))
        cols, in_rows, *state = call(
            functools.partial(weights_kernel, size, last, len(group)),
            [shape(width, 128), shape(24, rows)] + [shape(3, width + rows)] * (not last),
            scalar(layer // step % size),
            *group,
            below,
            above,
            scalars=1,
            after=latest[-1:],
        )
        if not last:
            own, below, above = state[0][:1], state[0][1:2], state[0][2:]
        for solve, places in zip((ups, downs), weight_places(size, last)):
            solve.append((step, size, cols, in_rows, *places))
    a_own, a_theirs, s_turned = call(
        turn_kernel,
        [shape(chips * rows, rows, dtype=BF16)] * 2 + [shape(width, width, dtype=BF16)],
        scalar(core),
        a_inverse,
        s_inverse,
        scalars=1,
        after=latest[-1:],
    )
    a_theirs = exchange(a_theirs, "dp", 1)

    def steps(solve, value, total, sent, part=0):
        n = value.shape[1]
        for i, (step, size, cols, in_rows, into_value, into_total) in enumerate(solve[:-1]):
            more = i + 1 < len(solve)
            outs = [shape(width, n), message(n)] + [shape(width, n)] * more
            kernel = functools.partial(step_kernel, into_value, into_total, more)
            others = [exchange(sent, "layer", flip * step) for flip in range(1, size)]
            value, sent, total = call(kernel, outs, value, total, cols, in_rows[:, part * n : (part + 1) * n], *others)
        return value, total, sent

    def order_of(solve, part):
        step, size, _, _, orders, place = solve[-1]
        if orders is None:
            return (step,), None, None, place
        (first, second), *places = orders[part % len(orders)]
        return (first * step, second * step), *places

    def cross(solve, part, value, total, sent):
        _, _, cols, in_rows, *_ = solve[-1]
        flips, _, places, _ = order_of(solve, part)
        n = sent.shape[1]
        got = exchange(sent, "layer", flips[0])
        if len(flips) == 1:
            return value, got
        whole = value.shape[1] > n
        at = in_rows if whole or n == rows else in_rows[:, part * n : (part + 1) * n]
        kernel = functools.partial(cross_kernel, places, part if whole else 0)
        value, sent = call(kernel, [shape(width, n), message(n)], value, total, cols, at, got)
        return value, exchange(sent, "layer", flips[1])

    _, _, cols, in_rows, *_ = ups[-1]
    applied = []
    for part in range(split):
        at = in_rows[:, part * lanes : (part + 1) * lanes]
        first = order_of(ups, part)[1] if len(ups) == 1 else None
        sent, value = blocks(part, [0], [message(lanes), shape(width, lanes)], first, (cols, in_rows))
        value, total, sent = steps(ups, value, value, sent, part)
        value, got = cross(ups, part, value, total, sent)
        kernel = functools.partial(side_s_kernel, [order_of(ups, part)[3]])
        applied.append(
            call(kernel, shape(width, lanes, dtype=BF16), value, s_turned, cols, at, got, after=applied[-1:])
        )

    def stack(items, after=()):
        return call(stack_kernel, shape(len(items), width, lanes, dtype=BF16), *items, after=after)

    have = [{0: (rows_of, None)} for rows_of in applied]
    arrivals = [[(part, 0) for part in range(split)]]

    def send(level, batch, after=()):
        items = [have[part][o] for part, o in batch]
        if len(items) == 1 and items[0][1] is None:
            got = exchange(items[0][0], "dp", 2 * level)
        else:
            got = exchange(stack([x if i is None else x[i] for x, i in items], after), "dp", 2 * level)
        came = [(part, o ^ level) for part, o in batch]
        have_of = [(got, i if len(batch) > 1 or items[0][1] is not None else None) for i in range(len(batch))]
        for (part, o), where in zip(came, have_of):
            have[part][o] = where
        return came, got

    for part in range(split):
        for level in reversed(levels[1:]):
            arrivals[0] += send(level, [(part, o) for o in list(have[part])])[0]
    if chips > 1:
        came, got = send(1, [(0, 0)])
        arrivals.append(came)
        for part in range(split):
            batch = [(part, o) for o in list(have[part]) if o > 1 and o % 2 == 0]
            batch += [(part + 1, 0)] if part + 1 < split else []
            if batch:
                came, _ = send(1, batch, [got])
                if part + 1 < split:
                    arrivals[-1] += came
                else:
                    arrivals.append(came)

    own, others, done = None, None, []
    for chosen in arrivals:
        arrays = list({id(have[part][o][0]): have[part][o][0] for part, o in chosen}.values())
        places = jnp.stack([(chip ^ o) * rows + part * lanes for part, o in chosen]).astype(jnp.int32)
        picks = [
            ([id(x) for x in arrays].index(id(have[part][o][0])), have[part][o][1], i)
            for i, (part, o) in enumerate(chosen)
        ]

        def product(a, before, out_shape, after=()):
            before = [] if before is None else [before]
            kernel = functools.partial(side_a_kernel, picks, bool(before))
            return call(kernel, out_shape, places, a, *before, *arrays, scalars=1, after=after)

        final = chosen is arrivals[-1]
        others = product(a_theirs, others, message(rows) if final else shape(width, rows), done)
        own = product(a_own, own, shape(width, rows))
        done = [own]
    others = exchange(others, "dp", 1)

    pieces = split if len(downs) == 1 and downs[-1][1] == 4 else 1
    outs = [shape(width, rows)] * 2 + [message(rows // pieces)] * pieces
    first = [order_of(downs, part)[1] if len(downs) == 1 else None for part in range(pieces)]
    _, _, cols, in_rows, *_ = downs[0]
    value, total, *sent = call(functools.partial(joint_kernel, 0, first), outs, own, others, cols, in_rows)
    if len(downs) > 1:
        value, total, sent[0] = steps(downs, value, total, sent[0])
    operands = [x for part in range(pieces) for x in cross(downs, part, value, total, sent[part])]
    _, _, cols, in_rows, *_ = downs[-1]
    places = [order_of(downs, part)[3] for part in range(pieces)]
    return call(functools.partial(last_kernel, places), shape(1, rows, width, dtype=BF16), cols, in_rows, *operands)


def solution(mesh):
    placed = (
        P("layer", "dp", None),
        P("layer", "dp", None),
        P("layer", "dp", None),
        P("layer", None, None),
        P("layer", "dp"),
        P("layer", None),
    )
    return jax.shard_map(
        shards, mesh=mesh, in_specs=placed, out_specs=P("layer", "dp", None), check_vma=False
    )
```

time: 85.3 us -> 76.3 us (0.89)
  starting transfers between devices: 34.2 us -> 27.2 us
  local copies, waits for them, and re-layouts: 4.24 us -> 1.11 us
  waiting for transfers between devices: 27.3 us -> 30 us
  Pallas kernels: 18.9 us -> 17.3 us
    ppermute x25 -> x24, starting transfers between devices: 34.2 us -> 27.2 us  [exchange(): lax.ppermute(x, axis, [(i, i ^ flip) for i in range(lax.axis_size(axis))])]
    unnamed x18 -> x10, local copies, waits for them, and re-layouts: 4.24 us -> 1.11 us
    ppermute x25 -> x24, waiting for transfers between devices: 27.3 us -> 30 us  [exchange(): lax.ppermute(x, axis, [(i, i ^ flip) for i in range(lax.axis_size(axis))])]
    pallas_call x23 -> x27, Pallas kernels: 18.9 us -> 17.3 us  [call(): pl.pallas_call(kernel, out_shape=out_shape, in_specs=[SMEM] * scalars + [...]
  transfers between devices with their start and end apart: 25 -> 24, of which waited for: 13 -> 16; matrix products, arithmetic and copies ran while one was open for 0% -> 0% of each run, Pallas kernels for 13% -> 16%
where the time goes in v4:
time: 76.3 us; the launch traced here: 76.2 us
  waiting for transfers between devices  30 us (39%)
  starting transfers between devices  27.2 us (36%)
  Pallas kernels  17.3 us (23%)
  local copies, waits for them, and re-layouts  1.11 us (1%)
    ppermute x24, waiting for transfers between devices, exchange(): lax.ppermute(x, axis, [(i, i ^ flip) for i in range(lax.axis_size(axis))])  30 us
    ppermute x24, starting transfers between devices, exchange(): lax.ppermute(x, axis, [(i, i ^ flip) for i in range(lax.axis_size(axis))])  27.2 us
    pallas_call x27, Pallas kernels, call(): pl.pallas_call(kernel, out_shape=out_shape, in_specs=[SMEM] * scalars + [...  17.3 us
  transfers between devices with their start and end apart: 24, of which 16 were waited for; matrix products, arithmetic and copies ran while one was open for 0% of the time, Pallas kernels for 16%

profile of v4, /device:TPU:0, one launch (start us, length us, event | category | flops | bytes accessed | tf_op | source)
XLA Modules:
  0.0 76.2 jit_solution(14399267532401068396)
XLA Ops:
  0.1 3.5 %shard_map.64 = (bf16[2,528,256]{2,1,0:T(8,128)(2,1)S(1)}, bf16[512,640]{1,0:T(8,128)(2,1)S(1)}, bf16[2,640,256]{2,1,0:T(8,128)(2,1)S(1)}, bf16[4,640,256]{2,1,0:T(8,128)(2,1)S(1)}, f32[1,768]{1,0:T(1,128)S(1)}) custom-call(s32[2]{0:T(128)S(1)} %pad_add_fusion.here_ref, bf16[1,640,512]{2,1,0:T(8,128)(2,1)} %grads_hbm.1, bf16[1,640,2048]{2,1,0:T(8,128)(2,1)} %inputs_hbm.1, ...), custom_call_target="tpu_custom_call" | custom-call | flops 1000000000 | bytes 100000000 | tf_op jit(solution)/shard_map/pallas_call | solution.py:292
  4.1 1.0 %shard_map.65 = bf16[2,528,256]{2,1,0:T(8,128)(2,1)S(1)} custom-call(bf16[512,640]{1,0:T(8,128)(2,1)S(1)} %get-tuple-element.32.refs_0_.turned_ref, bf16[2,640,256]{2,1,0:T(8,128)(2,1)S(1)} %get-tuple-element.35.refs_1_, bf16[2,528,256]{2,1,0:T(8,128)(2,1)S(1)} %get-tuple-element.34.refs_2_), custom_call_target="tpu_custom_call" | custom-call | flops 1000000000 | bytes 100000000 | tf_op jit(solution)/shard_map/pallas_call | solution.py:292
  6.1 3.0 %collective-permute-start.4 = (bf16[1,528,128]{2,1,0:T(8,128)(2,1)S(1)}, bf16[1,528,128]{2,1,0:T(8,128)(2,1)S(1)}, u32[]{:S(2)}, u32[]{:S(2)}) collective-permute-start(bf16[1,528,128]{2,1,0:T(8,128)(2,1)S(1)} %shard_map.66.refs_3_), channel_id=1, source_target_pairs={{0,2},{1,3},{2,0},{3,1},{4,6},{5,7},{6,4},{7,5},{8,10},{9,11},{10,... | collective-permute-start | bytes 405512 | tf_op jit(solution)/shard_map/ppermute | solution.py:22
  9.1 1.5 %collective-permute-start = (f32[1,768]{1,0:T(1,128)S(1)}, f32[1,768]{1,0:T(1,128)S(1)}, u32[]{:S(2)}, u32[]{:S(2)}) collective-permute-start(f32[1,768]{1,0:T(1,128)S(1)} %get-tuple-element.31.refs_1_.refs_3_), channel_id=1, source_target_pairs={{0,8},{8,0},{16,24},{24,16},{1,9},{9,1},{17,25},{25,17},{2,10},{10... | collective-permute-start | bytes 9224 | tf_op jit(solution)/shard_map/ppermute | solution.py:22
  10.6 1.1 %copy-done.3 = bf16[512,640]{1,0:T(8,128)(2,1)S(1)} copy-done((bf16[512,640]{1,0:T(8,128)(2,1)S(1)}, bf16[512,640]{1,0:T(8,128)(2,1)}, u32[]{:S(2)}) %copy-start.3) | copy-done | bytes 655384
  13.5 2.8 %collective-permute-start.5 = (bf16[1,528,128]{2,1,0:T(8,128)(2,1)S(1)}, bf16[1,528,128]{2,1,0:T(8,128)(2,1)S(1)}, u32[]{:S(2)}, u32[]{:S(2)}) collective-permute-start(bf16[1,528,128]{2,1,0:T(8,128)(2,1)S(1)} %shard_map.68.refs_3_), channel_id=1, source_target_pairs={{0,4},{1,5},{2,6},{3,7},{4,0},{5,1},{6,2},{7,3},{8,12},{9,13},{10,... | collective-permute-start | bytes 405512 | tf_op jit(solution)/shard_map/ppermute | solution.py:22
  16.8 1.6 %collective-permute-start.6 = (bf16[1,528,128]{2,1,0:T(8,128)(2,1)S(1)}, bf16[1,528,128]{2,1,0:T(8,128)(2,1)S(1)}, u32[]{:S(2)}, u32[]{:S(2)}) collective-permute-start(bf16[1,528,128]{2,1,0:T(8,128)(2,1)S(1)} %shard_map.69.refs_4_), channel_id=1, source_target_pairs={{0,2},{1,3},{2,0},{3,1},{4,6},{5,7},{6,4},{7,5},{8,10},{9,11},{10,... | collective-permute-start | bytes 405512 | tf_op jit(solution)/shard_map/ppermute | solution.py:22
  18.4 1.0 %collective-permute-done.3.refs_3_ = bf16[1,528,128]{2,1,0:T(8,128)(2,1)S(1)} collective-permute-done((bf16[1,528,128]{2,1,0:T(8,128)(2,1)S(1)}, bf16[1,528,128]{2,1,0:T(8,128)(2,1)S(1)}, u32[]{:S(2)}, u32[]{:S(2)}) %collective-permute-start.3) | collective-permute-done | bytes 135200 | tf_op jit(solution)/shard_map/ppermute | solution.py:22
  19.9 2.0 %collective-permute-start.9 = (bf16[1,528,128]{2,1,0:T(8,128)(2,1)S(1)}, bf16[1,528,128]{2,1,0:T(8,128)(2,1)S(1)}, u32[]{:S(2)}, u32[]{:S(2)}) collective-permute-start(bf16[1,528,128]{2,1,0:T(8,128)(2,1)S(1)} %shard_map.70.refs_3_), channel_id=1, source_target_pairs={{0,4},{1,5},{2,6},{3,7},{4,0},{5,1},{6,2},{7,3},{8,12},{9,13},{10,... | collective-permute-start | bytes 405512 | tf_op jit(solution)/shard_map/ppermute | solution.py:22
  22.6 3.6 %collective-permute-done.6.refs_4_ = bf16[1,528,128]{2,1,0:T(8,128)(2,1)S(1)} collective-permute-done((bf16[1,528,128]{2,1,0:T(8,128)(2,1)S(1)}, bf16[1,528,128]{2,1,0:T(8,128)(2,1)S(1)}, u32[]{:S(2)}, u32[]{:S(2)}) %collective-permute-start.6) | collective-permute-done | bytes 135200 | tf_op jit(solution)/shard_map/ppermute | solution.py:22
  26.8 2.0 %collective-permute-start.7 = (bf16[528,128]{1,0:T(8,128)(2,1)S(1)}, bf16[528,128]{1,0:T(8,128)(2,1)S(1)}, u32[]{:S(2)}, u32[]{:S(2)}) collective-permute-start(bf16[528,128]{1,0:T(8,128)(2,1)S(1)} %get-tuple-element.40.refs_7_), channel_id=1, source_target_pairs={{0,8},{8,0},{16,24},{24,16},{1,9},{9,1},{17,25},{25,17},{2,10},{10... | collective-permute-start | bytes 405512 | tf_op jit(solution)/shard_map/ppermute | solution.py:22
  29.5 1.6 %collective-permute-start.11 = (bf16[528,128]{1,0:T(8,128)(2,1)S(1)}, bf16[528,128]{1,0:T(8,128)(2,1)S(1)}, u32[]{:S(2)}, u32[]{:S(2)}) collective-permute-start(bf16[528,128]{1,0:T(8,128)(2,1)S(1)} %get-tuple-element.45), channel_id=1, source_target_pairs={{0,16},{8,24},{16,0},{24,8},{1,17},{9,25},{17,1},{25,9},{2,18},{10... | collective-permute-start | bytes 405512 | tf_op jit(solution)/shard_map/ppermute | solution.py:22
  32.2 1.5 %collective-permute-start.8 = (bf16[528,128]{1,0:T(8,128)(2,1)S(1)}, bf16[528,128]{1,0:T(8,128)(2,1)S(1)}, u32[]{:S(2)}, u32[]{:S(2)}) collective-permute-start(bf16[528,128]{1,0:T(8,128)(2,1)S(1)} %get-tuple-element.43), channel_id=1, source_target_pairs={{0,16},{8,24},{16,0},{24,8},{1,17},{9,25},{17,1},{25,9},{2,18},{10... | collective-permute-start | bytes 405512 | tf_op jit(solution)/shard_map/ppermute | solution.py:22
  34.3 1.6 %collective-permute-done.11.message_ref = bf16[528,128]{1,0:T(8,128)(2,1)S(1)} collective-permute-done((bf16[528,128]{1,0:T(8,128)(2,1)S(1)}, bf16[528,128]{1,0:T(8,128)(2,1)S(1)}, u32[]{:S(2)}, u32[]{:S(2)}) %collective-permute-start.11) | collective-permute-done | bytes 135200 | tf_op jit(solution)/shard_map/ppermute | solution.py:22
  37.8 1.2 %collective-permute-start.15 = (bf16[512,128]{1,0:T(8,128)(2,1)S(1)}, bf16[512,128]{1,0:T(8,128)(2,1)S(1)}, u32[]{:S(2)}, u32[]{:S(2)}) collective-permute-start(bf16[512,128]{1,0:T(8,128)(2,1)S(1)} %shard_map.76.refs_5_.refs_2_), channel_id=1, source_target_pairs={{0,2},{1,3},{2,0},{3,1},{4,6},{5,7},{6,4},{7,5},{8,10},{9,11},{10,... | collective-permute-start | bytes 393224 | tf_op jit(solution)/shard_map/ppermute | solution.py:22
  39.0 3.0 %collective-permute-start.13 = (bf16[512,128]{1,0:T(8,128)(2,1)S(1)}, bf16[512,128]{1,0:T(8,128)(2,1)S(1)}, u32[]{:S(2)}, u32[]{:S(2)}) collective-permute-start(bf16[512,128]{1,0:T(8,128)(2,1)S(1)} %shard_map.76.refs_5_.refs_2_), channel_id=1, source_target_pairs={{0,4},{1,5},{2,6},{3,7},{4,0},{5,1},{6,2},{7,3},{8,12},{9,13},{10,... | collective-permute-start | bytes 393224 | tf_op jit(solution)/shard_map/ppermute | solution.py:22
  42.5 1.2 %collective-permute-start.14 = (bf16[512,128]{1,0:T(8,128)(2,1)S(1)}, bf16[512,128]{1,0:T(8,128)(2,1)S(1)}, u32[]{:S(2)}, u32[]{:S(2)}) collective-permute-start(bf16[512,128]{1,0:T(8,128)(2,1)S(1)} %shard_map.79.refs_3_.refs_1_), channel_id=1, source_target_pairs={{0,4},{1,5},{2,6},{3,7},{4,0},{5,1},{6,2},{7,3},{8,12},{9,13},{10,... | collective-permute-start | bytes 393224 | tf_op jit(solution)/shard_map/ppermute | solution.py:22
  43.7 1.2 %collective-permute-done.15.refs_2_.refs_3_ = bf16[512,128]{1,0:T(8,128)(2,1)S(1)} collective-permute-done((bf16[512,128]{1,0:T(8,128)(2,1)S(1)}, bf16[512,128]{1,0:T(8,128)(2,1)S(1)}, u32[]{:S(2)}, u32[]{:S(2)}) %collective-permute-start.15) | collective-permute-done | bytes 131104 | tf_op jit(solution)/shard_map/ppermute | solution.py:22
  44.9 5.9 %collective-permute-done.13.refs_4_.refs_0_ = bf16[512,128]{1,0:T(8,128)(2,1)S(1)} collective-permute-done((bf16[512,128]{1,0:T(8,128)(2,1)S(1)}, bf16[512,128]{1,0:T(8,128)(2,1)S(1)}, u32[]{:S(2)}, u32[]{:S(2)}) %collective-permute-start.13) | collective-permute-done | bytes 131104 | tf_op jit(solution)/shard_map/ppermute | solution.py:22
  51.0 1.4 %collective-permute-done.14.refs_5_ = bf16[512,128]{1,0:T(8,128)(2,1)S(1)} collective-permute-done((bf16[512,128]{1,0:T(8,128)(2,1)S(1)}, bf16[512,128]{1,0:T(8,128)(2,1)S(1)}, u32[]{:S(2)}, u32[]{:S(2)}) %collective-permute-start.14) | collective-permute-done | bytes 131104 | tf_op jit(solution)/shard_map/ppermute | solution.py:22
  53.0 1.0 %shard_map.80.refs_2_.refs_5_ = f32[512,256]{1,0:T(8,128)S(1)} custom-call(s32[4]{0:T(128)S(1)} %pad_add_fusion.2.refs_0_, bf16[1024,256]{1,0:T(8,128)(2,1)S(1)} %get-tuple-element.38.refs_1_, bf16[512,128]{1,0:T(8,128)(2,1)S(1)} %shard_map.76.refs_5_.refs_2_, bf16[512,128]{1,0:T(8,128)(2,1)S(1)} %shard_map.79.refs_3_.refs_1_, ...), custom_call_target="tpu_custom_call" | custom-call | flops 1000000000 | bytes 100000000 | tf_op jit(solution)/shard_map/pallas_call | solution.py:292
  54.0 1.0 %shard_map.84.refs_2_ = f32[512,256]{1,0:T(8,128)S(1)} custom-call(s32[4]{0:T(128)S(1)} %pad_add_fusion.2.refs_0_, bf16[1024,256]{1,0:T(8,128)(2,1)S(1)} %collective-permute-done.18.refs_1_, bf16[512,128]{1,0:T(8,128)(2,1)S(1)} %shard_map.76.refs_5_.refs_2_, bf16[512,128]{1,0:T(8,128)(2,1)S(1)} %shard_map.79.refs_3_.refs_1_, ...), custom_call_target="tpu_custom_call" | custom-call | flops 1000000000 | bytes 100000000 | tf_op jit(solution)/shard_map/pallas_call | solution.py:292
  55.0 3.2 %collective-permute-done.16.refs_4_ = bf16[2,512,128]{2,1,0:T(8,128)(2,1)S(1)} collective-permute-done((bf16[2,512,128]{2,1,0:T(8,128)(2,1)S(1)}, bf16[2,512,128]{2,1,0:T(8,128)(2,1)S(1)}, u32[]{:S(2)}, u32[]{:S(2)}) %collective-permute-start.16) | collective-permute-done | bytes 262176 | tf_op jit(solution)/shard_map/ppermute | solution.py:22
  58.2 0.9 %shard_map.82.refs_2_.refs_4_ = f32[512,256]{1,0:T(8,128)S(1)} custom-call(s32[3]{0:T(128)S(1)} %pad_add_fusion.1.refs_0_, bf16[1024,256]{1,0:T(8,128)(2,1)S(1)} %get-tuple-element.38.refs_1_, f32[512,256]{1,0:T(8,128)S(1)} %shard_map.80.refs_2_.refs_5_, bf16[512,128]{1,0:T(8,128)(2,1)S(1)} %collective-permute-done.15.refs_2_.refs_3_, ...), custom_call_target="tpu_custom_call" | custom-call | flops 1000000000 | bytes 100000000 | tf_op jit(solution)/shard_map/pallas_call | solution.py:292
  59.1 0.9 %shard_map.85.refs_2_ = f32[512,256]{1,0:T(8,128)S(1)} custom-call(s32[3]{0:T(128)S(1)} %pad_add_fusion.1.refs_0_, bf16[1024,256]{1,0:T(8,128)(2,1)S(1)} %collective-permute-done.18.refs_1_, f32[512,256]{1,0:T(8,128)S(1)} %shard_map.84.refs_2_, bf16[512,128]{1,0:T(8,128)(2,1)S(1)} %collective-permute-done.15.refs_2_.refs_3_, ...), custom_call_target="tpu_custom_call" | custom-call | flops 1000000000 | bytes 100000000 | tf_op jit(solution)/shard_map/pallas_call | solution.py:292
  60.7 1.3 %collective-permute-done.19.theirs_ref = bf16[528,256]{1,0:T(8,128)(2,1)S(1)} collective-permute-done((bf16[528,256]{1,0:T(8,128)(2,1)S(1)}, bf16[528,256]{1,0:T(8,128)(2,1)S(1)}, u32[]{:S(2)}, u32[]{:S(2)}) %collective-permute-start.19) | collective-permute-done | bytes 270368 | tf_op jit(solution)/shard_map/ppermute | solution.py:22
  62.6 1.7 %collective-permute-start.22 = (bf16[528,128]{1,0:T(8,128)(2,1)S(1)}, bf16[528,128]{1,0:T(8,128)(2,1)S(1)}, u32[]{:S(2)}, u32[]{:S(2)}) collective-permute-start(bf16[528,128]{1,0:T(8,128)(2,1)S(1)} %get-tuple-element.54), channel_id=1, source_target_pairs={{0,16},{8,24},{16,0},{24,8},{1,17},{9,25},{17,1},{25,9},{2,18},{10... | collective-permute-start | bytes 405512 | tf_op jit(solution)/shard_map/ppermute | solution.py:22
  64.3 4.0 %collective-permute-done.22.message_ref = bf16[528,128]{1,0:T(8,128)(2,1)S(1)} collective-permute-done((bf16[528,128]{1,0:T(8,128)(2,1)S(1)}, bf16[528,128]{1,0:T(8,128)(2,1)S(1)}, u32[]{:S(2)}, u32[]{:S(2)}) %collective-permute-start.22) | collective-permute-done | bytes 135200 | tf_op jit(solution)/shard_map/ppermute | solution.py:22
  70.0 0.8 %collective-permute-start.21 = (bf16[528,128]{1,0:T(8,128)(2,1)S(1)}, bf16[528,128]{1,0:T(8,128)(2,1)S(1)}, u32[]{:S(2)}, u32[]{:S(2)}) collective-permute-start(bf16[528,128]{1,0:T(8,128)(2,1)S(1)} %get-tuple-element.53), channel_id=1, source_target_pairs={{0,16},{8,24},{16,0},{24,8},{1,17},{9,25},{17,1},{25,9},{2,18},{10... | collective-permute-start | bytes 405512 | tf_op jit(solution)/shard_map/ppermute | solution.py:22
  70.8 2.9 %collective-permute-done.23.refs_3_ = bf16[528,128]{1,0:T(8,128)(2,1)S(1)} collective-permute-done((bf16[528,128]{1,0:T(8,128)(2,1)S(1)}, bf16[528,128]{1,0:T(8,128)(2,1)S(1)}, u32[]{:S(2)}, u32[]{:S(2)}) %collective-permute-start.23) | collective-permute-done | bytes 135200 | tf_op jit(solution)/shard_map/ppermute | solution.py:22
  73.7 1.3 %collective-permute-done.21.refs_1_ = bf16[528,128]{1,0:T(8,128)(2,1)S(1)} collective-permute-done((bf16[528,128]{1,0:T(8,128)(2,1)S(1)}, bf16[528,128]{1,0:T(8,128)(2,1)S(1)}, u32[]{:S(2)}, u32[]{:S(2)}) %collective-permute-start.21) | collective-permute-done | bytes 135200 | tf_op jit(solution)/shard_map/ppermute | solution.py:22
  75.1 1.1 %shard_map.90 = bf16[1,256,512]{2,1,0:T(8,128)(2,1)} custom-call(f32[512,128]{1,0:T(8,128)S(1)} %get-tuple-element.36.cols_ref.refs_5_.refs_2_, f32[24,256]{1,0:T(8,128)S(1)} %get-tuple-element.37.refs_6_.rows_ref, f32[512,128]{1,0:T(8,128)S(1)} %get-tuple-element.52.refs_0_, bf16[528,128]{1,0:T(8,128)(2,1)S(1)} %collective-permute-done.21.refs_1_, ...), custom_call_target="tpu_custom_call" | custom-call | flops 1000000000 | bytes 100000000 | tf_op jit(solution)/shard_map/pallas_call | solution.py:292
  (58 shorter events, 13.9 us)
Async XLA Ops:
  3.5 2.5 %copy-start.2 = (bf16[512,640]{1,0:T(8,128)(2,1)}, bf16[512,640]{1,0:T(8,128)(2,1)S(1)}, u32[]{:S(2)}) copy-start(bf16[512,640]{1,0:T(8,128)(2,1)S(1)} %get-tuple-element.32.refs_0_.turned_ref) | copy-start | bytes 1966084
  3.6 2.1 %collective-permute-start.1 = (bf16[2,528,256]{2,1,0:T(8,128)(2,1)S(1)}, bf16[2,528,256]{2,1,0:T(8,128)(2,1)S(1)}, u32[]{:S(2)}, u32[]{:S(2)}) collective-permute-start(bf16[2,528,256]{2,1,0:T(8,128)(2,1)S(1)} %get-tuple-element.34.refs_2_), channel_id=1, source_target_pairs={{0,1},{1,0},{2,3},{3,2},{4,5},{5,4},{6,7},{7,6},{8,9},{9,8},{10,11... | collective-permute-start | bytes 1622024 | tf_op jit(solution)/shard_map/ppermute | solution.py:22
  5.1 7.6 %collective-permute-start.2 = (bf16[2,528,256]{2,1,0:T(8,128)(2,1)S(1)}, bf16[2,528,256]{2,1,0:T(8,128)(2,1)S(1)}, u32[]{:S(2)}, u32[]{:S(2)}) collective-permute-start(bf16[2,528,256]{2,1,0:T(8,128)(2,1)S(1)} %shard_map.65), channel_id=1, source_target_pairs={{0,1},{1,0},{2,3},{3,2},{4,5},{5,4},{6,7},{7,6},{8,9},{9,8},{10,11... | collective-permute-start | bytes 1622024 | tf_op jit(solution)/shard_map/ppermute | solution.py:22
  6.1 6.9 %collective-permute-start.4 = (bf16[1,528,128]{2,1,0:T(8,128)(2,1)S(1)}, bf16[1,528,128]{2,1,0:T(8,128)(2,1)S(1)}, u32[]{:S(2)}, u32[]{:S(2)}) collective-permute-start(bf16[1,528,128]{2,1,0:T(8,128)(2,1)S(1)} %shard_map.66.refs_3_), channel_id=1, source_target_pairs={{0,2},{1,3},{2,0},{3,1},{4,6},{5,7},{6,4},{7,5},{8,10},{9,11},{10,... | collective-permute-start | bytes 405512 | tf_op jit(solution)/shard_map/ppermute | solution.py:22
  9.1 13.3 %collective-permute-start = (f32[1,768]{1,0:T(1,128)S(1)}, f32[1,768]{1,0:T(1,128)S(1)}, u32[]{:S(2)}, u32[]{:S(2)}) collective-permute-start(f32[1,768]{1,0:T(1,128)S(1)} %get-tuple-element.31.refs_1_.refs_3_), channel_id=1, source_target_pairs={{0,8},{8,0},{16,24},{24,16},{1,9},{9,1},{17,25},{25,17},{2,10},{10... | collective-permute-start | bytes 9224 | tf_op jit(solution)/shard_map/ppermute | solution.py:22
  10.6 1.1 %copy-start.3 = (bf16[512,640]{1,0:T(8,128)(2,1)S(1)}, bf16[512,640]{1,0:T(8,128)(2,1)}, u32[]{:S(2)}) copy-start(bf16[512,640]{1,0:T(8,128)(2,1)} %copy-done.2) | copy-start | bytes 1966084
  12.1 7.3 %collective-permute-start.3 = (bf16[1,528,128]{2,1,0:T(8,128)(2,1)S(1)}, bf16[1,528,128]{2,1,0:T(8,128)(2,1)S(1)}, u32[]{:S(2)}, u32[]{:S(2)}) collective-permute-start(bf16[1,528,128]{2,1,0:T(8,128)(2,1)S(1)} %shard_map.67.refs_4_), channel_id=1, source_target_pairs={{0,2},{1,3},{2,0},{3,1},{4,6},{5,7},{6,4},{7,5},{8,10},{9,11},{10,... | collective-permute-start | bytes 405512 | tf_op jit(solution)/shard_map/ppermute | solution.py:22
  13.5 12.7 %collective-permute-start.5 = (bf16[1,528,128]{2,1,0:T(8,128)(2,1)S(1)}, bf16[1,528,128]{2,1,0:T(8,128)(2,1)S(1)}, u32[]{:S(2)}, u32[]{:S(2)}) collective-permute-start(bf16[1,528,128]{2,1,0:T(8,128)(2,1)S(1)} %shard_map.68.refs_3_), channel_id=1, source_target_pairs={{0,4},{1,5},{2,6},{3,7},{4,0},{5,1},{6,2},{7,3},{8,12},{9,13},{10,... | collective-permute-start | bytes 405512 | tf_op jit(solution)/shard_map/ppermute | solution.py:22
  16.8 9.4 %collective-permute-start.6 = (bf16[1,528,128]{2,1,0:T(8,128)(2,1)S(1)}, bf16[1,528,128]{2,1,0:T(8,128)(2,1)S(1)}, u32[]{:S(2)}, u32[]{:S(2)}) collective-permute-start(bf16[1,528,128]{2,1,0:T(8,128)(2,1)S(1)} %shard_map.69.refs_4_), channel_id=1, source_target_pairs={{0,2},{1,3},{2,0},{3,1},{4,6},{5,7},{6,4},{7,5},{8,10},{9,11},{10,... | collective-permute-start | bytes 405512 | tf_op jit(solution)/shard_map/ppermute | solution.py:22
  19.9 9.0 %collective-permute-start.9 = (bf16[1,528,128]{2,1,0:T(8,128)(2,1)S(1)}, bf16[1,528,128]{2,1,0:T(8,128)(2,1)S(1)}, u32[]{:S(2)}, u32[]{:S(2)}) collective-permute-start(bf16[1,528,128]{2,1,0:T(8,128)(2,1)S(1)} %shard_map.70.refs_3_), channel_id=1, source_target_pairs={{0,4},{1,5},{2,6},{3,7},{4,0},{5,1},{6,2},{7,3},{8,12},{9,13},{10,... | collective-permute-start | bytes 405512 | tf_op jit(solution)/shard_map/ppermute | solution.py:22
  22.3 3.9 %copy-start.4 = (bf16[512,640]{1,0:T(8,128)(2,1)S(1)}, bf16[512,640]{1,0:T(8,128)(2,1)}, u32[]{:S(2)}) copy-start(bf16[512,640]{1,0:T(8,128)(2,1)} %copy-done.2) | copy-start | bytes 1966084
  22.3 6.5 %collective-permute-start.10 = (bf16[1,528,128]{2,1,0:T(8,128)(2,1)S(1)}, bf16[1,528,128]{2,1,0:T(8,128)(2,1)S(1)}, u32[]{:S(2)}, u32[]{:S(2)}) collective-permute-start(bf16[1,528,128]{2,1,0:T(8,128)(2,1)S(1)} %shard_map.71.refs_5_.refs_3_), channel_id=1, source_target_pairs={{0,2},{1,3},{2,0},{3,1},{4,6},{5,7},{6,4},{7,5},{8,10},{9,11},{10,... | collective-permute-start | bytes 405512 | tf_op jit(solution)/shard_map/ppermute | solution.py:22
  26.8 5.1 %collective-permute-start.7 = (bf16[528,128]{1,0:T(8,128)(2,1)S(1)}, bf16[528,128]{1,0:T(8,128)(2,1)S(1)}, u32[]{:S(2)}, u32[]{:S(2)}) collective-permute-start(bf16[528,128]{1,0:T(8,128)(2,1)S(1)} %get-tuple-element.40.refs_7_), channel_id=1, source_target_pairs={{0,8},{8,0},{16,24},{24,16},{1,9},{9,1},{17,25},{25,17},{2,10},{10... | collective-permute-start | bytes 405512 | tf_op jit(solution)/shard_map/ppermute | solution.py:22
  29.5 4.3 %copy-start = (bf16[1,256,2048]{2,1,0:T(8,128)(2,1)S(1)}, bf16[1,256,2048]{2,1,0:T(8,128)(2,1)}, u32[]{:S(2)}) copy-start(bf16[1,256,2048]{2,1,0:T(8,128)(2,1)} %refs_1_.1) | copy-start | bytes 3145732
  29.5 4.2 %copy-start.1 = (bf16[1,512,512]{2,1,0:T(8,128)(2,1)S(1)}, bf16[1,512,512]{2,1,0:T(8,128)(2,1)}, u32[]{:S(2)}) copy-start(bf16[1,512,512]{2,1,0:T(8,128)(2,1)} %refs_2_.1) | copy-start | bytes 1572868
  29.5 6.3 %collective-permute-start.11 = (bf16[528,128]{1,0:T(8,128)(2,1)S(1)}, bf16[528,128]{1,0:T(8,128)(2,1)S(1)}, u32[]{:S(2)}, u32[]{:S(2)}) collective-permute-start(bf16[528,128]{1,0:T(8,128)(2,1)S(1)} %get-tuple-element.45), channel_id=1, source_target_pairs={{0,16},{8,24},{16,0},{24,8},{1,17},{9,25},{17,1},{25,9},{2,18},{10... | collective-permute-start | bytes 405512 | tf_op jit(solution)/shard_map/ppermute | solution.py:22
  32.2 5.1 %collective-permute-start.8 = (bf16[528,128]{1,0:T(8,128)(2,1)S(1)}, bf16[528,128]{1,0:T(8,128)(2,1)S(1)}, u32[]{:S(2)}, u32[]{:S(2)}) collective-permute-start(bf16[528,128]{1,0:T(8,128)(2,1)S(1)} %get-tuple-element.43), channel_id=1, source_target_pairs={{0,16},{8,24},{16,0},{24,8},{1,17},{9,25},{17,1},{25,9},{2,18},{10... | collective-permute-start | bytes 405512 | tf_op jit(solution)/shard_map/ppermute | solution.py:22
  34.2 19.8 %collective-permute-start.18 = (bf16[1024,256]{1,0:T(8,128)(2,1)S(1)}, bf16[1024,256]{1,0:T(8,128)(2,1)S(1)}, u32[]{:S(2)}, u32[]{:S(2)}) collective-permute-start(bf16[1024,256]{1,0:T(8,128)(2,1)S(1)} %get-tuple-element.48), channel_id=1, source_target_pairs={{0,1},{1,0},{2,3},{3,2},{4,5},{5,4},{6,7},{7,6},{8,9},{9,8},{10,11... | collective-permute-start | bytes 1572872 | tf_op jit(solution)/shard_map/ppermute | solution.py:22
  36.3 5.8 %collective-permute-start.12 = (bf16[528,128]{1,0:T(8,128)(2,1)S(1)}, bf16[528,128]{1,0:T(8,128)(2,1)S(1)}, u32[]{:S(2)}, u32[]{:S(2)}) collective-permute-start(bf16[528,128]{1,0:T(8,128)(2,1)S(1)} %get-tuple-element.47), channel_id=1, source_target_pairs={{0,8},{8,0},{16,24},{24,16},{1,9},{9,1},{17,25},{25,17},{2,10},{10... | collective-permute-start | bytes 405512 | tf_op jit(solution)/shard_map/ppermute | solution.py:22
  37.8 7.2 %collective-permute-start.15 = (bf16[512,128]{1,0:T(8,128)(2,1)S(1)}, bf16[512,128]{1,0:T(8,128)(2,1)S(1)}, u32[]{:S(2)}, u32[]{:S(2)}) collective-permute-start(bf16[512,128]{1,0:T(8,128)(2,1)S(1)} %shard_map.76.refs_5_.refs_2_), channel_id=1, source_target_pairs={{0,2},{1,3},{2,0},{3,1},{4,6},{5,7},{6,4},{7,5},{8,10},{9,11},{10,... | collective-permute-start | bytes 393224 | tf_op jit(solution)/shard_map/ppermute | solution.py:22
  39.0 11.8 %collective-permute-start.13 = (bf16[512,128]{1,0:T(8,128)(2,1)S(1)}, bf16[512,128]{1,0:T(8,128)(2,1)S(1)}, u32[]{:S(2)}, u32[]{:S(2)}) collective-permute-start(bf16[512,128]{1,0:T(8,128)(2,1)S(1)} %shard_map.76.refs_5_.refs_2_), channel_id=1, source_target_pairs={{0,4},{1,5},{2,6},{3,7},{4,0},{5,1},{6,2},{7,3},{8,12},{9,13},{10,... | collective-permute-start | bytes 393224 | tf_op jit(solution)/shard_map/ppermute | solution.py:22
  42.5 10.0 %collective-permute-start.14 = (bf16[512,128]{1,0:T(8,128)(2,1)S(1)}, bf16[512,128]{1,0:T(8,128)(2,1)S(1)}, u32[]{:S(2)}, u32[]{:S(2)}) collective-permute-start(bf16[512,128]{1,0:T(8,128)(2,1)S(1)} %shard_map.79.refs_3_.refs_1_), channel_id=1, source_target_pairs={{0,4},{1,5},{2,6},{3,7},{4,0},{5,1},{6,2},{7,3},{8,12},{9,13},{10,... | collective-permute-start | bytes 393224 | tf_op jit(solution)/shard_map/ppermute | solution.py:22
  50.8 7.3 %collective-permute-start.16 = (bf16[2,512,128]{2,1,0:T(8,128)(2,1)S(1)}, bf16[2,512,128]{2,1,0:T(8,128)(2,1)S(1)}, u32[]{:S(2)}, u32[]{:S(2)}) collective-permute-start(bf16[2,512,128]{2,1,0:T(8,128)(2,1)S(1)} %shard_map.81), channel_id=1, source_target_pairs={{0,2},{1,3},{2,0},{3,1},{4,6},{5,7},{6,4},{7,5},{8,10},{9,11},{10,... | collective-permute-start | bytes 786440 | tf_op jit(solution)/shard_map/ppermute | solution.py:22
  52.4 7.5 %collective-permute-start.17 = (bf16[512,128]{1,0:T(8,128)(2,1)S(1)}, bf16[512,128]{1,0:T(8,128)(2,1)S(1)}, u32[]{:S(2)}, u32[]{:S(2)}) collective-permute-start(bf16[512,128]{1,0:T(8,128)(2,1)S(1)} %collective-permute-done.14.refs_5_), channel_id=1, source_target_pairs={{0,2},{1,3},{2,0},{3,1},{4,6},{5,7},{6,4},{7,5},{8,10},{9,11},{10,... | collective-permute-start | bytes 393224 | tf_op jit(solution)/shard_map/ppermute | solution.py:22
  60.4 1.6 %collective-permute-start.19 = (bf16[528,256]{1,0:T(8,128)(2,1)S(1)}, bf16[528,256]{1,0:T(8,128)(2,1)S(1)}, u32[]{:S(2)}, u32[]{:S(2)}) collective-permute-start(bf16[528,256]{1,0:T(8,128)(2,1)S(1)} %shard_map.86), channel_id=1, source_target_pairs={{0,1},{1,0},{2,3},{3,2},{4,5},{5,4},{6,7},{7,6},{8,9},{9,8},{10,11... | collective-permute-start | bytes 811016 | tf_op jit(solution)/shard_map/ppermute | solution.py:22
  62.6 5.7 %collective-permute-start.22 = (bf16[528,128]{1,0:T(8,128)(2,1)S(1)}, bf16[528,128]{1,0:T(8,128)(2,1)S(1)}, u32[]{:S(2)}, u32[]{:S(2)}) collective-permute-start(bf16[528,128]{1,0:T(8,128)(2,1)S(1)} %get-tuple-element.54), channel_id=1, source_target_pairs={{0,16},{8,24},{16,0},{24,8},{1,17},{9,25},{17,1},{25,9},{2,18},{10... | collective-permute-start | bytes 405512 | tf_op jit(solution)/shard_map/ppermute | solution.py:22
  64.2 5.3 %collective-permute-start.20 = (bf16[528,128]{1,0:T(8,128)(2,1)S(1)}, bf16[528,128]{1,0:T(8,128)(2,1)S(1)}, u32[]{:S(2)}, u32[]{:S(2)}) collective-permute-start(bf16[528,128]{1,0:T(8,128)(2,1)S(1)} %get-tuple-element.51), channel_id=1, source_target_pairs={{0,8},{8,0},{16,24},{24,16},{1,9},{9,1},{17,25},{25,17},{2,10},{10... | collective-permute-start | bytes 405512 | tf_op jit(solution)/shard_map/ppermute | solution.py:22
  68.6 5.1 %collective-permute-start.23 = (bf16[528,128]{1,0:T(8,128)(2,1)S(1)}, bf16[528,128]{1,0:T(8,128)(2,1)S(1)}, u32[]{:S(2)}, u32[]{:S(2)}) collective-permute-start(bf16[528,128]{1,0:T(8,128)(2,1)S(1)} %get-tuple-element.56), channel_id=1, source_target_pairs={{0,8},{8,0},{16,24},{24,16},{1,9},{9,1},{17,25},{25,17},{2,10},{10... | collective-permute-start | bytes 405512 | tf_op jit(solution)/shard_map/ppermute | solution.py:22
  70.0 5.1 %collective-permute-start.21 = (bf16[528,128]{1,0:T(8,128)(2,1)S(1)}, bf16[528,128]{1,0:T(8,128)(2,1)S(1)}, u32[]{:S(2)}, u32[]{:S(2)}) collective-permute-start(bf16[528,128]{1,0:T(8,128)(2,1)S(1)} %get-tuple-element.53), channel_id=1, source_target_pairs={{0,16},{8,24},{16,0},{24,8},{1,17},{9,25},{17,1},{25,9},{2,18},{10... | collective-permute-start | bytes 405512 | tf_op jit(solution)/shard_map/ppermute | solution.py:22

commit v5 on v4

--- a/solution.py
+++ b/solution.py
@@ -12,7 +12,6 @@
 TINY = 1e-30
 F32, BF16 = jnp.float32, jnp.bfloat16
 VMEM = pl.BlockSpec(memory_space=pltpu.VMEM)
-SMEM = pl.BlockSpec(memory_space=pltpu.SMEM)
 HBM = pl.BlockSpec(memory_space=pltpu.HBM)
 FIRST_GRANT = 8
 SPLIT = 2
@@ -42,11 +41,16 @@
     return jnp.where(y < 0, -size, size) * top
 
 
+def core_and_chip():
+    place = lax.axis_index("dp")
+    return lax.rem(place, 2), lax.div(place, 2)
+
+
 def first_kernel(
-    here_ref, grads_hbm, inputs_hbm, out_decay, in_decay, sent_ref, turned_ref, rest_ref, own_ref, rates_ref, *scratch
+    grads_hbm, inputs_hbm, out_decay, in_decay, sent_ref, turned_ref, rest_ref, own_ref, rates_ref, *scratch
 ):
     grads_ref, inputs_ref, sems = scratch
-    core, chip = here_ref[0], here_ref[1]
+    core, chip = core_and_chip()
     width = out_decay.shape[1]
     chips, _, rows = own_ref.shape
     sem = iter(range(sems.shape[0]))
@@ -75,15 +79,19 @@
         arrival.wait()
 
 
-def rest_kernel(turned_ref, inputs_ref, sent_ref):
+def rest_kernel(turned_ref, inputs_ref, sent_ref, turned_out):
+    turned_out[...] = turned_ref[...]
     for i in range(inputs_ref.shape[0]):
         put(sent_ref.at[i], jnp.dot(turned_ref[...], inputs_ref[i], preferred_element_type=F32))
 
 
-def sum_kernel(part, offsets, picks, n, weighs, turned_ref, own_ref, theirs_ref, *refs):
-    messages, outs = refs[:n], refs[n + (2 if weighs else 0) :]
+def sum_kernel(part, offsets, picks, n, weighs, passes, turned_ref, own_ref, theirs_ref, *refs):
+    messages, outs = refs[:n], refs[n + (2 if weighs else 0) + passes :]
     lanes = outs[0].shape[-1]
     columns = pl.ds(part * lanes, lanes)
+    if passes:
+        outs[1][...] = refs[n][...]
+        outs = outs[:1]
     for i, o in enumerate(offsets):
         total = jnp.dot(turned_ref[...], own_ref[o, :, columns], preferred_element_type=F32)
         total = total + get(theirs_ref.at[o // 2, :, columns])
@@ -97,8 +105,8 @@
         put(outs[0].at[i] if len(outs[0].shape) == 3 else outs[0], total)
 
 
-def turn_kernel(core_ref, a_ref, s_ref, own_ref, send_ref, s_out):
-    core = core_ref[0]
+def turn_kernel(a_ref, s_ref, own_ref, send_ref, s_out):
+    core, _ = core_and_chip()
     rows = a_ref.shape[1]
     for i in range(own_ref.shape[0] // rows):
         for of, out in ((core, own_ref), (1 - core, send_ref)):
@@ -117,9 +125,10 @@
     return value
 
 
-def step_kernel(into_value, into_total, more, *refs):
+def step_kernel(into_value, into_total, more, columns, *refs):
     n = len(into_value)
     value_ref, total_ref, cols_ref, rows_ref = refs[:4]
+    rows_ref = rows_ref.at[:, columns]
     messages, outs = refs[4 : 4 + n], refs[4 + n :]
     outs[0][...] = weighed(into_value, cols_ref, rows_ref, messages, value_ref[...])
     total = weight(cols_ref, rows_ref, into_total[0]) * total_ref[...]
@@ -129,17 +138,16 @@
         outs[2][...] = total
 
 
-def cross_kernel(places, part, value_ref, total_ref, cols_ref, rows_ref, message_ref, value_out, sent_ref):
+def cross_kernel(places, columns, of, value_ref, total_ref, cols_ref, rows_ref, message_ref, value_out, sent_ref):
     into_value, mix_own, mix_got = places
-    lanes = sent_ref.shape[1]
-    columns = slice(part * lanes, (part + 1) * lanes)
     at = rows_ref.at[:, columns]
     got = get(message_ref)
-    value_out[...] = value_ref[:, columns] + weight(cols_ref, at, into_value) * got
-    put(sent_ref, weight(cols_ref, at, mix_own) * total_ref[:, columns] + weight(cols_ref, at, mix_got) * got)
-
-
-def side_s_kernel(places, value_ref, s_ref, cols_ref, rows_ref, *refs):
+    value_out[...] = value_ref[:, of] + weight(cols_ref, at, into_value) * got
+    put(sent_ref, weight(cols_ref, at, mix_own) * total_ref[:, of] + weight(cols_ref, at, mix_got) * got)
+
+
+def side_s_kernel(places, columns, value_ref, s_ref, cols_ref, rows_ref, *refs):
+    rows_ref = rows_ref.at[:, columns]
     upper = weighed(places, cols_ref, rows_ref, refs[: len(places)], value_ref[...])
     refs[-1][...] = jnp.dot(s_ref[...], upper.astype(BF16), preferred_element_type=F32).astype(BF16)
 
@@ -151,14 +159,17 @@
 
 def side_a_kernel(picks, has_before, *refs):
     refs = list(refs)
-    at_ref, a_ref = refs.pop(0), refs.pop(0)
+    a_ref, (_, chip) = refs.pop(0), core_and_chip()
     solved = refs.pop(0)[...] if has_before else None
-    for array, block, place in picks:
-        operand = refs[array][...] if block is None else refs[array][block]
-        lanes = operand.shape[1]
-        features = pl.ds(pl.multiple_of(at_ref[place], lanes), lanes)
-        term = jnp.dot(operand, a_ref[features, :], preferred_element_type=F32)
-        solved = term if solved is None else solved + term
+    rows = a_ref.shape[1]
+    operands, features = [], []
+    for array, block, part, o in picks:
+        operands.append(refs[array][...] if block is None else refs[array][block])
+        lanes = operands[-1].shape[1]
+        start = (chip ^ o) * rows + part * lanes
+        features.append(a_ref[pl.ds(pl.multiple_of(start, lanes), lanes), :])
+    term = jnp.dot(jnp.concatenate(operands, axis=1), jnp.concatenate(features, axis=0), preferred_element_type=F32)
+    solved = term if solved is None else solved + term
     if refs[-1].dtype == F32:
         refs[-1][...] = solved
     else:
@@ -197,12 +208,13 @@
     return out
 
 
-def weights_kernel(size, last, n, me_ref, *refs):
-    groups, (below_ref, above_ref) = refs[:n], refs[n : n + 2]
-    cols_ref, rows_ref, *state_ref = refs[n + 2 :]
+def weights_kernel(step, size, last, n, *refs):
+    groups, state = refs[:n], refs[n : n + (2 if step > 1 else 0)]
+    cols_ref, rows_ref, *state_ref = refs[n + len(state) :]
     group = [ref[i : i + 1, :] for ref in groups for i in range(ref.shape[0])]
-    below, above = below_ref[...], above_ref[...]
-    ones, zeros = jnp.ones_like(below), jnp.zeros_like(below)
+    ones, zeros = jnp.ones_like(group[0]), jnp.zeros_like(group[0])
+    below, above = [ref[...] for ref in state] or [group[0], ones]
+    mine = lax.rem(lax.div(lax.axis_index("layer"), step), size)
 
     def product(holds):
         out = ones
@@ -217,7 +229,7 @@
         return out
 
     stack = [group[0]]
-    for me, factor in ((me_ref[0], below), (size - 1 - me_ref[0], above)):
+    for me, factor in ((mine, below), (size - 1 - mine, above)):
         if not last:
             for flip in range(1, size):
                 peer = me ^ flip
@@ -245,7 +257,7 @@
     cols_ref[...] = table[:, :width].T
     rows_ref[...] = table[: rows_ref.shape[0], width:]
     if not last:
-        me = me_ref[0]
+        me = mine
         before = product(lambda q: q < me)
         state_ref[0][...] = jnp.concatenate([product(lambda q: q >= 0), below * before, above * before], axis=0)
 
@@ -266,8 +278,6 @@
 
 def shards(activations, out_grads, a_inverse, s_inverse, in_decay, out_decay):
     layers, peers = lax.axis_size("layer"), lax.axis_size("dp")
-    layer, here = lax.axis_index("layer"), lax.axis_index("dp")
-    core, chip = here % 2, here // 2
     chips = peers // 2
     rows = a_inverse.shape[1]
     width = out_grads.shape[2]
@@ -281,7 +291,7 @@
     def message(n):
         return shape(width + TAIL, n, dtype=BF16)
 
-    def call(kernel, out_shape, *operands, scalars=0, grant=4 * 2**20, hbm=0, scratch=(), after=()):
+    def call(kernel, out_shape, *operands, grant=4 * 2**20, hbm=0, scratch=(), after=()):
         several = isinstance(out_shape, (list, tuple))
         if after:
             inner, count = kernel, len(operands)
@@ -292,18 +302,14 @@
         return pl.pallas_call(
             kernel,
             out_shape=out_shape,
-            in_specs=[SMEM] * scalars
-            + [HBM] * hbm
-            + [VMEM] * (len(operands) - scalars - hbm)
+            in_specs=[HBM] * hbm
+            + [VMEM] * (len(operands) - hbm)
             + [pl.BlockSpec(memory_space=pl.ANY)] * len(after),
             out_specs=[VMEM] * len(out_shape) if several else VMEM,
             scratch_shapes=scratch,
             compiler_params=pltpu.CompilerParams(vmem_limit_bytes=grant),
             cost_estimate=pl.CostEstimate(flops=10**9, bytes_accessed=10**8, transcendentals=0),
         )(*operands, *after)
-
-    def scalar(x):
-        return x.reshape(1).astype(jnp.int32)
 
     odd, even = list(range(1, chips, 2)), list(range(0, chips, 2))
     sent, turned, rest, inputs, rates = call(
@@ -315,9 +321,7 @@
             shape(chips, tokens, rows, dtype=BF16),
             shape(1, width + rows),
         ],
-        jnp.stack([core, chip]).astype(jnp.int32),
         *(pltpu.with_memory_space_constraint(x, pltpu.HBM) for x in (out_grads, activations, out_decay, in_decay)),
-        scalars=1,
         hbm=4,
         grant=FIRST_GRANT * 2**20,
         scratch=[
@@ -327,26 +331,27 @@
         ],
     )
     theirs = {1: exchange(sent, "dp", 1)}
-    sent = call(rest_kernel, shape(len(even), width + TAIL, rows, dtype=BF16), turned, rest, after=(sent,))
+    outs = [shape(len(even), width + TAIL, rows, dtype=BF16), shape(width, tokens, dtype=BF16)]
+    sent, turned = call(rest_kernel, outs, turned, rest, after=(sent,))
     theirs[0] = exchange(sent, "dp", 1)
-    group = [rates, exchange(rates, "layer", 1)]
 
     levels = [1 << b for b in range(chips.bit_length() - 1)]
     received = [{} for _ in range(split)]
     latest = []
 
-    def blocks(part, offsets, outs, weighs=None, weights=()):
+    def blocks(part, offsets, outs, weighs=None, weights=(), passed=()):
         heard = [[(got, j) for got, j in received[part].get(o, [])] for o in offsets]
         arrays = list({id(got): got for some in heard for got, _ in some}.values())
         picks = [[([id(x) for x in arrays].index(id(got)), j) for got, j in some] for some in heard]
         outs = call(
-            functools.partial(sum_kernel, part, offsets, picks, len(arrays), weighs),
+            functools.partial(sum_kernel, part, offsets, picks, len(arrays), weighs, len(passed)),
             outs,
             turned,
             inputs,
             theirs[offsets[0] % 2],
             *arrays,
             *(weights if weighs else ()),
+            *passed,
             after=latest[-1:],
         )
         latest.append(outs[0])
@@ -359,13 +364,16 @@
         for part in range(split):
             for at, some in [(level, soon)] + held:
                 outs = [shape(len(some), width + TAIL, lanes, dtype=BF16)]
-                [sent] = blocks(part, some, outs)
+                final = len(latest) + 1 == split * (2 * len(levels) - 1)
+                sent, *passed = blocks(part, some, outs + [shape(1, width + rows)] * final, passed=[rates] * final)
+                rates = passed[0] if final else rates
                 got = exchange(sent, "dp", 2 * at)
                 received[part].update({o ^ at: received[part].get(o ^ at, []) + [(got, j)] for j, o in enumerate(some)})
         held = [(level, held_next)] if held_next else []
 
+    group = [rates, exchange(rates, "layer", 1)]
     ups, downs = [], []
-    below, above = rates, jnp.ones_like(rates)
+    state = []
     for step, size in digits(layers):
         last = step * size == layers
         if step > 1:
@@ -373,27 +381,22 @@
         if size == 4 and not last:
             group = [jnp.concatenate(group, axis=0)]
             group.append(exchange(group[0], "layer", 2 * step))
-        cols, in_rows, *state = call(
-            functools.partial(weights_kernel, size, last, len(group)),
+        cols, in_rows, *new = call(
+            functools.partial(weights_kernel, step, size, last, len(group)),
             [shape(width, 128), shape(24, rows)] + [shape(3, width + rows)] * (not last),
-            scalar(layer // step % size),
             *group,
-            below,
-            above,
-            scalars=1,
+            *state,
             after=latest[-1:],
         )
         if not last:
-            own, below, above = state[0][:1], state[0][1:2], state[0][2:]
+            own, state = new[0][:1], [new[0][1:2], new[0][2:]]
         for solve, places in zip((ups, downs), weight_places(size, last)):
             solve.append((step, size, cols, in_rows, *places))
     a_own, a_theirs, s_turned = call(
         turn_kernel,
         [shape(chips * rows, rows, dtype=BF16)] * 2 + [shape(width, width, dtype=BF16)],
-        scalar(core),
         a_inverse,
         s_inverse,
-        scalars=1,
         after=latest[-1:],
     )
     a_theirs = exchange(a_theirs, "dp", 1)
@@ -403,9 +406,10 @@
         for i, (step, size, cols, in_rows, into_value, into_total) in enumerate(solve[:-1]):
             more = i + 1 < len(solve)
             outs = [shape(width, n), message(n)] + [shape(width, n)] * more
-            kernel = functools.partial(step_kernel, into_value, into_total, more)
+            kernel = functools.partial(step_kernel, into_value, into_total, more, pl.ds(part * n, n))
             others = [exchange(sent, "layer", flip * step) for flip in range(1, size)]
-            value, sent, total = call(kernel, outs, value, total, cols, in_rows[:, part * n : (part + 1) * n], *others)
+            value, sent, *total = call(kernel, outs, value, total, cols, in_rows, *others)
+            total = total[0] if more else value
         return value, total, sent
 
     def order_of(solve, part):
@@ -422,23 +426,22 @@
         got = exchange(sent, "layer", flips[0])
         if len(flips) == 1:
             return value, got
-        whole = value.shape[1] > n
-        at = in_rows if whole or n == rows else in_rows[:, part * n : (part + 1) * n]
-        kernel = functools.partial(cross_kernel, places, part if whole else 0)
-        value, sent = call(kernel, [shape(width, n), message(n)], value, total, cols, at, got)
+        columns = slice(part * n, (part + 1) * n)
+        of = columns if value.shape[1] > n else slice(0, n)
+        kernel = functools.partial(cross_kernel, places, columns, of)
+        value, sent = call(kernel, [shape(width, n), message(n)], value, total, cols, in_rows, got)
         return value, exchange(sent, "layer", flips[1])
 
     _, _, cols, in_rows, *_ = ups[-1]
     applied = []
     for part in range(split):
-        at = in_rows[:, part * lanes : (part + 1) * lanes]
         first = order_of(ups, part)[1] if len(ups) == 1 else None
         sent, value = blocks(part, [0], [message(lanes), shape(width, lanes)], first, (cols, in_rows))
         value, total, sent = steps(ups, value, value, sent, part)
         value, got = cross(ups, part, value, total, sent)
-        kernel = functools.partial(side_s_kernel, [order_of(ups, part)[3]])
+        kernel = functools.partial(side_s_kernel, [order_of(ups, part)[3]], slice(part * lanes, (part + 1) * lanes))
         applied.append(
-            call(kernel, shape(width, lanes, dtype=BF16), value, s_turned, cols, at, got, after=applied[-1:])
+            call(kernel, shape(width, lanes, dtype=BF16), value, s_turned, cols, in_rows, got, after=applied[-1:])
         )
 
     def stack(items, after=()):
@@ -449,12 +452,12 @@
 
     def send(level, batch, after=()):
         items = [have[part][o] for part, o in batch]
-        if len(items) == 1 and items[0][1] is None:
+        if len(items) == 1 and not after:
             got = exchange(items[0][0], "dp", 2 * level)
         else:
             got = exchange(stack([x if i is None else x[i] for x, i in items], after), "dp", 2 * level)
         came = [(part, o ^ level) for part, o in batch]
-        have_of = [(got, i if len(batch) > 1 or items[0][1] is not None else None) for i in range(len(batch))]
+        have_of = [(got, i if len(batch) > 1 or after else None) for i in range(len(batch))]
         for (part, o), where in zip(came, have_of):
             have[part][o] = where
         return came, got
@@ -463,31 +466,27 @@
         for level in reversed(levels[1:]):
             arrivals[0] += send(level, [(part, o) for o in list(have[part])])[0]
     if chips > 1:
-        came, got = send(1, [(0, 0)])
-        arrivals.append(came)
-        for part in range(split):
-            batch = [(part, o) for o in list(have[part]) if o > 1 and o % 2 == 0]
-            batch += [(part + 1, 0)] if part + 1 < split else []
-            if batch:
-                came, _ = send(1, batch, [got])
-                if part + 1 < split:
-                    arrivals[-1] += came
-                else:
-                    arrivals.append(came)
+        plan = [[(part, 0)] for part in range(split)]
+        plan += [[(part, o) for o in have[part] if o > 1] for part in range(split)]
+        plan = [batch for batch in plan if batch]
+        gots = []
+        for i, batch in enumerate(plan):
+            came, got = send(1, batch, gots[:1] if i == split else [])
+            gots.append(got)
+            if i + 1 < len(plan) and i:
+                arrivals[-1] += came
+            else:
+                arrivals.append(came)
 
     own, others, done = None, None, []
     for chosen in arrivals:
         arrays = list({id(have[part][o][0]): have[part][o][0] for part, o in chosen}.values())
-        places = jnp.stack([(chip ^ o) * rows + part * lanes for part, o in chosen]).astype(jnp.int32)
-        picks = [
-            ([id(x) for x in arrays].index(id(have[part][o][0])), have[part][o][1], i)
-            for i, (part, o) in enumerate(chosen)
-        ]
+        picks = [([id(x) for x in arrays].index(id(have[part][o][0])), have[part][o][1], part, o) for part, o in chosen]
 
         def product(a, before, out_shape, after=()):
             before = [] if before is None else [before]
             kernel = functools.partial(side_a_kernel, picks, bool(before))
-            return call(kernel, out_shape, places, a, *before, *arrays, scalars=1, after=after)
+            return call(kernel, out_shape, a, *before, *arrays, after=after)
 
         final = chosen is arrivals[-1]
         others = product(a_theirs, others, message(rows) if final else shape(width, rows), done)

time: 76.3 us -> 72.7 us (0.953)
  starting transfers between devices: 27.2 us -> 30.6 us
  Pallas kernels: 17.3 us -> 14.2 us
  waiting for transfers between devices: 30 us -> 27.4 us
  local copies, waits for them, and re-layouts: 1.11 us -> 0.01 us
    ppermute x24 -> x25, starting transfers between devices: 27.2 us -> 30.6 us  [exchange(): lax.ppermute(x, axis, [(i, i ^ flip) for i in range(lax.axis_size(axis))])]
    pallas_call x27, Pallas kernels: 17.3 us -> 14.2 us  [call(): pl.pallas_call(kernel, out_shape=out_shape, in_specs=[HBM] * hbm + [VMEM]...]
    ppermute x24 -> x25, waiting for transfers between devices: 30 us -> 27.4 us  [exchange(): lax.ppermute(x, axis, [(i, i ^ flip) for i in range(lax.axis_size(axis))])]
    unnamed x10 -> x4, local copies, waits for them, and re-layouts: 1.11 us -> 0.01 us
  transfers between devices with their start and end apart: 24 -> 25, of which waited for: 16 -> 16; matrix products, arithmetic and copies ran while one was open for 0% -> 0% of each run, Pallas kernels for 16% -> 13%
where the time goes in v5:
time: 72.7 us; the launch traced here: 72.5 us
  starting transfers between devices  30.6 us (42%)
  waiting for transfers between devices  27.4 us (38%)
  Pallas kernels  14.2 us (20%)
    ppermute x25, starting transfers between devices, exchange(): lax.ppermute(x, axis, [(i, i ^ flip) for i in range(lax.axis_size(axis))])  30.6 us
    ppermute x25, waiting for transfers between devices, exchange(): lax.ppermute(x, axis, [(i, i ^ flip) for i in range(lax.axis_size(axis))])  27.4 us
    pallas_call x27, Pallas kernels, call(): pl.pallas_call(kernel, out_shape=out_shape, in_specs=[HBM] * hbm + [VMEM]...  14.2 us
  transfers between devices with their start and end apart: 25, of which 16 were waited for; matrix products, arithmetic and copies ran while one was open for 0% of the time, Pallas kernels for 13%

profile of v5, /device:TPU:0, one launch (start us, length us, event | category | flops | bytes accessed | tf_op | source)
XLA Modules:
  0.0 72.5 jit_solution(1639727014373179685)
XLA Ops:
  0.0 2.9 %shard_map.64 = (bf16[2,528,256]{2,1,0:T(8,128)(2,1)S(1)}, bf16[512,640]{1,0:T(8,128)(2,1)S(1)}, bf16[2,640,256]{2,1,0:T(8,128)(2,1)S(1)}, bf16[4,640,256]{2,1,0:T(8,128)(2,1)S(1)}, f32[1,768]{1,0:T(1,128)S(1)}) custom-call(bf16[1,640,512]{2,1,0:T(8,128)(2,1)} %grads_hbm.1, bf16[1,640,2048]{2,1,0:T(8,128)(2,1)} %inputs_hbm.1, f32[1,512]{1,0:T(1,128)} %out_decay.1, ...), custom_call_target="tpu_custom_call" | custom-call | flops 1000000000 | bytes 100000000 | tf_op jit(solution)/shard_map/pallas_call | solution.py:302
  2.9 0.5 collective-permute-start
  3.4 1.0 %shard_map.65 = (bf16[2,528,256]{2,1,0:T(8,128)(2,1)S(1)}, bf16[512,640]{1,0:T(8,128)(2,1)S(1)}) custom-call(bf16[512,640]{1,0:T(8,128)(2,1)S(1)} %get-tuple-element.35.refs_0_, bf16[2,640,256]{2,1,0:T(8,128)(2,1)S(1)} %get-tuple-element.36.refs_1_, bf16[2,528,256]{2,1,0:T(8,128)(2,1)S(1)} %get-tuple-element.37.refs_2_), custom_call_target="tpu_custom_call" | custom-call | flops 1000000000 | bytes 100000000 | tf_op jit(solution)/shard_map/pallas_call | solution.py:302
  5.4 3.0 %collective-permute-start.3 = (bf16[1,528,128]{2,1,0:T(8,128)(2,1)S(1)}, bf16[1,528,128]{2,1,0:T(8,128)(2,1)S(1)}, u32[]{:S(2)}, u32[]{:S(2)}) collective-permute-start(bf16[1,528,128]{2,1,0:T(8,128)(2,1)S(1)} %shard_map.66.refs_3_), channel_id=1, source_target_pairs={{0,2},{1,3},{2,0},{3,1},{4,6},{5,7},{6,4},{7,5},{8,10},{9,11},{10,... | collective-permute-start | bytes 405512 | tf_op jit(solution)/shard_map/ppermute | solution.py:21
  9.0 3.8 %collective-permute-done.3.refs_3_ = bf16[1,528,128]{2,1,0:T(8,128)(2,1)S(1)} collective-permute-done((bf16[1,528,128]{2,1,0:T(8,128)(2,1)S(1)}, bf16[1,528,128]{2,1,0:T(8,128)(2,1)S(1)}, u32[]{:S(2)}, u32[]{:S(2)}) %collective-permute-start.3) | collective-permute-done | bytes 135200 | tf_op jit(solution)/shard_map/ppermute | solution.py:21
  13.3 3.2 %collective-permute-start.5 = (bf16[1,528,128]{2,1,0:T(8,128)(2,1)S(1)}, bf16[1,528,128]{2,1,0:T(8,128)(2,1)S(1)}, u32[]{:S(2)}, u32[]{:S(2)}) collective-permute-start(bf16[1,528,128]{2,1,0:T(8,128)(2,1)S(1)} %shard_map.68.refs_3_), channel_id=1, source_target_pairs={{0,4},{1,5},{2,6},{3,7},{4,0},{5,1},{6,2},{7,3},{8,12},{9,13},{10,... | collective-permute-start | bytes 405512 | tf_op jit(solution)/shard_map/ppermute | solution.py:21
  16.9 1.6 %collective-permute-start.6 = (bf16[1,528,128]{2,1,0:T(8,128)(2,1)S(1)}, bf16[1,528,128]{2,1,0:T(8,128)(2,1)S(1)}, u32[]{:S(2)}, u32[]{:S(2)}) collective-permute-start(bf16[1,528,128]{2,1,0:T(8,128)(2,1)S(1)} %shard_map.69.refs_4_), channel_id=1, source_target_pairs={{0,2},{1,3},{2,0},{3,1},{4,6},{5,7},{6,4},{7,5},{8,10},{9,11},{10,... | collective-permute-start | bytes 405512 | tf_op jit(solution)/shard_map/ppermute | solution.py:21
  19.4 1.6 %collective-permute-start.4 = (f32[1,768]{1,0:T(1,128)S(1)}, f32[1,768]{1,0:T(1,128)S(1)}, u32[]{:S(2)}, u32[]{:S(2)}) collective-permute-start(f32[1,768]{1,0:T(1,128)S(1)} %get-tuple-element.42.refs_0_), channel_id=1, source_target_pairs={{0,8},{8,0},{16,24},{24,16},{1,9},{9,1},{17,25},{25,17},{2,10},{10... | collective-permute-start | bytes 9224 | tf_op jit(solution)/shard_map/ppermute | solution.py:21
  21.3 0.7 collective-permute-start.10
  22.0 1.1 %collective-permute-done.4.refs_1_ = f32[1,768]{1,0:T(1,128)S(1)} collective-permute-done((f32[1,768]{1,0:T(1,128)S(1)}, f32[1,768]{1,0:T(1,128)S(1)}, u32[]{:S(2)}, u32[]{:S(2)}) %collective-permute-start.4) | collective-permute-done | bytes 3104 | tf_op jit(solution)/shard_map/ppermute | solution.py:21
  23.6 0.6 shard_map.74
  24.2 3.9 %collective-permute-start.7 = (bf16[528,128]{1,0:T(8,128)(2,1)S(1)}, bf16[528,128]{1,0:T(8,128)(2,1)S(1)}, u32[]{:S(2)}, u32[]{:S(2)}) collective-permute-start(bf16[528,128]{1,0:T(8,128)(2,1)S(1)} %get-tuple-element.48.refs_7_), channel_id=1, source_target_pairs={{0,8},{8,0},{16,24},{24,16},{1,9},{9,1},{17,25},{25,17},{2,10},{10... | collective-permute-start | bytes 405512 | tf_op jit(solution)/shard_map/ppermute | solution.py:21
  28.3 0.6 shard_map.77
  29.0 1.6 %collective-permute-start.11 = (bf16[528,128]{1,0:T(8,128)(2,1)S(1)}, bf16[528,128]{1,0:T(8,128)(2,1)S(1)}, u32[]{:S(2)}, u32[]{:S(2)}) collective-permute-start(bf16[528,128]{1,0:T(8,128)(2,1)S(1)} %get-tuple-element.53), channel_id=1, source_target_pairs={{0,16},{8,24},{16,0},{24,8},{1,17},{9,25},{17,1},{25,9},{2,18},{10... | collective-permute-start | bytes 405512 | tf_op jit(solution)/shard_map/ppermute | solution.py:21
  31.5 1.6 %collective-permute-start.8 = (bf16[528,128]{1,0:T(8,128)(2,1)S(1)}, bf16[528,128]{1,0:T(8,128)(2,1)S(1)}, u32[]{:S(2)}, u32[]{:S(2)}) collective-permute-start(bf16[528,128]{1,0:T(8,128)(2,1)S(1)} %get-tuple-element.51), channel_id=1, source_target_pairs={{0,16},{8,24},{16,0},{24,8},{1,17},{9,25},{17,1},{25,9},{2,18},{10... | collective-permute-start | bytes 405512 | tf_op jit(solution)/shard_map/ppermute | solution.py:21
  33.1 1.0 %collective-permute-done.11.message_ref = bf16[528,128]{1,0:T(8,128)(2,1)S(1)} collective-permute-done((bf16[528,128]{1,0:T(8,128)(2,1)S(1)}, bf16[528,128]{1,0:T(8,128)(2,1)S(1)}, u32[]{:S(2)}, u32[]{:S(2)}) %collective-permute-start.11) | collective-permute-done | bytes 135200 | tf_op jit(solution)/shard_map/ppermute | solution.py:21
  34.4 2.6 %collective-permute-start.12 = (bf16[528,128]{1,0:T(8,128)(2,1)S(1)}, bf16[528,128]{1,0:T(8,128)(2,1)S(1)}, u32[]{:S(2)}, u32[]{:S(2)}) collective-permute-start(bf16[528,128]{1,0:T(8,128)(2,1)S(1)} %get-tuple-element.55), channel_id=1, source_target_pairs={{0,8},{8,0},{16,24},{24,16},{1,9},{9,1},{17,25},{25,17},{2,10},{10... | collective-permute-start | bytes 405512 | tf_op jit(solution)/shard_map/ppermute | solution.py:21
  37.5 0.9 %collective-permute-start.15 = (bf16[512,128]{1,0:T(8,128)(2,1)S(1)}, bf16[512,128]{1,0:T(8,128)(2,1)S(1)}, u32[]{:S(2)}, u32[]{:S(2)}) collective-permute-start(bf16[512,128]{1,0:T(8,128)(2,1)S(1)} %shard_map.76.refs_5_.refs_1_), channel_id=1, source_target_pairs={{0,2},{1,3},{2,0},{3,1},{4,6},{5,7},{6,4},{7,5},{8,10},{9,11},{10,... | collective-permute-start | bytes 393224 | tf_op jit(solution)/shard_map/ppermute | solution.py:21
  38.4 2.4 %collective-permute-start.13 = (bf16[512,128]{1,0:T(8,128)(2,1)S(1)}, bf16[512,128]{1,0:T(8,128)(2,1)S(1)}, u32[]{:S(2)}, u32[]{:S(2)}) collective-permute-start(bf16[512,128]{1,0:T(8,128)(2,1)S(1)} %shard_map.76.refs_5_.refs_1_), channel_id=1, source_target_pairs={{0,4},{1,5},{2,6},{3,7},{4,0},{5,1},{6,2},{7,3},{8,12},{9,13},{10,... | collective-permute-start | bytes 393224 | tf_op jit(solution)/shard_map/ppermute | solution.py:21
  41.2 0.6 collective-permute-start.14
  41.8 2.8 %collective-permute-start.16 = (bf16[512,128]{1,0:T(8,128)(2,1)S(1)}, bf16[512,128]{1,0:T(8,128)(2,1)S(1)}, u32[]{:S(2)}, u32[]{:S(2)}) collective-permute-start(bf16[512,128]{1,0:T(8,128)(2,1)S(1)} %shard_map.79.refs_2_), channel_id=1, source_target_pairs={{0,2},{1,3},{2,0},{3,1},{4,6},{5,7},{6,4},{7,5},{8,10},{9,11},{10,... | collective-permute-start | bytes 393224 | tf_op jit(solution)/shard_map/ppermute | solution.py:21
  44.7 5.2 %collective-permute-done.13.refs_3_.refs_0_ = bf16[512,128]{1,0:T(8,128)(2,1)S(1)} collective-permute-done((bf16[512,128]{1,0:T(8,128)(2,1)S(1)}, bf16[512,128]{1,0:T(8,128)(2,1)S(1)}, u32[]{:S(2)}, u32[]{:S(2)}) %collective-permute-start.13) | collective-permute-done | bytes 131104 | tf_op jit(solution)/shard_map/ppermute | solution.py:21
  50.0 1.5 %collective-permute-done.14.refs_4_ = bf16[512,128]{1,0:T(8,128)(2,1)S(1)} collective-permute-done((bf16[512,128]{1,0:T(8,128)(2,1)S(1)}, bf16[512,128]{1,0:T(8,128)(2,1)S(1)}, u32[]{:S(2)}, u32[]{:S(2)}) %collective-permute-start.14) | collective-permute-done | bytes 131104 | tf_op jit(solution)/shard_map/ppermute | solution.py:21
  52.7 3.1 %collective-permute-done.17.refs_4_ = bf16[1,512,128]{2,1,0:T(8,128)(2,1)S(1)} collective-permute-done((bf16[1,512,128]{2,1,0:T(8,128)(2,1)S(1)}, bf16[1,512,128]{2,1,0:T(8,128)(2,1)S(1)}, u32[]{:S(2)}, u32[]{:S(2)}) %collective-permute-start.17) | collective-permute-done | bytes 131104 | tf_op jit(solution)/shard_map/ppermute | solution.py:21
  56.4 0.8 %collective-permute-done.18.refs_2_ = bf16[512,128]{1,0:T(8,128)(2,1)S(1)} collective-permute-done((bf16[512,128]{1,0:T(8,128)(2,1)S(1)}, bf16[512,128]{1,0:T(8,128)(2,1)S(1)}, u32[]{:S(2)}, u32[]{:S(2)}) %collective-permute-start.18) | collective-permute-done | bytes 131104 | tf_op jit(solution)/shard_map/ppermute | solution.py:21
  57.9 1.3 %collective-permute-done.20.theirs_ref = bf16[528,256]{1,0:T(8,128)(2,1)S(1)} collective-permute-done((bf16[528,256]{1,0:T(8,128)(2,1)S(1)}, bf16[528,256]{1,0:T(8,128)(2,1)S(1)}, u32[]{:S(2)}, u32[]{:S(2)}) %collective-permute-start.20) | collective-permute-done | bytes 270368 | tf_op jit(solution)/shard_map/ppermute | solution.py:21
  59.8 1.0 %collective-permute-start.21 = (bf16[528,128]{1,0:T(8,128)(2,1)S(1)}, bf16[528,128]{1,0:T(8,128)(2,1)S(1)}, u32[]{:S(2)}, u32[]{:S(2)}) collective-permute-start(bf16[528,128]{1,0:T(8,128)(2,1)S(1)} %get-tuple-element.59), channel_id=1, source_target_pairs={{0,8},{8,0},{16,24},{24,16},{1,9},{9,1},{17,25},{25,17},{2,10},{10... | collective-permute-start | bytes 405512 | tf_op jit(solution)/shard_map/ppermute | solution.py:21
  60.8 4.7 %collective-permute-done.23.message_ref = bf16[528,128]{1,0:T(8,128)(2,1)S(1)} collective-permute-done((bf16[528,128]{1,0:T(8,128)(2,1)S(1)}, bf16[528,128]{1,0:T(8,128)(2,1)S(1)}, u32[]{:S(2)}, u32[]{:S(2)}) %collective-permute-start.23) | collective-permute-done | bytes 135200 | tf_op jit(solution)/shard_map/ppermute | solution.py:21
  66.4 1.2 %collective-permute-start.22 = (bf16[528,128]{1,0:T(8,128)(2,1)S(1)}, bf16[528,128]{1,0:T(8,128)(2,1)S(1)}, u32[]{:S(2)}, u32[]{:S(2)}) collective-permute-start(bf16[528,128]{1,0:T(8,128)(2,1)S(1)} %get-tuple-element.61), channel_id=1, source_target_pairs={{0,16},{8,24},{16,0},{24,8},{1,17},{9,25},{17,1},{25,9},{2,18},{10... | collective-permute-start | bytes 405512 | tf_op jit(solution)/shard_map/ppermute | solution.py:21
  67.6 3.3 %collective-permute-done.24.refs_3_ = bf16[528,128]{1,0:T(8,128)(2,1)S(1)} collective-permute-done((bf16[528,128]{1,0:T(8,128)(2,1)S(1)}, bf16[528,128]{1,0:T(8,128)(2,1)S(1)}, u32[]{:S(2)}, u32[]{:S(2)}) %collective-permute-start.24) | collective-permute-done | bytes 135200 | tf_op jit(solution)/shard_map/ppermute | solution.py:21
  70.9 0.6 collective-permute-done.22.refs_1_
  71.4 1.1 %shard_map.90 = bf16[1,256,512]{2,1,0:T(8,128)(2,1)} custom-call(f32[512,128]{1,0:T(8,128)S(1)} %get-tuple-element.44.cols_ref.refs_5_.refs_2_, f32[24,256]{1,0:T(8,128)S(1)} %get-tuple-element.45.rows_ref.refs_6_.refs_3_, f32[512,128]{1,0:T(8,128)S(1)} %get-tuple-element.60.refs_0_, bf16[528,128]{1,0:T(8,128)(2,1)S(1)} %collective-permute-done.22.refs_1_, ...), custom_call_target="tpu_custom_call" | custom-call | flops 1000000000 | bytes 100000000 | tf_op jit(solution)/shard_map/pallas_call | solution.py:302
  (49 shorter events, 10.6 us)
Async XLA Ops:
  2.9 2.1 %collective-permute-start = (bf16[2,528,256]{2,1,0:T(8,128)(2,1)S(1)}, bf16[2,528,256]{2,1,0:T(8,128)(2,1)S(1)}, u32[]{:S(2)}, u32[]{:S(2)}) collective-permute-start(bf16[2,528,256]{2,1,0:T(8,128)(2,1)S(1)} %get-tuple-element.37.refs_2_), channel_id=1, source_target_pairs={{0,1},{1,0},{2,3},{3,2},{4,5},{5,4},{6,7},{7,6},{8,9},{9,8},{10,11... | collective-permute-start | bytes 1622024 | tf_op jit(solution)/shard_map/ppermute | solution.py:21
  4.4 4.6 %collective-permute-start.1 = (bf16[2,528,256]{2,1,0:T(8,128)(2,1)S(1)}, bf16[2,528,256]{2,1,0:T(8,128)(2,1)S(1)}, u32[]{:S(2)}, u32[]{:S(2)}) collective-permute-start(bf16[2,528,256]{2,1,0:T(8,128)(2,1)S(1)} %get-tuple-element.41), channel_id=1, source_target_pairs={{0,1},{1,0},{2,3},{3,2},{4,5},{5,4},{6,7},{7,6},{8,9},{9,8},{10,11... | collective-permute-start | bytes 1622024 | tf_op jit(solution)/shard_map/ppermute | solution.py:21
  5.4 7.4 %collective-permute-start.3 = (bf16[1,528,128]{2,1,0:T(8,128)(2,1)S(1)}, bf16[1,528,128]{2,1,0:T(8,128)(2,1)S(1)}, u32[]{:S(2)}, u32[]{:S(2)}) collective-permute-start(bf16[1,528,128]{2,1,0:T(8,128)(2,1)S(1)} %shard_map.66.refs_3_), channel_id=1, source_target_pairs={{0,2},{1,3},{2,0},{3,1},{4,6},{5,7},{6,4},{7,5},{8,10},{9,11},{10,... | collective-permute-start | bytes 405512 | tf_op jit(solution)/shard_map/ppermute | solution.py:21
  8.9 9.6 %collective-permute-start.2 = (bf16[1,528,128]{2,1,0:T(8,128)(2,1)S(1)}, bf16[1,528,128]{2,1,0:T(8,128)(2,1)S(1)}, u32[]{:S(2)}, u32[]{:S(2)}) collective-permute-start(bf16[1,528,128]{2,1,0:T(8,128)(2,1)S(1)} %shard_map.67.refs_4_), channel_id=1, source_target_pairs={{0,2},{1,3},{2,0},{3,1},{4,6},{5,7},{6,4},{7,5},{8,10},{9,11},{10,... | collective-permute-start | bytes 405512 | tf_op jit(solution)/shard_map/ppermute | solution.py:21
  13.3 10.3 %collective-permute-start.5 = (bf16[1,528,128]{2,1,0:T(8,128)(2,1)S(1)}, bf16[1,528,128]{2,1,0:T(8,128)(2,1)S(1)}, u32[]{:S(2)}, u32[]{:S(2)}) collective-permute-start(bf16[1,528,128]{2,1,0:T(8,128)(2,1)S(1)} %shard_map.68.refs_3_), channel_id=1, source_target_pairs={{0,4},{1,5},{2,6},{3,7},{4,0},{5,1},{6,2},{7,3},{8,12},{9,13},{10,... | collective-permute-start | bytes 405512 | tf_op jit(solution)/shard_map/ppermute | solution.py:21
  16.9 6.7 %collective-permute-start.6 = (bf16[1,528,128]{2,1,0:T(8,128)(2,1)S(1)}, bf16[1,528,128]{2,1,0:T(8,128)(2,1)S(1)}, u32[]{:S(2)}, u32[]{:S(2)}) collective-permute-start(bf16[1,528,128]{2,1,0:T(8,128)(2,1)S(1)} %shard_map.69.refs_4_), channel_id=1, source_target_pairs={{0,2},{1,3},{2,0},{3,1},{4,6},{5,7},{6,4},{7,5},{8,10},{9,11},{10,... | collective-permute-start | bytes 405512 | tf_op jit(solution)/shard_map/ppermute | solution.py:21
  19.4 3.7 %collective-permute-start.4 = (f32[1,768]{1,0:T(1,128)S(1)}, f32[1,768]{1,0:T(1,128)S(1)}, u32[]{:S(2)}, u32[]{:S(2)}) collective-permute-start(f32[1,768]{1,0:T(1,128)S(1)} %get-tuple-element.42.refs_0_), channel_id=1, source_target_pairs={{0,8},{8,0},{16,24},{24,16},{1,9},{9,1},{17,25},{25,17},{2,10},{10... | collective-permute-start | bytes 9224 | tf_op jit(solution)/shard_map/ppermute | solution.py:21
  21.0 7.3 %collective-permute-start.9 = (bf16[1,528,128]{2,1,0:T(8,128)(2,1)S(1)}, bf16[1,528,128]{2,1,0:T(8,128)(2,1)S(1)}, u32[]{:S(2)}, u32[]{:S(2)}) collective-permute-start(bf16[1,528,128]{2,1,0:T(8,128)(2,1)S(1)} %shard_map.70.refs_4_), channel_id=1, source_target_pairs={{0,4},{1,5},{2,6},{3,7},{4,0},{5,1},{6,2},{7,3},{8,12},{9,13},{10,... | collective-permute-start | bytes 405512 | tf_op jit(solution)/shard_map/ppermute | solution.py:21
  21.3 6.8 %collective-permute-start.10 = (bf16[1,528,128]{2,1,0:T(8,128)(2,1)S(1)}, bf16[1,528,128]{2,1,0:T(8,128)(2,1)S(1)}, u32[]{:S(2)}, u32[]{:S(2)}) collective-permute-start(bf16[1,528,128]{2,1,0:T(8,128)(2,1)S(1)} %get-tuple-element.43.refs_2_.refs_5_), channel_id=1, source_target_pairs={{0,2},{1,3},{2,0},{3,1},{4,6},{5,7},{6,4},{7,5},{8,10},{9,11},{10,... | collective-permute-start | bytes 405512 | tf_op jit(solution)/shard_map/ppermute | solution.py:21
  24.2 6.4 %copy-start = (bf16[1,256,2048]{2,1,0:T(8,128)(2,1)S(1)}, bf16[1,256,2048]{2,1,0:T(8,128)(2,1)}, u32[]{:S(2)}) copy-start(bf16[1,256,2048]{2,1,0:T(8,128)(2,1)} %refs_0_.1) | copy-start | bytes 3145732
  24.2 6.4 %copy-start.1 = (bf16[1,512,512]{2,1,0:T(8,128)(2,1)S(1)}, bf16[1,512,512]{2,1,0:T(8,128)(2,1)}, u32[]{:S(2)}) copy-start(bf16[1,512,512]{2,1,0:T(8,128)(2,1)} %refs_1_.1) | copy-start | bytes 1572868
  24.2 6.9 %collective-permute-start.7 = (bf16[528,128]{1,0:T(8,128)(2,1)S(1)}, bf16[528,128]{1,0:T(8,128)(2,1)S(1)}, u32[]{:S(2)}, u32[]{:S(2)}) collective-permute-start(bf16[528,128]{1,0:T(8,128)(2,1)S(1)} %get-tuple-element.48.refs_7_), channel_id=1, source_target_pairs={{0,8},{8,0},{16,24},{24,16},{1,9},{9,1},{17,25},{25,17},{2,10},{10... | collective-permute-start | bytes 405512 | tf_op jit(solution)/shard_map/ppermute | solution.py:21
  29.0 5.1 %collective-permute-start.11 = (bf16[528,128]{1,0:T(8,128)(2,1)S(1)}, bf16[528,128]{1,0:T(8,128)(2,1)S(1)}, u32[]{:S(2)}, u32[]{:S(2)}) collective-permute-start(bf16[528,128]{1,0:T(8,128)(2,1)S(1)} %get-tuple-element.53), channel_id=1, source_target_pairs={{0,16},{8,24},{16,0},{24,8},{1,17},{9,25},{17,1},{25,9},{2,18},{10... | collective-permute-start | bytes 405512 | tf_op jit(solution)/shard_map/ppermute | solution.py:21
  31.5 5.6 %collective-permute-start.8 = (bf16[528,128]{1,0:T(8,128)(2,1)S(1)}, bf16[528,128]{1,0:T(8,128)(2,1)S(1)}, u32[]{:S(2)}, u32[]{:S(2)}) collective-permute-start(bf16[528,128]{1,0:T(8,128)(2,1)S(1)} %get-tuple-element.51), channel_id=1, source_target_pairs={{0,16},{8,24},{16,0},{24,8},{1,17},{9,25},{17,1},{25,9},{2,18},{10... | collective-permute-start | bytes 405512 | tf_op jit(solution)/shard_map/ppermute | solution.py:21
  33.1 19.3 %collective-permute-start.19 = (bf16[1024,256]{1,0:T(8,128)(2,1)S(1)}, bf16[1024,256]{1,0:T(8,128)(2,1)S(1)}, u32[]{:S(2)}, u32[]{:S(2)}) collective-permute-start(bf16[1024,256]{1,0:T(8,128)(2,1)S(1)} %get-tuple-element.56), channel_id=1, source_target_pairs={{0,1},{1,0},{2,3},{3,2},{4,5},{5,4},{6,7},{7,6},{8,9},{9,8},{10,11... | collective-permute-start | bytes 1572872 | tf_op jit(solution)/shard_map/ppermute | solution.py:21
  34.4 6.3 %collective-permute-start.12 = (bf16[528,128]{1,0:T(8,128)(2,1)S(1)}, bf16[528,128]{1,0:T(8,128)(2,1)S(1)}, u32[]{:S(2)}, u32[]{:S(2)}) collective-permute-start(bf16[528,128]{1,0:T(8,128)(2,1)S(1)} %get-tuple-element.55), channel_id=1, source_target_pairs={{0,8},{8,0},{16,24},{24,16},{1,9},{9,1},{17,25},{25,17},{2,10},{10... | collective-permute-start | bytes 405512 | tf_op jit(solution)/shard_map/ppermute | solution.py:21
  37.5 7.2 %collective-permute-start.15 = (bf16[512,128]{1,0:T(8,128)(2,1)S(1)}, bf16[512,128]{1,0:T(8,128)(2,1)S(1)}, u32[]{:S(2)}, u32[]{:S(2)}) collective-permute-start(bf16[512,128]{1,0:T(8,128)(2,1)S(1)} %shard_map.76.refs_5_.refs_1_), channel_id=1, source_target_pairs={{0,2},{1,3},{2,0},{3,1},{4,6},{5,7},{6,4},{7,5},{8,10},{9,11},{10,... | collective-permute-start | bytes 393224 | tf_op jit(solution)/shard_map/ppermute | solution.py:21
  38.4 11.6 %collective-permute-start.13 = (bf16[512,128]{1,0:T(8,128)(2,1)S(1)}, bf16[512,128]{1,0:T(8,128)(2,1)S(1)}, u32[]{:S(2)}, u32[]{:S(2)}) collective-permute-start(bf16[512,128]{1,0:T(8,128)(2,1)S(1)} %shard_map.76.refs_5_.refs_1_), channel_id=1, source_target_pairs={{0,4},{1,5},{2,6},{3,7},{4,0},{5,1},{6,2},{7,3},{8,12},{9,13},{10,... | collective-permute-start | bytes 393224 | tf_op jit(solution)/shard_map/ppermute | solution.py:21
  41.2 10.4 %collective-permute-start.14 = (bf16[512,128]{1,0:T(8,128)(2,1)S(1)}, bf16[512,128]{1,0:T(8,128)(2,1)S(1)}, u32[]{:S(2)}, u32[]{:S(2)}) collective-permute-start(bf16[512,128]{1,0:T(8,128)(2,1)S(1)} %shard_map.79.refs_2_), channel_id=1, source_target_pairs={{0,4},{1,5},{2,6},{3,7},{4,0},{5,1},{6,2},{7,3},{8,12},{9,13},{10,... | collective-permute-start | bytes 393224 | tf_op jit(solution)/shard_map/ppermute | solution.py:21
  41.8 10.9 %collective-permute-start.16 = (bf16[512,128]{1,0:T(8,128)(2,1)S(1)}, bf16[512,128]{1,0:T(8,128)(2,1)S(1)}, u32[]{:S(2)}, u32[]{:S(2)}) collective-permute-start(bf16[512,128]{1,0:T(8,128)(2,1)S(1)} %shard_map.79.refs_2_), channel_id=1, source_target_pairs={{0,2},{1,3},{2,0},{3,1},{4,6},{5,7},{6,4},{7,5},{8,10},{9,11},{10,... | collective-permute-start | bytes 393224 | tf_op jit(solution)/shard_map/ppermute | solution.py:21
  50.0 5.8 %collective-permute-start.17 = (bf16[1,512,128]{2,1,0:T(8,128)(2,1)S(1)}, bf16[1,512,128]{2,1,0:T(8,128)(2,1)S(1)}, u32[]{:S(2)}, u32[]{:S(2)}) collective-permute-start(bf16[1,512,128]{2,1,0:T(8,128)(2,1)S(1)} %shard_map.81), channel_id=1, source_target_pairs={{0,2},{1,3},{2,0},{3,1},{4,6},{5,7},{6,4},{7,5},{8,10},{9,11},{10,... | collective-permute-start | bytes 393224 | tf_op jit(solution)/shard_map/ppermute | solution.py:21
  51.6 5.6 %collective-permute-start.18 = (bf16[512,128]{1,0:T(8,128)(2,1)S(1)}, bf16[512,128]{1,0:T(8,128)(2,1)S(1)}, u32[]{:S(2)}, u32[]{:S(2)}) collective-permute-start(bf16[512,128]{1,0:T(8,128)(2,1)S(1)} %collective-permute-done.14.refs_4_), channel_id=1, source_target_pairs={{0,2},{1,3},{2,0},{3,1},{4,6},{5,7},{6,4},{7,5},{8,10},{9,11},{10,... | collective-permute-start | bytes 393224 | tf_op jit(solution)/shard_map/ppermute | solution.py:21
  57.6 1.6 %collective-permute-start.20 = (bf16[528,256]{1,0:T(8,128)(2,1)S(1)}, bf16[528,256]{1,0:T(8,128)(2,1)S(1)}, u32[]{:S(2)}, u32[]{:S(2)}) collective-permute-start(bf16[528,256]{1,0:T(8,128)(2,1)S(1)} %shard_map.86), channel_id=1, source_target_pairs={{0,1},{1,0},{2,3},{3,2},{4,5},{5,4},{6,7},{7,6},{8,9},{9,8},{10,11... | collective-permute-start | bytes 811016 | tf_op jit(solution)/shard_map/ppermute | solution.py:21
  59.7 5.7 %collective-permute-start.23 = (bf16[528,128]{1,0:T(8,128)(2,1)S(1)}, bf16[528,128]{1,0:T(8,128)(2,1)S(1)}, u32[]{:S(2)}, u32[]{:S(2)}) collective-permute-start(bf16[528,128]{1,0:T(8,128)(2,1)S(1)} %get-tuple-element.62), channel_id=1, source_target_pairs={{0,16},{8,24},{16,0},{24,8},{1,17},{9,25},{17,1},{25,9},{2,18},{10... | collective-permute-start | bytes 405512 | tf_op jit(solution)/shard_map/ppermute | solution.py:21
  59.8 6.2 %collective-permute-start.21 = (bf16[528,128]{1,0:T(8,128)(2,1)S(1)}, bf16[528,128]{1,0:T(8,128)(2,1)S(1)}, u32[]{:S(2)}, u32[]{:S(2)}) collective-permute-start(bf16[528,128]{1,0:T(8,128)(2,1)S(1)} %get-tuple-element.59), channel_id=1, source_target_pairs={{0,8},{8,0},{16,24},{24,16},{1,9},{9,1},{17,25},{25,17},{2,10},{10... | collective-permute-start | bytes 405512 | tf_op jit(solution)/shard_map/ppermute | solution.py:21
  65.8 5.1 %collective-permute-start.24 = (bf16[528,128]{1,0:T(8,128)(2,1)S(1)}, bf16[528,128]{1,0:T(8,128)(2,1)S(1)}, u32[]{:S(2)}, u32[]{:S(2)}) collective-permute-start(bf16[528,128]{1,0:T(8,128)(2,1)S(1)} %get-tuple-element.64), channel_id=1, source_target_pairs={{0,8},{8,0},{16,24},{24,16},{1,9},{9,1},{17,25},{25,17},{2,10},{10... | collective-permute-start | bytes 405512 | tf_op jit(solution)/shard_map/ppermute | solution.py:21
  66.4 5.1 %collective-permute-start.22 = (bf16[528,128]{1,0:T(8,128)(2,1)S(1)}, bf16[528,128]{1,0:T(8,128)(2,1)S(1)}, u32[]{:S(2)}, u32[]{:S(2)}) collective-permute-start(bf16[528,128]{1,0:T(8,128)(2,1)S(1)} %get-tuple-element.61), channel_id=1, source_target_pairs={{0,16},{8,24},{16,0},{24,8},{1,17},{9,25},{17,1},{25,9},{2,18},{10... | collective-permute-start | bytes 405512 | tf_op jit(solution)/shard_map/ppermute | solution.py:21

commit v6 on v5

--- a/solution.py
+++ b/solution.py
@@ -38,7 +38,7 @@
     y = ref[:rows, :].astype(F32)
     square = lax.rsqrt(lax.rsqrt(jnp.abs(y) + 1e-37))
     size = square * lax.rsqrt(square)
-    return jnp.where(y < 0, -size, size) * top
+    return jnp.where(y < 0, -top, top) * size
 
 
 def core_and_chip():
@@ -190,13 +190,19 @@
 
 
 def last_kernel(places, cols_ref, rows_ref, *refs):
-    out_ref = refs[-1]
+    out_ref, turned_ref, sems = refs[-3:]
+    copies = []
     for i, place in enumerate(places):
         value_ref, message_ref = refs[2 * i : 2 * i + 2]
         lanes = value_ref.shape[1]
         columns = slice(i * lanes, (i + 1) * lanes)
         lower = weighed([place], cols_ref, rows_ref.at[:, columns], [message_ref], value_ref[...])
-        out_ref[0, columns, :] = lower.T.astype(BF16)
+        turned_ref[columns, :] = lower.astype(BF16).T
+        rows = pl.ds(i * lanes, lanes)
+        copies.append(pltpu.make_async_copy(turned_ref.at[rows], out_ref.at[0, rows], sems.at[i]))
+        copies[-1].start()
+    for copy in copies:
+        copy.wait()
 
 
 def digits(layers):
@@ -291,7 +297,7 @@
     def message(n):
         return shape(width + TAIL, n, dtype=BF16)
 
-    def call(kernel, out_shape, *operands, grant=4 * 2**20, hbm=0, scratch=(), after=()):
+    def call(kernel, out_shape, *operands, grant=4 * 2**20, hbm=0, scratch=(), after=(), anywhere=False):
         several = isinstance(out_shape, (list, tuple))
         if after:
             inner, count = kernel, len(operands)
@@ -305,10 +311,10 @@
             in_specs=[HBM] * hbm
             + [VMEM] * (len(operands) - hbm)
             + [pl.BlockSpec(memory_space=pl.ANY)] * len(after),
-            out_specs=[VMEM] * len(out_shape) if several else VMEM,
+            out_specs=[VMEM] * len(out_shape) if several else pl.BlockSpec(memory_space=pl.ANY) if anywhere else VMEM,
             scratch_shapes=scratch,
             compiler_params=pltpu.CompilerParams(vmem_limit_bytes=grant),
-            cost_estimate=pl.CostEstimate(flops=10**9, bytes_accessed=10**8, transcendentals=0),
+            cost_estimate=pl.CostEstimate(flops=12 * 10**8, bytes_accessed=10**8, transcendentals=0),
         )(*operands, *after)
 
     odd, even = list(range(1, chips, 2)), list(range(0, chips, 2))
@@ -504,7 +510,15 @@
     operands = [x for part in range(pieces) for x in cross(downs, part, value, total, sent[part])]
     _, _, cols, in_rows, *_ = downs[-1]
     places = [order_of(downs, part)[3] for part in range(pieces)]
-    return call(functools.partial(last_kernel, places), shape(1, rows, width, dtype=BF16), cols, in_rows, *operands)
+    return call(
+        functools.partial(last_kernel, places),
+        shape(1, rows, width, dtype=BF16),
+        cols,
+        in_rows,
+        *operands,
+        scratch=[pltpu.VMEM((rows, width), BF16), pltpu.SemaphoreType.DMA((len(places),))],
+        anywhere=True,
+    )
 
 
 def solution(mesh):

time: 72.7 us -> 72.5 us (level)
  no operation moved by 1% of the time
where the time goes in v6:
time: 72.5 us; the launch traced here: 72.4 us
  starting transfers between devices  30.7 us (42%)
  waiting for transfers between devices  27.3 us (38%)
  Pallas kernels  14.1 us (19%)
    ppermute x25, starting transfers between devices, exchange(): lax.ppermute(x, axis, [(i, i ^ flip) for i in range(lax.axis_size(axis))])  30.7 us
    ppermute x25, waiting for transfers between devices, exchange(): lax.ppermute(x, axis, [(i, i ^ flip) for i in range(lax.axis_size(axis))])  27.3 us
    pallas_call x27, Pallas kernels, call(): pl.pallas_call(kernel, out_shape=out_shape, in_specs=[HBM] * hbm + [VMEM]...  14.1 us
  transfers between devices with their start and end apart: 25, of which 16 were waited for; matrix products, arithmetic and copies ran while one was open for 0% of the time, Pallas kernels for 13%

profile of v6, /device:TPU:0, one launch (start us, length us, event | category | flops | bytes accessed | tf_op | source)
XLA Modules:
  0.0 72.4 jit_solution(9954733448263358225)
XLA Ops:
  0.0 2.9 %shard_map.64 = (bf16[2,528,256]{2,1,0:T(8,128)(2,1)S(1)}, bf16[512,640]{1,0:T(8,128)(2,1)S(1)}, bf16[2,640,256]{2,1,0:T(8,128)(2,1)S(1)}, bf16[4,640,256]{2,1,0:T(8,128)(2,1)S(1)}, f32[1,768]{1,0:T(1,128)S(1)}) custom-call(bf16[1,640,512]{2,1,0:T(8,128)(2,1)} %grads_hbm.1, bf16[1,640,2048]{2,1,0:T(8,128)(2,1)} %inputs_hbm.1, f32[1,512]{1,0:T(1,128)} %out_decay.1, ...), custom_call_target="tpu_custom_call" | custom-call | flops 1200000000 | bytes 100000000 | tf_op jit(solution)/shard_map/pallas_call | solution.py:308
  2.9 0.5 collective-permute-start
  3.4 1.0 %shard_map.65 = (bf16[2,528,256]{2,1,0:T(8,128)(2,1)S(1)}, bf16[512,640]{1,0:T(8,128)(2,1)S(1)}) custom-call(bf16[512,640]{1,0:T(8,128)(2,1)S(1)} %get-tuple-element.35.refs_0_, bf16[2,640,256]{2,1,0:T(8,128)(2,1)S(1)} %get-tuple-element.36.refs_1_, bf16[2,528,256]{2,1,0:T(8,128)(2,1)S(1)} %get-tuple-element.37.refs_2_), custom_call_target="tpu_custom_call" | custom-call | flops 1200000000 | bytes 100000000 | tf_op jit(solution)/shard_map/pallas_call | solution.py:308
  5.4 3.0 %collective-permute-start.3 = (bf16[1,528,128]{2,1,0:T(8,128)(2,1)S(1)}, bf16[1,528,128]{2,1,0:T(8,128)(2,1)S(1)}, u32[]{:S(2)}, u32[]{:S(2)}) collective-permute-start(bf16[1,528,128]{2,1,0:T(8,128)(2,1)S(1)} %shard_map.66.refs_3_), channel_id=1, source_target_pairs={{0,2},{1,3},{2,0},{3,1},{4,6},{5,7},{6,4},{7,5},{8,10},{9,11},{10,... | collective-permute-start | bytes 405512 | tf_op jit(solution)/shard_map/ppermute | solution.py:21
  9.0 3.8 %collective-permute-done.3.refs_3_ = bf16[1,528,128]{2,1,0:T(8,128)(2,1)S(1)} collective-permute-done((bf16[1,528,128]{2,1,0:T(8,128)(2,1)S(1)}, bf16[1,528,128]{2,1,0:T(8,128)(2,1)S(1)}, u32[]{:S(2)}, u32[]{:S(2)}) %collective-permute-start.3) | collective-permute-done | bytes 135200 | tf_op jit(solution)/shard_map/ppermute | solution.py:21
  13.3 3.1 %collective-permute-start.5 = (bf16[1,528,128]{2,1,0:T(8,128)(2,1)S(1)}, bf16[1,528,128]{2,1,0:T(8,128)(2,1)S(1)}, u32[]{:S(2)}, u32[]{:S(2)}) collective-permute-start(bf16[1,528,128]{2,1,0:T(8,128)(2,1)S(1)} %shard_map.68.refs_3_), channel_id=1, source_target_pairs={{0,4},{1,5},{2,6},{3,7},{4,0},{5,1},{6,2},{7,3},{8,12},{9,13},{10,... | collective-permute-start | bytes 405512 | tf_op jit(solution)/shard_map/ppermute | solution.py:21
  16.9 1.6 %collective-permute-start.6 = (bf16[1,528,128]{2,1,0:T(8,128)(2,1)S(1)}, bf16[1,528,128]{2,1,0:T(8,128)(2,1)S(1)}, u32[]{:S(2)}, u32[]{:S(2)}) collective-permute-start(bf16[1,528,128]{2,1,0:T(8,128)(2,1)S(1)} %shard_map.69.refs_4_), channel_id=1, source_target_pairs={{0,2},{1,3},{2,0},{3,1},{4,6},{5,7},{6,4},{7,5},{8,10},{9,11},{10,... | collective-permute-start | bytes 405512 | tf_op jit(solution)/shard_map/ppermute | solution.py:21
  19.4 1.6 %collective-permute-start.4 = (f32[1,768]{1,0:T(1,128)S(1)}, f32[1,768]{1,0:T(1,128)S(1)}, u32[]{:S(2)}, u32[]{:S(2)}) collective-permute-start(f32[1,768]{1,0:T(1,128)S(1)} %get-tuple-element.42.refs_0_), channel_id=1, source_target_pairs={{0,8},{8,0},{16,24},{24,16},{1,9},{9,1},{17,25},{25,17},{2,10},{10... | collective-permute-start | bytes 9224 | tf_op jit(solution)/shard_map/ppermute | solution.py:21
  21.3 0.7 collective-permute-start.10
  22.0 1.1 %collective-permute-done.4.refs_1_ = f32[1,768]{1,0:T(1,128)S(1)} collective-permute-done((f32[1,768]{1,0:T(1,128)S(1)}, f32[1,768]{1,0:T(1,128)S(1)}, u32[]{:S(2)}, u32[]{:S(2)}) %collective-permute-start.4) | collective-permute-done | bytes 3104 | tf_op jit(solution)/shard_map/ppermute | solution.py:21
  23.5 0.6 shard_map.74
  24.1 4.0 %collective-permute-start.7 = (bf16[528,128]{1,0:T(8,128)(2,1)S(1)}, bf16[528,128]{1,0:T(8,128)(2,1)S(1)}, u32[]{:S(2)}, u32[]{:S(2)}) collective-permute-start(bf16[528,128]{1,0:T(8,128)(2,1)S(1)} %get-tuple-element.48.refs_7_), channel_id=1, source_target_pairs={{0,8},{8,0},{16,24},{24,16},{1,9},{9,1},{17,25},{25,17},{2,10},{10... | collective-permute-start | bytes 405512 | tf_op jit(solution)/shard_map/ppermute | solution.py:21
  28.3 0.6 shard_map.77
  28.9 1.6 %collective-permute-start.11 = (bf16[528,128]{1,0:T(8,128)(2,1)S(1)}, bf16[528,128]{1,0:T(8,128)(2,1)S(1)}, u32[]{:S(2)}, u32[]{:S(2)}) collective-permute-start(bf16[528,128]{1,0:T(8,128)(2,1)S(1)} %get-tuple-element.53), channel_id=1, source_target_pairs={{0,16},{8,24},{16,0},{24,8},{1,17},{9,25},{17,1},{25,9},{2,18},{10... | collective-permute-start | bytes 405512 | tf_op jit(solution)/shard_map/ppermute | solution.py:21
  31.5 1.6 %collective-permute-start.8 = (bf16[528,128]{1,0:T(8,128)(2,1)S(1)}, bf16[528,128]{1,0:T(8,128)(2,1)S(1)}, u32[]{:S(2)}, u32[]{:S(2)}) collective-permute-start(bf16[528,128]{1,0:T(8,128)(2,1)S(1)} %get-tuple-element.51), channel_id=1, source_target_pairs={{0,16},{8,24},{16,0},{24,8},{1,17},{9,25},{17,1},{25,9},{2,18},{10... | collective-permute-start | bytes 405512 | tf_op jit(solution)/shard_map/ppermute | solution.py:21
  33.1 0.9 %collective-permute-done.11.message_ref = bf16[528,128]{1,0:T(8,128)(2,1)S(1)} collective-permute-done((bf16[528,128]{1,0:T(8,128)(2,1)S(1)}, bf16[528,128]{1,0:T(8,128)(2,1)S(1)}, u32[]{:S(2)}, u32[]{:S(2)}) %collective-permute-start.11) | collective-permute-done | bytes 135200 | tf_op jit(solution)/shard_map/ppermute | solution.py:21
  34.4 2.6 %collective-permute-start.12 = (bf16[528,128]{1,0:T(8,128)(2,1)S(1)}, bf16[528,128]{1,0:T(8,128)(2,1)S(1)}, u32[]{:S(2)}, u32[]{:S(2)}) collective-permute-start(bf16[528,128]{1,0:T(8,128)(2,1)S(1)} %get-tuple-element.55), channel_id=1, source_target_pairs={{0,8},{8,0},{16,24},{24,16},{1,9},{9,1},{17,25},{25,17},{2,10},{10... | collective-permute-start | bytes 405512 | tf_op jit(solution)/shard_map/ppermute | solution.py:21
  37.4 0.9 %collective-permute-start.15 = (bf16[512,128]{1,0:T(8,128)(2,1)S(1)}, bf16[512,128]{1,0:T(8,128)(2,1)S(1)}, u32[]{:S(2)}, u32[]{:S(2)}) collective-permute-start(bf16[512,128]{1,0:T(8,128)(2,1)S(1)} %shard_map.76.refs_5_.refs_1_), channel_id=1, source_target_pairs={{0,2},{1,3},{2,0},{3,1},{4,6},{5,7},{6,4},{7,5},{8,10},{9,11},{10,... | collective-permute-start | bytes 393224 | tf_op jit(solution)/shard_map/ppermute | solution.py:21
  38.3 2.4 %collective-permute-start.13 = (bf16[512,128]{1,0:T(8,128)(2,1)S(1)}, bf16[512,128]{1,0:T(8,128)(2,1)S(1)}, u32[]{:S(2)}, u32[]{:S(2)}) collective-permute-start(bf16[512,128]{1,0:T(8,128)(2,1)S(1)} %shard_map.76.refs_5_.refs_1_), channel_id=1, source_target_pairs={{0,4},{1,5},{2,6},{3,7},{4,0},{5,1},{6,2},{7,3},{8,12},{9,13},{10,... | collective-permute-start | bytes 393224 | tf_op jit(solution)/shard_map/ppermute | solution.py:21
  41.2 0.6 collective-permute-start.14
  41.8 2.8 %collective-permute-start.16 = (bf16[512,128]{1,0:T(8,128)(2,1)S(1)}, bf16[512,128]{1,0:T(8,128)(2,1)S(1)}, u32[]{:S(2)}, u32[]{:S(2)}) collective-permute-start(bf16[512,128]{1,0:T(8,128)(2,1)S(1)} %shard_map.79.refs_2_), channel_id=1, source_target_pairs={{0,2},{1,3},{2,0},{3,1},{4,6},{5,7},{6,4},{7,5},{8,10},{9,11},{10,... | collective-permute-start | bytes 393224 | tf_op jit(solution)/shard_map/ppermute | solution.py:21
  44.7 5.2 %collective-permute-done.13.refs_3_.refs_0_ = bf16[512,128]{1,0:T(8,128)(2,1)S(1)} collective-permute-done((bf16[512,128]{1,0:T(8,128)(2,1)S(1)}, bf16[512,128]{1,0:T(8,128)(2,1)S(1)}, u32[]{:S(2)}, u32[]{:S(2)}) %collective-permute-start.13) | collective-permute-done | bytes 131104 | tf_op jit(solution)/shard_map/ppermute | solution.py:21
  50.0 1.6 %collective-permute-done.14.refs_4_ = bf16[512,128]{1,0:T(8,128)(2,1)S(1)} collective-permute-done((bf16[512,128]{1,0:T(8,128)(2,1)S(1)}, bf16[512,128]{1,0:T(8,128)(2,1)S(1)}, u32[]{:S(2)}, u32[]{:S(2)}) %collective-permute-start.14) | collective-permute-done | bytes 131104 | tf_op jit(solution)/shard_map/ppermute | solution.py:21
  52.6 3.0 %collective-permute-done.17.refs_4_ = bf16[1,512,128]{2,1,0:T(8,128)(2,1)S(1)} collective-permute-done((bf16[1,512,128]{2,1,0:T(8,128)(2,1)S(1)}, bf16[1,512,128]{2,1,0:T(8,128)(2,1)S(1)}, u32[]{:S(2)}, u32[]{:S(2)}) %collective-permute-start.17) | collective-permute-done | bytes 131104 | tf_op jit(solution)/shard_map/ppermute | solution.py:21
  56.3 0.8 %collective-permute-done.18.refs_2_ = bf16[512,128]{1,0:T(8,128)(2,1)S(1)} collective-permute-done((bf16[512,128]{1,0:T(8,128)(2,1)S(1)}, bf16[512,128]{1,0:T(8,128)(2,1)S(1)}, u32[]{:S(2)}, u32[]{:S(2)}) %collective-permute-start.18) | collective-permute-done | bytes 131104 | tf_op jit(solution)/shard_map/ppermute | solution.py:21
  57.8 1.3 %collective-permute-done.20.theirs_ref = bf16[528,256]{1,0:T(8,128)(2,1)S(1)} collective-permute-done((bf16[528,256]{1,0:T(8,128)(2,1)S(1)}, bf16[528,256]{1,0:T(8,128)(2,1)S(1)}, u32[]{:S(2)}, u32[]{:S(2)}) %collective-permute-start.20) | collective-permute-done | bytes 270368 | tf_op jit(solution)/shard_map/ppermute | solution.py:21
  59.7 1.0 %collective-permute-start.21 = (bf16[528,128]{1,0:T(8,128)(2,1)S(1)}, bf16[528,128]{1,0:T(8,128)(2,1)S(1)}, u32[]{:S(2)}, u32[]{:S(2)}) collective-permute-start(bf16[528,128]{1,0:T(8,128)(2,1)S(1)} %get-tuple-element.59), channel_id=1, source_target_pairs={{0,8},{8,0},{16,24},{24,16},{1,9},{9,1},{17,25},{25,17},{2,10},{10... | collective-permute-start | bytes 405512 | tf_op jit(solution)/shard_map/ppermute | solution.py:21
  60.7 4.6 %collective-permute-done.23.message_ref = bf16[528,128]{1,0:T(8,128)(2,1)S(1)} collective-permute-done((bf16[528,128]{1,0:T(8,128)(2,1)S(1)}, bf16[528,128]{1,0:T(8,128)(2,1)S(1)}, u32[]{:S(2)}, u32[]{:S(2)}) %collective-permute-start.23) | collective-permute-done | bytes 135200 | tf_op jit(solution)/shard_map/ppermute | solution.py:21
  66.3 1.2 %collective-permute-start.22 = (bf16[528,128]{1,0:T(8,128)(2,1)S(1)}, bf16[528,128]{1,0:T(8,128)(2,1)S(1)}, u32[]{:S(2)}, u32[]{:S(2)}) collective-permute-start(bf16[528,128]{1,0:T(8,128)(2,1)S(1)} %get-tuple-element.61), channel_id=1, source_target_pairs={{0,16},{8,24},{16,0},{24,8},{1,17},{9,25},{17,1},{25,9},{2,18},{10... | collective-permute-start | bytes 405512 | tf_op jit(solution)/shard_map/ppermute | solution.py:21
  67.5 3.3 %collective-permute-done.24.refs_3_ = bf16[528,128]{1,0:T(8,128)(2,1)S(1)} collective-permute-done((bf16[528,128]{1,0:T(8,128)(2,1)S(1)}, bf16[528,128]{1,0:T(8,128)(2,1)S(1)}, u32[]{:S(2)}, u32[]{:S(2)}) %collective-permute-start.24) | collective-permute-done | bytes 135200 | tf_op jit(solution)/shard_map/ppermute | solution.py:21
  70.8 0.6 collective-permute-done.22.refs_1_
  71.3 1.1 %shard_map.90 = bf16[1,256,512]{2,1,0:T(8,128)(2,1)} custom-call(f32[512,128]{1,0:T(8,128)S(1)} %get-tuple-element.44.cols_ref.refs_5_.refs_2_, f32[24,256]{1,0:T(8,128)S(1)} %get-tuple-element.45.rows_ref.refs_6_.refs_3_, f32[512,128]{1,0:T(8,128)S(1)} %get-tuple-element.60.refs_0_, bf16[528,128]{1,0:T(8,128)(2,1)S(1)} %collective-permute-done.22.refs_1_, ...), custom_call_target="tpu_custom_call" | custom-call | flops 1200000000 | bytes 100000000 | tf_op jit(solution)/shard_map/pallas_call | solution.py:308
  (49 shorter events, 10.6 us)
Async XLA Ops:
  2.9 2.1 %collective-permute-start = (bf16[2,528,256]{2,1,0:T(8,128)(2,1)S(1)}, bf16[2,528,256]{2,1,0:T(8,128)(2,1)S(1)}, u32[]{:S(2)}, u32[]{:S(2)}) collective-permute-start(bf16[2,528,256]{2,1,0:T(8,128)(2,1)S(1)} %get-tuple-element.37.refs_2_), channel_id=1, source_target_pairs={{0,1},{1,0},{2,3},{3,2},{4,5},{5,4},{6,7},{7,6},{8,9},{9,8},{10,11... | collective-permute-start | bytes 1622024 | tf_op jit(solution)/shard_map/ppermute | solution.py:21
  4.4 4.6 %collective-permute-start.1 = (bf16[2,528,256]{2,1,0:T(8,128)(2,1)S(1)}, bf16[2,528,256]{2,1,0:T(8,128)(2,1)S(1)}, u32[]{:S(2)}, u32[]{:S(2)}) collective-permute-start(bf16[2,528,256]{2,1,0:T(8,128)(2,1)S(1)} %get-tuple-element.41), channel_id=1, source_target_pairs={{0,1},{1,0},{2,3},{3,2},{4,5},{5,4},{6,7},{7,6},{8,9},{9,8},{10,11... | collective-permute-start | bytes 1622024 | tf_op jit(solution)/shard_map/ppermute | solution.py:21
  5.4 7.4 %collective-permute-start.3 = (bf16[1,528,128]{2,1,0:T(8,128)(2,1)S(1)}, bf16[1,528,128]{2,1,0:T(8,128)(2,1)S(1)}, u32[]{:S(2)}, u32[]{:S(2)}) collective-permute-start(bf16[1,528,128]{2,1,0:T(8,128)(2,1)S(1)} %shard_map.66.refs_3_), channel_id=1, source_target_pairs={{0,2},{1,3},{2,0},{3,1},{4,6},{5,7},{6,4},{7,5},{8,10},{9,11},{10,... | collective-permute-start | bytes 405512 | tf_op jit(solution)/shard_map/ppermute | solution.py:21
  8.9 9.6 %collective-permute-start.2 = (bf16[1,528,128]{2,1,0:T(8,128)(2,1)S(1)}, bf16[1,528,128]{2,1,0:T(8,128)(2,1)S(1)}, u32[]{:S(2)}, u32[]{:S(2)}) collective-permute-start(bf16[1,528,128]{2,1,0:T(8,128)(2,1)S(1)} %shard_map.67.refs_4_), channel_id=1, source_target_pairs={{0,2},{1,3},{2,0},{3,1},{4,6},{5,7},{6,4},{7,5},{8,10},{9,11},{10,... | collective-permute-start | bytes 405512 | tf_op jit(solution)/shard_map/ppermute | solution.py:21
  13.3 10.2 %collective-permute-start.5 = (bf16[1,528,128]{2,1,0:T(8,128)(2,1)S(1)}, bf16[1,528,128]{2,1,0:T(8,128)(2,1)S(1)}, u32[]{:S(2)}, u32[]{:S(2)}) collective-permute-start(bf16[1,528,128]{2,1,0:T(8,128)(2,1)S(1)} %shard_map.68.refs_3_), channel_id=1, source_target_pairs={{0,4},{1,5},{2,6},{3,7},{4,0},{5,1},{6,2},{7,3},{8,12},{9,13},{10,... | collective-permute-start | bytes 405512 | tf_op jit(solution)/shard_map/ppermute | solution.py:21
  16.9 6.7 %collective-permute-start.6 = (bf16[1,528,128]{2,1,0:T(8,128)(2,1)S(1)}, bf16[1,528,128]{2,1,0:T(8,128)(2,1)S(1)}, u32[]{:S(2)}, u32[]{:S(2)}) collective-permute-start(bf16[1,528,128]{2,1,0:T(8,128)(2,1)S(1)} %shard_map.69.refs_4_), channel_id=1, source_target_pairs={{0,2},{1,3},{2,0},{3,1},{4,6},{5,7},{6,4},{7,5},{8,10},{9,11},{10,... | collective-permute-start | bytes 405512 | tf_op jit(solution)/shard_map/ppermute | solution.py:21
  19.4 3.7 %collective-permute-start.4 = (f32[1,768]{1,0:T(1,128)S(1)}, f32[1,768]{1,0:T(1,128)S(1)}, u32[]{:S(2)}, u32[]{:S(2)}) collective-permute-start(f32[1,768]{1,0:T(1,128)S(1)} %get-tuple-element.42.refs_0_), channel_id=1, source_target_pairs={{0,8},{8,0},{16,24},{24,16},{1,9},{9,1},{17,25},{25,17},{2,10},{10... | collective-permute-start | bytes 9224 | tf_op jit(solution)/shard_map/ppermute | solution.py:21
  21.0 7.3 %collective-permute-start.9 = (bf16[1,528,128]{2,1,0:T(8,128)(2,1)S(1)}, bf16[1,528,128]{2,1,0:T(8,128)(2,1)S(1)}, u32[]{:S(2)}, u32[]{:S(2)}) collective-permute-start(bf16[1,528,128]{2,1,0:T(8,128)(2,1)S(1)} %shard_map.70.refs_4_), channel_id=1, source_target_pairs={{0,4},{1,5},{2,6},{3,7},{4,0},{5,1},{6,2},{7,3},{8,12},{9,13},{10,... | collective-permute-start | bytes 405512 | tf_op jit(solution)/shard_map/ppermute | solution.py:21
  21.3 6.8 %collective-permute-start.10 = (bf16[1,528,128]{2,1,0:T(8,128)(2,1)S(1)}, bf16[1,528,128]{2,1,0:T(8,128)(2,1)S(1)}, u32[]{:S(2)}, u32[]{:S(2)}) collective-permute-start(bf16[1,528,128]{2,1,0:T(8,128)(2,1)S(1)} %get-tuple-element.43.refs_2_.refs_5_), channel_id=1, source_target_pairs={{0,2},{1,3},{2,0},{3,1},{4,6},{5,7},{6,4},{7,5},{8,10},{9,11},{10,... | collective-permute-start | bytes 405512 | tf_op jit(solution)/shard_map/ppermute | solution.py:21
  24.1 6.4 %copy-start = (bf16[1,256,2048]{2,1,0:T(8,128)(2,1)S(1)}, bf16[1,256,2048]{2,1,0:T(8,128)(2,1)}, u32[]{:S(2)}) copy-start(bf16[1,256,2048]{2,1,0:T(8,128)(2,1)} %refs_0_.1) | copy-start | bytes 3145732
  24.1 6.4 %copy-start.1 = (bf16[1,512,512]{2,1,0:T(8,128)(2,1)S(1)}, bf16[1,512,512]{2,1,0:T(8,128)(2,1)}, u32[]{:S(2)}) copy-start(bf16[1,512,512]{2,1,0:T(8,128)(2,1)} %refs_1_.1) | copy-start | bytes 1572868
  24.1 7.0 %collective-permute-start.7 = (bf16[528,128]{1,0:T(8,128)(2,1)S(1)}, bf16[528,128]{1,0:T(8,128)(2,1)S(1)}, u32[]{:S(2)}, u32[]{:S(2)}) collective-permute-start(bf16[528,128]{1,0:T(8,128)(2,1)S(1)} %get-tuple-element.48.refs_7_), channel_id=1, source_target_pairs={{0,8},{8,0},{16,24},{24,16},{1,9},{9,1},{17,25},{25,17},{2,10},{10... | collective-permute-start | bytes 405512 | tf_op jit(solution)/shard_map/ppermute | solution.py:21
  28.9 5.1 %collective-permute-start.11 = (bf16[528,128]{1,0:T(8,128)(2,1)S(1)}, bf16[528,128]{1,0:T(8,128)(2,1)S(1)}, u32[]{:S(2)}, u32[]{:S(2)}) collective-permute-start(bf16[528,128]{1,0:T(8,128)(2,1)S(1)} %get-tuple-element.53), channel_id=1, source_target_pairs={{0,16},{8,24},{16,0},{24,8},{1,17},{9,25},{17,1},{25,9},{2,18},{10... | collective-permute-start | bytes 405512 | tf_op jit(solution)/shard_map/ppermute | solution.py:21
  31.5 5.5 %collective-permute-start.8 = (bf16[528,128]{1,0:T(8,128)(2,1)S(1)}, bf16[528,128]{1,0:T(8,128)(2,1)S(1)}, u32[]{:S(2)}, u32[]{:S(2)}) collective-permute-start(bf16[528,128]{1,0:T(8,128)(2,1)S(1)} %get-tuple-element.51), channel_id=1, source_target_pairs={{0,16},{8,24},{16,0},{24,8},{1,17},{9,25},{17,1},{25,9},{2,18},{10... | collective-permute-start | bytes 405512 | tf_op jit(solution)/shard_map/ppermute | solution.py:21
  33.1 19.2 %collective-permute-start.19 = (bf16[1024,256]{1,0:T(8,128)(2,1)S(1)}, bf16[1024,256]{1,0:T(8,128)(2,1)S(1)}, u32[]{:S(2)}, u32[]{:S(2)}) collective-permute-start(bf16[1024,256]{1,0:T(8,128)(2,1)S(1)} %get-tuple-element.56), channel_id=1, source_target_pairs={{0,1},{1,0},{2,3},{3,2},{4,5},{5,4},{6,7},{7,6},{8,9},{9,8},{10,11... | collective-permute-start | bytes 1572872 | tf_op jit(solution)/shard_map/ppermute | solution.py:21
  34.4 6.3 %collective-permute-start.12 = (bf16[528,128]{1,0:T(8,128)(2,1)S(1)}, bf16[528,128]{1,0:T(8,128)(2,1)S(1)}, u32[]{:S(2)}, u32[]{:S(2)}) collective-permute-start(bf16[528,128]{1,0:T(8,128)(2,1)S(1)} %get-tuple-element.55), channel_id=1, source_target_pairs={{0,8},{8,0},{16,24},{24,16},{1,9},{9,1},{17,25},{25,17},{2,10},{10... | collective-permute-start | bytes 405512 | tf_op jit(solution)/shard_map/ppermute | solution.py:21
  37.4 7.3 %collective-permute-start.15 = (bf16[512,128]{1,0:T(8,128)(2,1)S(1)}, bf16[512,128]{1,0:T(8,128)(2,1)S(1)}, u32[]{:S(2)}, u32[]{:S(2)}) collective-permute-start(bf16[512,128]{1,0:T(8,128)(2,1)S(1)} %shard_map.76.refs_5_.refs_1_), channel_id=1, source_target_pairs={{0,2},{1,3},{2,0},{3,1},{4,6},{5,7},{6,4},{7,5},{8,10},{9,11},{10,... | collective-permute-start | bytes 393224 | tf_op jit(solution)/shard_map/ppermute | solution.py:21
  38.3 11.6 %collective-permute-start.13 = (bf16[512,128]{1,0:T(8,128)(2,1)S(1)}, bf16[512,128]{1,0:T(8,128)(2,1)S(1)}, u32[]{:S(2)}, u32[]{:S(2)}) collective-permute-start(bf16[512,128]{1,0:T(8,128)(2,1)S(1)} %shard_map.76.refs_5_.refs_1_), channel_id=1, source_target_pairs={{0,4},{1,5},{2,6},{3,7},{4,0},{5,1},{6,2},{7,3},{8,12},{9,13},{10,... | collective-permute-start | bytes 393224 | tf_op jit(solution)/shard_map/ppermute | solution.py:21
  41.2 10.4 %collective-permute-start.14 = (bf16[512,128]{1,0:T(8,128)(2,1)S(1)}, bf16[512,128]{1,0:T(8,128)(2,1)S(1)}, u32[]{:S(2)}, u32[]{:S(2)}) collective-permute-start(bf16[512,128]{1,0:T(8,128)(2,1)S(1)} %shard_map.79.refs_2_), channel_id=1, source_target_pairs={{0,4},{1,5},{2,6},{3,7},{4,0},{5,1},{6,2},{7,3},{8,12},{9,13},{10,... | collective-permute-start | bytes 393224 | tf_op jit(solution)/shard_map/ppermute | solution.py:21
  41.8 10.8 %collective-permute-start.16 = (bf16[512,128]{1,0:T(8,128)(2,1)S(1)}, bf16[512,128]{1,0:T(8,128)(2,1)S(1)}, u32[]{:S(2)}, u32[]{:S(2)}) collective-permute-start(bf16[512,128]{1,0:T(8,128)(2,1)S(1)} %shard_map.79.refs_2_), channel_id=1, source_target_pairs={{0,2},{1,3},{2,0},{3,1},{4,6},{5,7},{6,4},{7,5},{8,10},{9,11},{10,... | collective-permute-start | bytes 393224 | tf_op jit(solution)/shard_map/ppermute | solution.py:21
  49.9 5.8 %collective-permute-start.17 = (bf16[1,512,128]{2,1,0:T(8,128)(2,1)S(1)}, bf16[1,512,128]{2,1,0:T(8,128)(2,1)S(1)}, u32[]{:S(2)}, u32[]{:S(2)}) collective-permute-start(bf16[1,512,128]{2,1,0:T(8,128)(2,1)S(1)} %shard_map.81), channel_id=1, source_target_pairs={{0,2},{1,3},{2,0},{3,1},{4,6},{5,7},{6,4},{7,5},{8,10},{9,11},{10,... | collective-permute-start | bytes 393224 | tf_op jit(solution)/shard_map/ppermute | solution.py:21
  51.5 5.6 %collective-permute-start.18 = (bf16[512,128]{1,0:T(8,128)(2,1)S(1)}, bf16[512,128]{1,0:T(8,128)(2,1)S(1)}, u32[]{:S(2)}, u32[]{:S(2)}) collective-permute-start(bf16[512,128]{1,0:T(8,128)(2,1)S(1)} %collective-permute-done.14.refs_4_), channel_id=1, source_target_pairs={{0,2},{1,3},{2,0},{3,1},{4,6},{5,7},{6,4},{7,5},{8,10},{9,11},{10,... | collective-permute-start | bytes 393224 | tf_op jit(solution)/shard_map/ppermute | solution.py:21
  57.5 1.6 %collective-permute-start.20 = (bf16[528,256]{1,0:T(8,128)(2,1)S(1)}, bf16[528,256]{1,0:T(8,128)(2,1)S(1)}, u32[]{:S(2)}, u32[]{:S(2)}) collective-permute-start(bf16[528,256]{1,0:T(8,128)(2,1)S(1)} %shard_map.86), channel_id=1, source_target_pairs={{0,1},{1,0},{2,3},{3,2},{4,5},{5,4},{6,7},{7,6},{8,9},{9,8},{10,11... | collective-permute-start | bytes 811016 | tf_op jit(solution)/shard_map/ppermute | solution.py:21
  59.6 5.7 %collective-permute-start.23 = (bf16[528,128]{1,0:T(8,128)(2,1)S(1)}, bf16[528,128]{1,0:T(8,128)(2,1)S(1)}, u32[]{:S(2)}, u32[]{:S(2)}) collective-permute-start(bf16[528,128]{1,0:T(8,128)(2,1)S(1)} %get-tuple-element.62), channel_id=1, source_target_pairs={{0,16},{8,24},{16,0},{24,8},{1,17},{9,25},{17,1},{25,9},{2,18},{10... | collective-permute-start | bytes 405512 | tf_op jit(solution)/shard_map/ppermute | solution.py:21
  59.7 6.2 %collective-permute-start.21 = (bf16[528,128]{1,0:T(8,128)(2,1)S(1)}, bf16[528,128]{1,0:T(8,128)(2,1)S(1)}, u32[]{:S(2)}, u32[]{:S(2)}) collective-permute-start(bf16[528,128]{1,0:T(8,128)(2,1)S(1)} %get-tuple-element.59), channel_id=1, source_target_pairs={{0,8},{8,0},{16,24},{24,16},{1,9},{9,1},{17,25},{25,17},{2,10},{10... | collective-permute-start | bytes 405512 | tf_op jit(solution)/shard_map/ppermute | solution.py:21
  65.7 5.1 %collective-permute-start.24 = (bf16[528,128]{1,0:T(8,128)(2,1)S(1)}, bf16[528,128]{1,0:T(8,128)(2,1)S(1)}, u32[]{:S(2)}, u32[]{:S(2)}) collective-permute-start(bf16[528,128]{1,0:T(8,128)(2,1)S(1)} %get-tuple-element.64), channel_id=1, source_target_pairs={{0,8},{8,0},{16,24},{24,16},{1,9},{9,1},{17,25},{25,17},{2,10},{10... | collective-permute-start | bytes 405512 | tf_op jit(solution)/shard_map/ppermute | solution.py:21
  66.3 5.1 %collective-permute-start.22 = (bf16[528,128]{1,0:T(8,128)(2,1)S(1)}, bf16[528,128]{1,0:T(8,128)(2,1)S(1)}, u32[]{:S(2)}, u32[]{:S(2)}) collective-permute-start(bf16[528,128]{1,0:T(8,128)(2,1)S(1)} %get-tuple-element.61), channel_id=1, source_target_pairs={{0,16},{8,24},{16,0},{24,8},{1,17},{9,25},{17,1},{25,9},{2,18},{10... | collective-permute-start | bytes 405512 | tf_op jit(solution)/shard_map/ppermute | solution.py:21

commit v7 on v6

--- a/solution.py
+++ b/solution.py
@@ -264,8 +264,8 @@
     rows_ref[...] = table[: rows_ref.shape[0], width:]
     if not last:
         me = mine
-        before = product(lambda q: q < me)
-        state_ref[0][...] = jnp.concatenate([product(lambda q: q >= 0), below * before, above * before], axis=0)
+        below, above = below * product(lambda q: q > me), above * product(lambda q: q < me)
+        state_ref[0][...] = jnp.concatenate([product(lambda q: q >= 0), below, above], axis=0)
 
 
 def weight_places(size, last):

time: 72.5 us -> 72.5 us (level)
  no operation moved by 1% of the time
where the time goes in v7:
time: 72.5 us; the launch traced here: 72.4 us
  starting transfers between devices  30.7 us (42%)
  waiting for transfers between devices  27.3 us (38%)
  Pallas kernels  14.1 us (19%)
    ppermute x25, starting transfers between devices, exchange(): lax.ppermute(x, axis, [(i, i ^ flip) for i in range(lax.axis_size(axis))])  30.7 us
    ppermute x25, waiting for transfers between devices, exchange(): lax.ppermute(x, axis, [(i, i ^ flip) for i in range(lax.axis_size(axis))])  27.3 us
    pallas_call x27, Pallas kernels, call(): pl.pallas_call(kernel, out_shape=out_shape, in_specs=[HBM] * hbm + [VMEM]...  14.1 us
  transfers between devices with their start and end apart: 25, of which 16 were waited for; matrix products, arithmetic and copies ran while one was open for 0% of the time, Pallas kernels for 13%

profile of v7, /device:TPU:0, one launch (start us, length us, event | category | flops | bytes accessed | tf_op | source)
XLA Modules:
  0.0 72.4 jit_solution(9954733448263358225)
XLA Ops:
  0.0 2.9 %shard_map.64 = (bf16[2,528,256]{2,1,0:T(8,128)(2,1)S(1)}, bf16[512,640]{1,0:T(8,128)(2,1)S(1)}, bf16[2,640,256]{2,1,0:T(8,128)(2,1)S(1)}, bf16[4,640,256]{2,1,0:T(8,128)(2,1)S(1)}, f32[1,768]{1,0:T(1,128)S(1)}) custom-call(bf16[1,640,512]{2,1,0:T(8,128)(2,1)} %grads_hbm.1, bf16[1,640,2048]{2,1,0:T(8,128)(2,1)} %inputs_hbm.1, f32[1,512]{1,0:T(1,128)} %out_decay.1, ...), custom_call_target="tpu_custom_call" | custom-call | flops 1200000000 | bytes 100000000 | tf_op jit(solution)/shard_map/pallas_call | solution.py:308
  2.9 0.5 collective-permute-start
  3.4 1.0 %shard_map.65 = (bf16[2,528,256]{2,1,0:T(8,128)(2,1)S(1)}, bf16[512,640]{1,0:T(8,128)(2,1)S(1)}) custom-call(bf16[512,640]{1,0:T(8,128)(2,1)S(1)} %get-tuple-element.35.refs_0_, bf16[2,640,256]{2,1,0:T(8,128)(2,1)S(1)} %get-tuple-element.36.refs_1_, bf16[2,528,256]{2,1,0:T(8,128)(2,1)S(1)} %get-tuple-element.37.refs_2_), custom_call_target="tpu_custom_call" | custom-call | flops 1200000000 | bytes 100000000 | tf_op jit(solution)/shard_map/pallas_call | solution.py:308
  5.4 3.0 %collective-permute-start.3 = (bf16[1,528,128]{2,1,0:T(8,128)(2,1)S(1)}, bf16[1,528,128]{2,1,0:T(8,128)(2,1)S(1)}, u32[]{:S(2)}, u32[]{:S(2)}) collective-permute-start(bf16[1,528,128]{2,1,0:T(8,128)(2,1)S(1)} %shard_map.66.refs_3_), channel_id=1, source_target_pairs={{0,2},{1,3},{2,0},{3,1},{4,6},{5,7},{6,4},{7,5},{8,10},{9,11},{10,... | collective-permute-start | bytes 405512 | tf_op jit(solution)/shard_map/ppermute | solution.py:21
  9.0 3.8 %collective-permute-done.3.refs_3_ = bf16[1,528,128]{2,1,0:T(8,128)(2,1)S(1)} collective-permute-done((bf16[1,528,128]{2,1,0:T(8,128)(2,1)S(1)}, bf16[1,528,128]{2,1,0:T(8,128)(2,1)S(1)}, u32[]{:S(2)}, u32[]{:S(2)}) %collective-permute-start.3) | collective-permute-done | bytes 135200 | tf_op jit(solution)/shard_map/ppermute | solution.py:21
  13.3 3.1 %collective-permute-start.5 = (bf16[1,528,128]{2,1,0:T(8,128)(2,1)S(1)}, bf16[1,528,128]{2,1,0:T(8,128)(2,1)S(1)}, u32[]{:S(2)}, u32[]{:S(2)}) collective-permute-start(bf16[1,528,128]{2,1,0:T(8,128)(2,1)S(1)} %shard_map.68.refs_3_), channel_id=1, source_target_pairs={{0,4},{1,5},{2,6},{3,7},{4,0},{5,1},{6,2},{7,3},{8,12},{9,13},{10,... | collective-permute-start | bytes 405512 | tf_op jit(solution)/shard_map/ppermute | solution.py:21
  16.9 1.6 %collective-permute-start.6 = (bf16[1,528,128]{2,1,0:T(8,128)(2,1)S(1)}, bf16[1,528,128]{2,1,0:T(8,128)(2,1)S(1)}, u32[]{:S(2)}, u32[]{:S(2)}) collective-permute-start(bf16[1,528,128]{2,1,0:T(8,128)(2,1)S(1)} %shard_map.69.refs_4_), channel_id=1, source_target_pairs={{0,2},{1,3},{2,0},{3,1},{4,6},{5,7},{6,4},{7,5},{8,10},{9,11},{10,... | collective-permute-start | bytes 405512 | tf_op jit(solution)/shard_map/ppermute | solution.py:21
  19.4 1.6 %collective-permute-start.4 = (f32[1,768]{1,0:T(1,128)S(1)}, f32[1,768]{1,0:T(1,128)S(1)}, u32[]{:S(2)}, u32[]{:S(2)}) collective-permute-start(f32[1,768]{1,0:T(1,128)S(1)} %get-tuple-element.42.refs_0_), channel_id=1, source_target_pairs={{0,8},{8,0},{16,24},{24,16},{1,9},{9,1},{17,25},{25,17},{2,10},{10... | collective-permute-start | bytes 9224 | tf_op jit(solution)/shard_map/ppermute | solution.py:21
  21.3 0.7 collective-permute-start.10
  22.0 1.1 %collective-permute-done.4.refs_1_ = f32[1,768]{1,0:T(1,128)S(1)} collective-permute-done((f32[1,768]{1,0:T(1,128)S(1)}, f32[1,768]{1,0:T(1,128)S(1)}, u32[]{:S(2)}, u32[]{:S(2)}) %collective-permute-start.4) | collective-permute-done | bytes 3104 | tf_op jit(solution)/shard_map/ppermute | solution.py:21
  23.5 0.6 shard_map.74
  24.1 4.0 %collective-permute-start.7 = (bf16[528,128]{1,0:T(8,128)(2,1)S(1)}, bf16[528,128]{1,0:T(8,128)(2,1)S(1)}, u32[]{:S(2)}, u32[]{:S(2)}) collective-permute-start(bf16[528,128]{1,0:T(8,128)(2,1)S(1)} %get-tuple-element.48.refs_7_), channel_id=1, source_target_pairs={{0,8},{8,0},{16,24},{24,16},{1,9},{9,1},{17,25},{25,17},{2,10},{10... | collective-permute-start | bytes 405512 | tf_op jit(solution)/shard_map/ppermute | solution.py:21
  28.3 0.6 shard_map.77
  28.9 1.6 %collective-permute-start.11 = (bf16[528,128]{1,0:T(8,128)(2,1)S(1)}, bf16[528,128]{1,0:T(8,128)(2,1)S(1)}, u32[]{:S(2)}, u32[]{:S(2)}) collective-permute-start(bf16[528,128]{1,0:T(8,128)(2,1)S(1)} %get-tuple-element.53), channel_id=1, source_target_pairs={{0,16},{8,24},{16,0},{24,8},{1,17},{9,25},{17,1},{25,9},{2,18},{10... | collective-permute-start | bytes 405512 | tf_op jit(solution)/shard_map/ppermute | solution.py:21
  31.5 1.6 %collective-permute-start.8 = (bf16[528,128]{1,0:T(8,128)(2,1)S(1)}, bf16[528,128]{1,0:T(8,128)(2,1)S(1)}, u32[]{:S(2)}, u32[]{:S(2)}) collective-permute-start(bf16[528,128]{1,0:T(8,128)(2,1)S(1)} %get-tuple-element.51), channel_id=1, source_target_pairs={{0,16},{8,24},{16,0},{24,8},{1,17},{9,25},{17,1},{25,9},{2,18},{10... | collective-permute-start | bytes 405512 | tf_op jit(solution)/shard_map/ppermute | solution.py:21
  33.1 0.9 %collective-permute-done.11.message_ref = bf16[528,128]{1,0:T(8,128)(2,1)S(1)} collective-permute-done((bf16[528,128]{1,0:T(8,128)(2,1)S(1)}, bf16[528,128]{1,0:T(8,128)(2,1)S(1)}, u32[]{:S(2)}, u32[]{:S(2)}) %collective-permute-start.11) | collective-permute-done | bytes 135200 | tf_op jit(solution)/shard_map/ppermute | solution.py:21
  34.4 2.6 %collective-permute-start.12 = (bf16[528,128]{1,0:T(8,128)(2,1)S(1)}, bf16[528,128]{1,0:T(8,128)(2,1)S(1)}, u32[]{:S(2)}, u32[]{:S(2)}) collective-permute-start(bf16[528,128]{1,0:T(8,128)(2,1)S(1)} %get-tuple-element.55), channel_id=1, source_target_pairs={{0,8},{8,0},{16,24},{24,16},{1,9},{9,1},{17,25},{25,17},{2,10},{10... | collective-permute-start | bytes 405512 | tf_op jit(solution)/shard_map/ppermute | solution.py:21
  37.4 0.9 %collective-permute-start.15 = (bf16[512,128]{1,0:T(8,128)(2,1)S(1)}, bf16[512,128]{1,0:T(8,128)(2,1)S(1)}, u32[]{:S(2)}, u32[]{:S(2)}) collective-permute-start(bf16[512,128]{1,0:T(8,128)(2,1)S(1)} %shard_map.76.refs_5_.refs_1_), channel_id=1, source_target_pairs={{0,2},{1,3},{2,0},{3,1},{4,6},{5,7},{6,4},{7,5},{8,10},{9,11},{10,... | collective-permute-start | bytes 393224 | tf_op jit(solution)/shard_map/ppermute | solution.py:21
  38.3 2.4 %collective-permute-start.13 = (bf16[512,128]{1,0:T(8,128)(2,1)S(1)}, bf16[512,128]{1,0:T(8,128)(2,1)S(1)}, u32[]{:S(2)}, u32[]{:S(2)}) collective-permute-start(bf16[512,128]{1,0:T(8,128)(2,1)S(1)} %shard_map.76.refs_5_.refs_1_), channel_id=1, source_target_pairs={{0,4},{1,5},{2,6},{3,7},{4,0},{5,1},{6,2},{7,3},{8,12},{9,13},{10,... | collective-permute-start | bytes 393224 | tf_op jit(solution)/shard_map/ppermute | solution.py:21
  41.2 0.6 collective-permute-start.14
  41.8 2.8 %collective-permute-start.16 = (bf16[512,128]{1,0:T(8,128)(2,1)S(1)}, bf16[512,128]{1,0:T(8,128)(2,1)S(1)}, u32[]{:S(2)}, u32[]{:S(2)}) collective-permute-start(bf16[512,128]{1,0:T(8,128)(2,1)S(1)} %shard_map.79.refs_2_), channel_id=1, source_target_pairs={{0,2},{1,3},{2,0},{3,1},{4,6},{5,7},{6,4},{7,5},{8,10},{9,11},{10,... | collective-permute-start | bytes 393224 | tf_op jit(solution)/shard_map/ppermute | solution.py:21
  44.7 5.2 %collective-permute-done.13.refs_3_.refs_0_ = bf16[512,128]{1,0:T(8,128)(2,1)S(1)} collective-permute-done((bf16[512,128]{1,0:T(8,128)(2,1)S(1)}, bf16[512,128]{1,0:T(8,128)(2,1)S(1)}, u32[]{:S(2)}, u32[]{:S(2)}) %collective-permute-start.13) | collective-permute-done | bytes 131104 | tf_op jit(solution)/shard_map/ppermute | solution.py:21
  50.0 1.6 %collective-permute-done.14.refs_4_ = bf16[512,128]{1,0:T(8,128)(2,1)S(1)} collective-permute-done((bf16[512,128]{1,0:T(8,128)(2,1)S(1)}, bf16[512,128]{1,0:T(8,128)(2,1)S(1)}, u32[]{:S(2)}, u32[]{:S(2)}) %collective-permute-start.14) | collective-permute-done | bytes 131104 | tf_op jit(solution)/shard_map/ppermute | solution.py:21
  52.6 3.0 %collective-permute-done.17.refs_4_ = bf16[1,512,128]{2,1,0:T(8,128)(2,1)S(1)} collective-permute-done((bf16[1,512,128]{2,1,0:T(8,128)(2,1)S(1)}, bf16[1,512,128]{2,1,0:T(8,128)(2,1)S(1)}, u32[]{:S(2)}, u32[]{:S(2)}) %collective-permute-start.17) | collective-permute-done | bytes 131104 | tf_op jit(solution)/shard_map/ppermute | solution.py:21
  56.3 0.8 %collective-permute-done.18.refs_2_ = bf16[512,128]{1,0:T(8,128)(2,1)S(1)} collective-permute-done((bf16[512,128]{1,0:T(8,128)(2,1)S(1)}, bf16[512,128]{1,0:T(8,128)(2,1)S(1)}, u32[]{:S(2)}, u32[]{:S(2)}) %collective-permute-start.18) | collective-permute-done | bytes 131104 | tf_op jit(solution)/shard_map/ppermute | solution.py:21
  57.8 1.3 %collective-permute-done.20.theirs_ref = bf16[528,256]{1,0:T(8,128)(2,1)S(1)} collective-permute-done((bf16[528,256]{1,0:T(8,128)(2,1)S(1)}, bf16[528,256]{1,0:T(8,128)(2,1)S(1)}, u32[]{:S(2)}, u32[]{:S(2)}) %collective-permute-start.20) | collective-permute-done | bytes 270368 | tf_op jit(solution)/shard_map/ppermute | solution.py:21
  59.7 1.0 %collective-permute-start.21 = (bf16[528,128]{1,0:T(8,128)(2,1)S(1)}, bf16[528,128]{1,0:T(8,128)(2,1)S(1)}, u32[]{:S(2)}, u32[]{:S(2)}) collective-permute-start(bf16[528,128]{1,0:T(8,128)(2,1)S(1)} %get-tuple-element.59), channel_id=1, source_target_pairs={{0,8},{8,0},{16,24},{24,16},{1,9},{9,1},{17,25},{25,17},{2,10},{10... | collective-permute-start | bytes 405512 | tf_op jit(solution)/shard_map/ppermute | solution.py:21
  60.7 4.6 %collective-permute-done.23.message_ref = bf16[528,128]{1,0:T(8,128)(2,1)S(1)} collective-permute-done((bf16[528,128]{1,0:T(8,128)(2,1)S(1)}, bf16[528,128]{1,0:T(8,128)(2,1)S(1)}, u32[]{:S(2)}, u32[]{:S(2)}) %collective-permute-start.23) | collective-permute-done | bytes 135200 | tf_op jit(solution)/shard_map/ppermute | solution.py:21
  66.3 1.2 %collective-permute-start.22 = (bf16[528,128]{1,0:T(8,128)(2,1)S(1)}, bf16[528,128]{1,0:T(8,128)(2,1)S(1)}, u32[]{:S(2)}, u32[]{:S(2)}) collective-permute-start(bf16[528,128]{1,0:T(8,128)(2,1)S(1)} %get-tuple-element.61), channel_id=1, source_target_pairs={{0,16},{8,24},{16,0},{24,8},{1,17},{9,25},{17,1},{25,9},{2,18},{10... | collective-permute-start | bytes 405512 | tf_op jit(solution)/shard_map/ppermute | solution.py:21
  67.5 3.3 %collective-permute-done.24.refs_3_ = bf16[528,128]{1,0:T(8,128)(2,1)S(1)} collective-permute-done((bf16[528,128]{1,0:T(8,128)(2,1)S(1)}, bf16[528,128]{1,0:T(8,128)(2,1)S(1)}, u32[]{:S(2)}, u32[]{:S(2)}) %collective-permute-start.24) | collective-permute-done | bytes 135200 | tf_op jit(solution)/shard_map/ppermute | solution.py:21
  70.8 0.6 collective-permute-done.22.refs_1_
  71.3 1.1 %shard_map.90 = bf16[1,256,512]{2,1,0:T(8,128)(2,1)} custom-call(f32[512,128]{1,0:T(8,128)S(1)} %get-tuple-element.44.cols_ref.refs_5_.refs_2_, f32[24,256]{1,0:T(8,128)S(1)} %get-tuple-element.45.rows_ref.refs_6_.refs_3_, f32[512,128]{1,0:T(8,128)S(1)} %get-tuple-element.60.refs_0_, bf16[528,128]{1,0:T(8,128)(2,1)S(1)} %collective-permute-done.22.refs_1_, ...), custom_call_target="tpu_custom_call" | custom-call | flops 1200000000 | bytes 100000000 | tf_op jit(solution)/shard_map/pallas_call | solution.py:308
  (49 shorter events, 10.6 us)
Async XLA Ops:
  2.9 2.1 %collective-permute-start = (bf16[2,528,256]{2,1,0:T(8,128)(2,1)S(1)}, bf16[2,528,256]{2,1,0:T(8,128)(2,1)S(1)}, u32[]{:S(2)}, u32[]{:S(2)}) collective-permute-start(bf16[2,528,256]{2,1,0:T(8,128)(2,1)S(1)} %get-tuple-element.37.refs_2_), channel_id=1, source_target_pairs={{0,1},{1,0},{2,3},{3,2},{4,5},{5,4},{6,7},{7,6},{8,9},{9,8},{10,11... | collective-permute-start | bytes 1622024 | tf_op jit(solution)/shard_map/ppermute | solution.py:21
  4.4 4.6 %collective-permute-start.1 = (bf16[2,528,256]{2,1,0:T(8,128)(2,1)S(1)}, bf16[2,528,256]{2,1,0:T(8,128)(2,1)S(1)}, u32[]{:S(2)}, u32[]{:S(2)}) collective-permute-start(bf16[2,528,256]{2,1,0:T(8,128)(2,1)S(1)} %get-tuple-element.41), channel_id=1, source_target_pairs={{0,1},{1,0},{2,3},{3,2},{4,5},{5,4},{6,7},{7,6},{8,9},{9,8},{10,11... | collective-permute-start | bytes 1622024 | tf_op jit(solution)/shard_map/ppermute | solution.py:21
  5.4 7.4 %collective-permute-start.3 = (bf16[1,528,128]{2,1,0:T(8,128)(2,1)S(1)}, bf16[1,528,128]{2,1,0:T(8,128)(2,1)S(1)}, u32[]{:S(2)}, u32[]{:S(2)}) collective-permute-start(bf16[1,528,128]{2,1,0:T(8,128)(2,1)S(1)} %shard_map.66.refs_3_), channel_id=1, source_target_pairs={{0,2},{1,3},{2,0},{3,1},{4,6},{5,7},{6,4},{7,5},{8,10},{9,11},{10,... | collective-permute-start | bytes 405512 | tf_op jit(solution)/shard_map/ppermute | solution.py:21
  8.9 9.6 %collective-permute-start.2 = (bf16[1,528,128]{2,1,0:T(8,128)(2,1)S(1)}, bf16[1,528,128]{2,1,0:T(8,128)(2,1)S(1)}, u32[]{:S(2)}, u32[]{:S(2)}) collective-permute-start(bf16[1,528,128]{2,1,0:T(8,128)(2,1)S(1)} %shard_map.67.refs_4_), channel_id=1, source_target_pairs={{0,2},{1,3},{2,0},{3,1},{4,6},{5,7},{6,4},{7,5},{8,10},{9,11},{10,... | collective-permute-start | bytes 405512 | tf_op jit(solution)/shard_map/ppermute | solution.py:21
  13.3 10.2 %collective-permute-start.5 = (bf16[1,528,128]{2,1,0:T(8,128)(2,1)S(1)}, bf16[1,528,128]{2,1,0:T(8,128)(2,1)S(1)}, u32[]{:S(2)}, u32[]{:S(2)}) collective-permute-start(bf16[1,528,128]{2,1,0:T(8,128)(2,1)S(1)} %shard_map.68.refs_3_), channel_id=1, source_target_pairs={{0,4},{1,5},{2,6},{3,7},{4,0},{5,1},{6,2},{7,3},{8,12},{9,13},{10,... | collective-permute-start | bytes 405512 | tf_op jit(solution)/shard_map/ppermute | solution.py:21
  16.9 6.7 %collective-permute-start.6 = (bf16[1,528,128]{2,1,0:T(8,128)(2,1)S(1)}, bf16[1,528,128]{2,1,0:T(8,128)(2,1)S(1)}, u32[]{:S(2)}, u32[]{:S(2)}) collective-permute-start(bf16[1,528,128]{2,1,0:T(8,128)(2,1)S(1)} %shard_map.69.refs_4_), channel_id=1, source_target_pairs={{0,2},{1,3},{2,0},{3,1},{4,6},{5,7},{6,4},{7,5},{8,10},{9,11},{10,... | collective-permute-start | bytes 405512 | tf_op jit(solution)/shard_map/ppermute | solution.py:21
  19.4 3.7 %collective-permute-start.4 = (f32[1,768]{1,0:T(1,128)S(1)}, f32[1,768]{1,0:T(1,128)S(1)}, u32[]{:S(2)}, u32[]{:S(2)}) collective-permute-start(f32[1,768]{1,0:T(1,128)S(1)} %get-tuple-element.42.refs_0_), channel_id=1, source_target_pairs={{0,8},{8,0},{16,24},{24,16},{1,9},{9,1},{17,25},{25,17},{2,10},{10... | collective-permute-start | bytes 9224 | tf_op jit(solution)/shard_map/ppermute | solution.py:21
  21.0 7.3 %collective-permute-start.9 = (bf16[1,528,128]{2,1,0:T(8,128)(2,1)S(1)}, bf16[1,528,128]{2,1,0:T(8,128)(2,1)S(1)}, u32[]{:S(2)}, u32[]{:S(2)}) collective-permute-start(bf16[1,528,128]{2,1,0:T(8,128)(2,1)S(1)} %shard_map.70.refs_4_), channel_id=1, source_target_pairs={{0,4},{1,5},{2,6},{3,7},{4,0},{5,1},{6,2},{7,3},{8,12},{9,13},{10,... | collective-permute-start | bytes 405512 | tf_op jit(solution)/shard_map/ppermute | solution.py:21
  21.3 6.8 %collective-permute-start.10 = (bf16[1,528,128]{2,1,0:T(8,128)(2,1)S(1)}, bf16[1,528,128]{2,1,0:T(8,128)(2,1)S(1)}, u32[]{:S(2)}, u32[]{:S(2)}) collective-permute-start(bf16[1,528,128]{2,1,0:T(8,128)(2,1)S(1)} %get-tuple-element.43.refs_2_.refs_5_), channel_id=1, source_target_pairs={{0,2},{1,3},{2,0},{3,1},{4,6},{5,7},{6,4},{7,5},{8,10},{9,11},{10,... | collective-permute-start | bytes 405512 | tf_op jit(solution)/shard_map/ppermute | solution.py:21
  24.1 6.4 %copy-start = (bf16[1,256,2048]{2,1,0:T(8,128)(2,1)S(1)}, bf16[1,256,2048]{2,1,0:T(8,128)(2,1)}, u32[]{:S(2)}) copy-start(bf16[1,256,2048]{2,1,0:T(8,128)(2,1)} %refs_0_.1) | copy-start | bytes 3145732
  24.1 6.4 %copy-start.1 = (bf16[1,512,512]{2,1,0:T(8,128)(2,1)S(1)}, bf16[1,512,512]{2,1,0:T(8,128)(2,1)}, u32[]{:S(2)}) copy-start(bf16[1,512,512]{2,1,0:T(8,128)(2,1)} %refs_1_.1) | copy-start | bytes 1572868
  24.1 7.0 %collective-permute-start.7 = (bf16[528,128]{1,0:T(8,128)(2,1)S(1)}, bf16[528,128]{1,0:T(8,128)(2,1)S(1)}, u32[]{:S(2)}, u32[]{:S(2)}) collective-permute-start(bf16[528,128]{1,0:T(8,128)(2,1)S(1)} %get-tuple-element.48.refs_7_), channel_id=1, source_target_pairs={{0,8},{8,0},{16,24},{24,16},{1,9},{9,1},{17,25},{25,17},{2,10},{10... | collective-permute-start | bytes 405512 | tf_op jit(solution)/shard_map/ppermute | solution.py:21
  28.9 5.1 %collective-permute-start.11 = (bf16[528,128]{1,0:T(8,128)(2,1)S(1)}, bf16[528,128]{1,0:T(8,128)(2,1)S(1)}, u32[]{:S(2)}, u32[]{:S(2)}) collective-permute-start(bf16[528,128]{1,0:T(8,128)(2,1)S(1)} %get-tuple-element.53), channel_id=1, source_target_pairs={{0,16},{8,24},{16,0},{24,8},{1,17},{9,25},{17,1},{25,9},{2,18},{10... | collective-permute-start | bytes 405512 | tf_op jit(solution)/shard_map/ppermute | solution.py:21
  31.5 5.5 %collective-permute-start.8 = (bf16[528,128]{1,0:T(8,128)(2,1)S(1)}, bf16[528,128]{1,0:T(8,128)(2,1)S(1)}, u32[]{:S(2)}, u32[]{:S(2)}) collective-permute-start(bf16[528,128]{1,0:T(8,128)(2,1)S(1)} %get-tuple-element.51), channel_id=1, source_target_pairs={{0,16},{8,24},{16,0},{24,8},{1,17},{9,25},{17,1},{25,9},{2,18},{10... | collective-permute-start | bytes 405512 | tf_op jit(solution)/shard_map/ppermute | solution.py:21
  33.1 19.2 %collective-permute-start.19 = (bf16[1024,256]{1,0:T(8,128)(2,1)S(1)}, bf16[1024,256]{1,0:T(8,128)(2,1)S(1)}, u32[]{:S(2)}, u32[]{:S(2)}) collective-permute-start(bf16[1024,256]{1,0:T(8,128)(2,1)S(1)} %get-tuple-element.56), channel_id=1, source_target_pairs={{0,1},{1,0},{2,3},{3,2},{4,5},{5,4},{6,7},{7,6},{8,9},{9,8},{10,11... | collective-permute-start | bytes 1572872 | tf_op jit(solution)/shard_map/ppermute | solution.py:21
  34.4 6.3 %collective-permute-start.12 = (bf16[528,128]{1,0:T(8,128)(2,1)S(1)}, bf16[528,128]{1,0:T(8,128)(2,1)S(1)}, u32[]{:S(2)}, u32[]{:S(2)}) collective-permute-start(bf16[528,128]{1,0:T(8,128)(2,1)S(1)} %get-tuple-element.55), channel_id=1, source_target_pairs={{0,8},{8,0},{16,24},{24,16},{1,9},{9,1},{17,25},{25,17},{2,10},{10... | collective-permute-start | bytes 405512 | tf_op jit(solution)/shard_map/ppermute | solution.py:21
  37.4 7.3 %collective-permute-start.15 = (bf16[512,128]{1,0:T(8,128)(2,1)S(1)}, bf16[512,128]{1,0:T(8,128)(2,1)S(1)}, u32[]{:S(2)}, u32[]{:S(2)}) collective-permute-start(bf16[512,128]{1,0:T(8,128)(2,1)S(1)} %shard_map.76.refs_5_.refs_1_), channel_id=1, source_target_pairs={{0,2},{1,3},{2,0},{3,1},{4,6},{5,7},{6,4},{7,5},{8,10},{9,11},{10,... | collective-permute-start | bytes 393224 | tf_op jit(solution)/shard_map/ppermute | solution.py:21
  38.3 11.6 %collective-permute-start.13 = (bf16[512,128]{1,0:T(8,128)(2,1)S(1)}, bf16[512,128]{1,0:T(8,128)(2,1)S(1)}, u32[]{:S(2)}, u32[]{:S(2)}) collective-permute-start(bf16[512,128]{1,0:T(8,128)(2,1)S(1)} %shard_map.76.refs_5_.refs_1_), channel_id=1, source_target_pairs={{0,4},{1,5},{2,6},{3,7},{4,0},{5,1},{6,2},{7,3},{8,12},{9,13},{10,... | collective-permute-start | bytes 393224 | tf_op jit(solution)/shard_map/ppermute | solution.py:21
  41.2 10.4 %collective-permute-start.14 = (bf16[512,128]{1,0:T(8,128)(2,1)S(1)}, bf16[512,128]{1,0:T(8,128)(2,1)S(1)}, u32[]{:S(2)}, u32[]{:S(2)}) collective-permute-start(bf16[512,128]{1,0:T(8,128)(2,1)S(1)} %shard_map.79.refs_2_), channel_id=1, source_target_pairs={{0,4},{1,5},{2,6},{3,7},{4,0},{5,1},{6,2},{7,3},{8,12},{9,13},{10,... | collective-permute-start | bytes 393224 | tf_op jit(solution)/shard_map/ppermute | solution.py:21
  41.8 10.8 %collective-permute-start.16 = (bf16[512,128]{1,0:T(8,128)(2,1)S(1)}, bf16[512,128]{1,0:T(8,128)(2,1)S(1)}, u32[]{:S(2)}, u32[]{:S(2)}) collective-permute-start(bf16[512,128]{1,0:T(8,128)(2,1)S(1)} %shard_map.79.refs_2_), channel_id=1, source_target_pairs={{0,2},{1,3},{2,0},{3,1},{4,6},{5,7},{6,4},{7,5},{8,10},{9,11},{10,... | collective-permute-start | bytes 393224 | tf_op jit(solution)/shard_map/ppermute | solution.py:21
  49.9 5.8 %collective-permute-start.17 = (bf16[1,512,128]{2,1,0:T(8,128)(2,1)S(1)}, bf16[1,512,128]{2,1,0:T(8,128)(2,1)S(1)}, u32[]{:S(2)}, u32[]{:S(2)}) collective-permute-start(bf16[1,512,128]{2,1,0:T(8,128)(2,1)S(1)} %shard_map.81), channel_id=1, source_target_pairs={{0,2},{1,3},{2,0},{3,1},{4,6},{5,7},{6,4},{7,5},{8,10},{9,11},{10,... | collective-permute-start | bytes 393224 | tf_op jit(solution)/shard_map/ppermute | solution.py:21
  51.5 5.6 %collective-permute-start.18 = (bf16[512,128]{1,0:T(8,128)(2,1)S(1)}, bf16[512,128]{1,0:T(8,128)(2,1)S(1)}, u32[]{:S(2)}, u32[]{:S(2)}) collective-permute-start(bf16[512,128]{1,0:T(8,128)(2,1)S(1)} %collective-permute-done.14.refs_4_), channel_id=1, source_target_pairs={{0,2},{1,3},{2,0},{3,1},{4,6},{5,7},{6,4},{7,5},{8,10},{9,11},{10,... | collective-permute-start | bytes 393224 | tf_op jit(solution)/shard_map/ppermute | solution.py:21
  57.5 1.6 %collective-permute-start.20 = (bf16[528,256]{1,0:T(8,128)(2,1)S(1)}, bf16[528,256]{1,0:T(8,128)(2,1)S(1)}, u32[]{:S(2)}, u32[]{:S(2)}) collective-permute-start(bf16[528,256]{1,0:T(8,128)(2,1)S(1)} %shard_map.86), channel_id=1, source_target_pairs={{0,1},{1,0},{2,3},{3,2},{4,5},{5,4},{6,7},{7,6},{8,9},{9,8},{10,11... | collective-permute-start | bytes 811016 | tf_op jit(solution)/shard_map/ppermute | solution.py:21
  59.6 5.7 %collective-permute-start.23 = (bf16[528,128]{1,0:T(8,128)(2,1)S(1)}, bf16[528,128]{1,0:T(8,128)(2,1)S(1)}, u32[]{:S(2)}, u32[]{:S(2)}) collective-permute-start(bf16[528,128]{1,0:T(8,128)(2,1)S(1)} %get-tuple-element.62), channel_id=1, source_target_pairs={{0,16},{8,24},{16,0},{24,8},{1,17},{9,25},{17,1},{25,9},{2,18},{10... | collective-permute-start | bytes 405512 | tf_op jit(solution)/shard_map/ppermute | solution.py:21
  59.7 6.2 %collective-permute-start.21 = (bf16[528,128]{1,0:T(8,128)(2,1)S(1)}, bf16[528,128]{1,0:T(8,128)(2,1)S(1)}, u32[]{:S(2)}, u32[]{:S(2)}) collective-permute-start(bf16[528,128]{1,0:T(8,128)(2,1)S(1)} %get-tuple-element.59), channel_id=1, source_target_pairs={{0,8},{8,0},{16,24},{24,16},{1,9},{9,1},{17,25},{25,17},{2,10},{10... | collective-permute-start | bytes 405512 | tf_op jit(solution)/shard_map/ppermute | solution.py:21
  65.7 5.1 %collective-permute-start.24 = (bf16[528,128]{1,0:T(8,128)(2,1)S(1)}, bf16[528,128]{1,0:T(8,128)(2,1)S(1)}, u32[]{:S(2)}, u32[]{:S(2)}) collective-permute-start(bf16[528,128]{1,0:T(8,128)(2,1)S(1)} %get-tuple-element.64), channel_id=1, source_target_pairs={{0,8},{8,0},{16,24},{24,16},{1,9},{9,1},{17,25},{25,17},{2,10},{10... | collective-permute-start | bytes 405512 | tf_op jit(solution)/shard_map/ppermute | solution.py:21
  66.3 5.1 %collective-permute-start.22 = (bf16[528,128]{1,0:T(8,128)(2,1)S(1)}, bf16[528,128]{1,0:T(8,128)(2,1)S(1)}, u32[]{:S(2)}, u32[]{:S(2)}) collective-permute-start(bf16[528,128]{1,0:T(8,128)(2,1)S(1)} %get-tuple-element.61), channel_id=1, source_target_pairs={{0,16},{8,24},{16,0},{24,8},{1,17},{9,25},{17,1},{25,9},{2,18},{10... | collective-permute-start | bytes 405512 | tf_op jit(solution)/shard_map/ppermute | solution.py:21

commit v8 on v7

--- a/solution.py
+++ b/solution.py
@@ -66,11 +66,11 @@
 
     lead = copy(grads_hbm.at[0], grads_ref)
     theirs = [load(o, 1 - core, inputs_ref.at[i]) for i, o in enumerate(range(1, chips, 2))]
+    lead.wait()
     others = [load(o, 1 - core, rest_ref.at[i]) for i, o in enumerate(range(0, chips, 2))]
     others += [load(o, core, own_ref.at[o]) for o in range(chips)]
     others.append(copy(out_decay, rates_ref.at[:, pl.ds(0, width)]))
     others.append(copy(in_decay, rates_ref.at[:, pl.ds(width, rows)]))
-    lead.wait()
     turned_ref[...] = grads_ref[...].T
     for i, arrival in enumerate(theirs):
         arrival.wait()

time: 72.5 us -> 72.6 us (level)
  no operation moved by 1% of the time
where the time goes in v8:
time: 72.6 us; the launch traced here: 72.5 us
  starting transfers between devices  30.8 us (42%)
  waiting for transfers between devices  27.3 us (38%)
  Pallas kernels  14 us (19%)
    ppermute x25, starting transfers between devices, exchange(): lax.ppermute(x, axis, [(i, i ^ flip) for i in range(lax.axis_size(axis))])  30.8 us
    ppermute x25, waiting for transfers between devices, exchange(): lax.ppermute(x, axis, [(i, i ^ flip) for i in range(lax.axis_size(axis))])  27.3 us
    pallas_call x27, Pallas kernels, call(): pl.pallas_call(kernel, out_shape=out_shape, in_specs=[HBM] * hbm + [VMEM]...  14 us
  transfers between devices with their start and end apart: 25, of which 16 were waited for; matrix products, arithmetic and copies ran while one was open for 0% of the time, Pallas kernels for 13%

profile of v8, /device:TPU:0, one launch (start us, length us, event | category | flops | bytes accessed | tf_op | source)
XLA Modules:
  0.0 72.5 jit_solution(9115753812528154780)
XLA Ops:
  0.0 2.9 %shard_map.64 = (bf16[2,528,256]{2,1,0:T(8,128)(2,1)S(1)}, bf16[512,640]{1,0:T(8,128)(2,1)S(1)}, bf16[2,640,256]{2,1,0:T(8,128)(2,1)S(1)}, bf16[4,640,256]{2,1,0:T(8,128)(2,1)S(1)}, f32[1,768]{1,0:T(1,128)S(1)}) custom-call(bf16[1,640,512]{2,1,0:T(8,128)(2,1)} %grads_hbm.1, bf16[1,640,2048]{2,1,0:T(8,128)(2,1)} %inputs_hbm.1, f32[1,512]{1,0:T(1,128)} %out_decay.1, ...), custom_call_target="tpu_custom_call" | custom-call | flops 1200000000 | bytes 100000000 | tf_op jit(solution)/shard_map/pallas_call | solution.py:308
  3.4 1.0 %shard_map.65 = (bf16[2,528,256]{2,1,0:T(8,128)(2,1)S(1)}, bf16[512,640]{1,0:T(8,128)(2,1)S(1)}) custom-call(bf16[512,640]{1,0:T(8,128)(2,1)S(1)} %get-tuple-element.35.refs_0_, bf16[2,640,256]{2,1,0:T(8,128)(2,1)S(1)} %get-tuple-element.36.refs_1_, bf16[2,528,256]{2,1,0:T(8,128)(2,1)S(1)} %get-tuple-element.37.refs_2_), custom_call_target="tpu_custom_call" | custom-call | flops 1200000000 | bytes 100000000 | tf_op jit(solution)/shard_map/pallas_call | solution.py:308
  5.4 3.0 %collective-permute-start.3 = (bf16[1,528,128]{2,1,0:T(8,128)(2,1)S(1)}, bf16[1,528,128]{2,1,0:T(8,128)(2,1)S(1)}, u32[]{:S(2)}, u32[]{:S(2)}) collective-permute-start(bf16[1,528,128]{2,1,0:T(8,128)(2,1)S(1)} %shard_map.66.refs_3_), channel_id=1, source_target_pairs={{0,2},{1,3},{2,0},{3,1},{4,6},{5,7},{6,4},{7,5},{8,10},{9,11},{10,... | collective-permute-start | bytes 405512 | tf_op jit(solution)/shard_map/ppermute | solution.py:21
  9.0 3.8 %collective-permute-done.3.refs_3_ = bf16[1,528,128]{2,1,0:T(8,128)(2,1)S(1)} collective-permute-done((bf16[1,528,128]{2,1,0:T(8,128)(2,1)S(1)}, bf16[1,528,128]{2,1,0:T(8,128)(2,1)S(1)}, u32[]{:S(2)}, u32[]{:S(2)}) %collective-permute-start.3) | collective-permute-done | bytes 135200 | tf_op jit(solution)/shard_map/ppermute | solution.py:21
  13.3 3.1 %collective-permute-start.5 = (bf16[1,528,128]{2,1,0:T(8,128)(2,1)S(1)}, bf16[1,528,128]{2,1,0:T(8,128)(2,1)S(1)}, u32[]{:S(2)}, u32[]{:S(2)}) collective-permute-start(bf16[1,528,128]{2,1,0:T(8,128)(2,1)S(1)} %shard_map.68.refs_3_), channel_id=1, source_target_pairs={{0,4},{1,5},{2,6},{3,7},{4,0},{5,1},{6,2},{7,3},{8,12},{9,13},{10,... | collective-permute-start | bytes 405512 | tf_op jit(solution)/shard_map/ppermute | solution.py:21
  16.9 1.6 %collective-permute-start.6 = (bf16[1,528,128]{2,1,0:T(8,128)(2,1)S(1)}, bf16[1,528,128]{2,1,0:T(8,128)(2,1)S(1)}, u32[]{:S(2)}, u32[]{:S(2)}) collective-permute-start(bf16[1,528,128]{2,1,0:T(8,128)(2,1)S(1)} %shard_map.69.refs_4_), channel_id=1, source_target_pairs={{0,2},{1,3},{2,0},{3,1},{4,6},{5,7},{6,4},{7,5},{8,10},{9,11},{10,... | collective-permute-start | bytes 405512 | tf_op jit(solution)/shard_map/ppermute | solution.py:21
  19.4 1.6 %collective-permute-start.4 = (f32[1,768]{1,0:T(1,128)S(1)}, f32[1,768]{1,0:T(1,128)S(1)}, u32[]{:S(2)}, u32[]{:S(2)}) collective-permute-start(f32[1,768]{1,0:T(1,128)S(1)} %get-tuple-element.42.refs_0_), channel_id=1, source_target_pairs={{0,8},{8,0},{16,24},{24,16},{1,9},{9,1},{17,25},{25,17},{2,10},{10... | collective-permute-start | bytes 9224 | tf_op jit(solution)/shard_map/ppermute | solution.py:21
  21.3 0.7 collective-permute-start.10
  22.0 1.1 %collective-permute-done.4.refs_1_ = f32[1,768]{1,0:T(1,128)S(1)} collective-permute-done((f32[1,768]{1,0:T(1,128)S(1)}, f32[1,768]{1,0:T(1,128)S(1)}, u32[]{:S(2)}, u32[]{:S(2)}) %collective-permute-start.4) | collective-permute-done | bytes 3104 | tf_op jit(solution)/shard_map/ppermute | solution.py:21
  23.5 0.6 shard_map.74
  24.1 4.0 %collective-permute-start.7 = (bf16[528,128]{1,0:T(8,128)(2,1)S(1)}, bf16[528,128]{1,0:T(8,128)(2,1)S(1)}, u32[]{:S(2)}, u32[]{:S(2)}) collective-permute-start(bf16[528,128]{1,0:T(8,128)(2,1)S(1)} %get-tuple-element.48.refs_7_), channel_id=1, source_target_pairs={{0,8},{8,0},{16,24},{24,16},{1,9},{9,1},{17,25},{25,17},{2,10},{10... | collective-permute-start | bytes 405512 | tf_op jit(solution)/shard_map/ppermute | solution.py:21
  28.3 0.6 shard_map.77
  28.9 1.6 %collective-permute-start.11 = (bf16[528,128]{1,0:T(8,128)(2,1)S(1)}, bf16[528,128]{1,0:T(8,128)(2,1)S(1)}, u32[]{:S(2)}, u32[]{:S(2)}) collective-permute-start(bf16[528,128]{1,0:T(8,128)(2,1)S(1)} %get-tuple-element.53), channel_id=1, source_target_pairs={{0,16},{8,24},{16,0},{24,8},{1,17},{9,25},{17,1},{25,9},{2,18},{10... | collective-permute-start | bytes 405512 | tf_op jit(solution)/shard_map/ppermute | solution.py:21
  31.5 1.6 %collective-permute-start.8 = (bf16[528,128]{1,0:T(8,128)(2,1)S(1)}, bf16[528,128]{1,0:T(8,128)(2,1)S(1)}, u32[]{:S(2)}, u32[]{:S(2)}) collective-permute-start(bf16[528,128]{1,0:T(8,128)(2,1)S(1)} %get-tuple-element.51), channel_id=1, source_target_pairs={{0,16},{8,24},{16,0},{24,8},{1,17},{9,25},{17,1},{25,9},{2,18},{10... | collective-permute-start | bytes 405512 | tf_op jit(solution)/shard_map/ppermute | solution.py:21
  33.1 0.9 %collective-permute-done.11.message_ref = bf16[528,128]{1,0:T(8,128)(2,1)S(1)} collective-permute-done((bf16[528,128]{1,0:T(8,128)(2,1)S(1)}, bf16[528,128]{1,0:T(8,128)(2,1)S(1)}, u32[]{:S(2)}, u32[]{:S(2)}) %collective-permute-start.11) | collective-permute-done | bytes 135200 | tf_op jit(solution)/shard_map/ppermute | solution.py:21
  34.4 2.7 %collective-permute-start.12 = (bf16[528,128]{1,0:T(8,128)(2,1)S(1)}, bf16[528,128]{1,0:T(8,128)(2,1)S(1)}, u32[]{:S(2)}, u32[]{:S(2)}) collective-permute-start(bf16[528,128]{1,0:T(8,128)(2,1)S(1)} %get-tuple-element.55), channel_id=1, source_target_pairs={{0,8},{8,0},{16,24},{24,16},{1,9},{9,1},{17,25},{25,17},{2,10},{10... | collective-permute-start | bytes 405512 | tf_op jit(solution)/shard_map/ppermute | solution.py:21
  37.5 0.9 %collective-permute-start.15 = (bf16[512,128]{1,0:T(8,128)(2,1)S(1)}, bf16[512,128]{1,0:T(8,128)(2,1)S(1)}, u32[]{:S(2)}, u32[]{:S(2)}) collective-permute-start(bf16[512,128]{1,0:T(8,128)(2,1)S(1)} %shard_map.76.refs_5_.refs_1_), channel_id=1, source_target_pairs={{0,2},{1,3},{2,0},{3,1},{4,6},{5,7},{6,4},{7,5},{8,10},{9,11},{10,... | collective-permute-start | bytes 393224 | tf_op jit(solution)/shard_map/ppermute | solution.py:21
  38.3 2.4 %collective-permute-start.13 = (bf16[512,128]{1,0:T(8,128)(2,1)S(1)}, bf16[512,128]{1,0:T(8,128)(2,1)S(1)}, u32[]{:S(2)}, u32[]{:S(2)}) collective-permute-start(bf16[512,128]{1,0:T(8,128)(2,1)S(1)} %shard_map.76.refs_5_.refs_1_), channel_id=1, source_target_pairs={{0,4},{1,5},{2,6},{3,7},{4,0},{5,1},{6,2},{7,3},{8,12},{9,13},{10,... | collective-permute-start | bytes 393224 | tf_op jit(solution)/shard_map/ppermute | solution.py:21
  41.1 0.6 collective-permute-start.14
  41.8 2.8 %collective-permute-start.16 = (bf16[512,128]{1,0:T(8,128)(2,1)S(1)}, bf16[512,128]{1,0:T(8,128)(2,1)S(1)}, u32[]{:S(2)}, u32[]{:S(2)}) collective-permute-start(bf16[512,128]{1,0:T(8,128)(2,1)S(1)} %shard_map.79.refs_2_), channel_id=1, source_target_pairs={{0,2},{1,3},{2,0},{3,1},{4,6},{5,7},{6,4},{7,5},{8,10},{9,11},{10,... | collective-permute-start | bytes 393224 | tf_op jit(solution)/shard_map/ppermute | solution.py:21
  44.7 5.2 %collective-permute-done.13.refs_3_.refs_0_ = bf16[512,128]{1,0:T(8,128)(2,1)S(1)} collective-permute-done((bf16[512,128]{1,0:T(8,128)(2,1)S(1)}, bf16[512,128]{1,0:T(8,128)(2,1)S(1)}, u32[]{:S(2)}, u32[]{:S(2)}) %collective-permute-start.13) | collective-permute-done | bytes 131104 | tf_op jit(solution)/shard_map/ppermute | solution.py:21
  50.0 1.5 %collective-permute-done.14.refs_4_ = bf16[512,128]{1,0:T(8,128)(2,1)S(1)} collective-permute-done((bf16[512,128]{1,0:T(8,128)(2,1)S(1)}, bf16[512,128]{1,0:T(8,128)(2,1)S(1)}, u32[]{:S(2)}, u32[]{:S(2)}) %collective-permute-start.14) | collective-permute-done | bytes 131104 | tf_op jit(solution)/shard_map/ppermute | solution.py:21
  51.5 0.5 collective-permute-start.18
  52.7 3.0 %collective-permute-done.17.refs_4_ = bf16[1,512,128]{2,1,0:T(8,128)(2,1)S(1)} collective-permute-done((bf16[1,512,128]{2,1,0:T(8,128)(2,1)S(1)}, bf16[1,512,128]{2,1,0:T(8,128)(2,1)S(1)}, u32[]{:S(2)}, u32[]{:S(2)}) %collective-permute-start.17) | collective-permute-done | bytes 131104 | tf_op jit(solution)/shard_map/ppermute | solution.py:21
  56.3 0.8 %collective-permute-done.18.refs_2_ = bf16[512,128]{1,0:T(8,128)(2,1)S(1)} collective-permute-done((bf16[512,128]{1,0:T(8,128)(2,1)S(1)}, bf16[512,128]{1,0:T(8,128)(2,1)S(1)}, u32[]{:S(2)}, u32[]{:S(2)}) %collective-permute-start.18) | collective-permute-done | bytes 131104 | tf_op jit(solution)/shard_map/ppermute | solution.py:21
  57.8 1.3 %collective-permute-done.20.theirs_ref = bf16[528,256]{1,0:T(8,128)(2,1)S(1)} collective-permute-done((bf16[528,256]{1,0:T(8,128)(2,1)S(1)}, bf16[528,256]{1,0:T(8,128)(2,1)S(1)}, u32[]{:S(2)}, u32[]{:S(2)}) %collective-permute-start.20) | collective-permute-done | bytes 270368 | tf_op jit(solution)/shard_map/ppermute | solution.py:21
  59.7 1.0 %collective-permute-start.21 = (bf16[528,128]{1,0:T(8,128)(2,1)S(1)}, bf16[528,128]{1,0:T(8,128)(2,1)S(1)}, u32[]{:S(2)}, u32[]{:S(2)}) collective-permute-start(bf16[528,128]{1,0:T(8,128)(2,1)S(1)} %get-tuple-element.59), channel_id=1, source_target_pairs={{0,8},{8,0},{16,24},{24,16},{1,9},{9,1},{17,25},{25,17},{2,10},{10... | collective-permute-start | bytes 405512 | tf_op jit(solution)/shard_map/ppermute | solution.py:21
  60.7 4.6 %collective-permute-done.23.message_ref = bf16[528,128]{1,0:T(8,128)(2,1)S(1)} collective-permute-done((bf16[528,128]{1,0:T(8,128)(2,1)S(1)}, bf16[528,128]{1,0:T(8,128)(2,1)S(1)}, u32[]{:S(2)}, u32[]{:S(2)}) %collective-permute-start.23) | collective-permute-done | bytes 135200 | tf_op jit(solution)/shard_map/ppermute | solution.py:21
  66.3 1.2 %collective-permute-start.22 = (bf16[528,128]{1,0:T(8,128)(2,1)S(1)}, bf16[528,128]{1,0:T(8,128)(2,1)S(1)}, u32[]{:S(2)}, u32[]{:S(2)}) collective-permute-start(bf16[528,128]{1,0:T(8,128)(2,1)S(1)} %get-tuple-element.61), channel_id=1, source_target_pairs={{0,16},{8,24},{16,0},{24,8},{1,17},{9,25},{17,1},{25,9},{2,18},{10... | collective-permute-start | bytes 405512 | tf_op jit(solution)/shard_map/ppermute | solution.py:21
  67.5 3.3 %collective-permute-done.24.refs_3_ = bf16[528,128]{1,0:T(8,128)(2,1)S(1)} collective-permute-done((bf16[528,128]{1,0:T(8,128)(2,1)S(1)}, bf16[528,128]{1,0:T(8,128)(2,1)S(1)}, u32[]{:S(2)}, u32[]{:S(2)}) %collective-permute-start.24) | collective-permute-done | bytes 135200 | tf_op jit(solution)/shard_map/ppermute | solution.py:21
  70.8 0.6 collective-permute-done.22.refs_1_
  71.4 1.1 %shard_map.90 = bf16[1,256,512]{2,1,0:T(8,128)(2,1)} custom-call(f32[512,128]{1,0:T(8,128)S(1)} %get-tuple-element.44.cols_ref.refs_5_.refs_2_, f32[24,256]{1,0:T(8,128)S(1)} %get-tuple-element.45.rows_ref.refs_6_.refs_3_, f32[512,128]{1,0:T(8,128)S(1)} %get-tuple-element.60.refs_0_, bf16[528,128]{1,0:T(8,128)(2,1)S(1)} %collective-permute-done.22.refs_1_, ...), custom_call_target="tpu_custom_call" | custom-call | flops 1200000000 | bytes 100000000 | tf_op jit(solution)/shard_map/pallas_call | solution.py:308
  (49 shorter events, 10.7 us)
Async XLA Ops:
  2.9 2.1 %collective-permute-start = (bf16[2,528,256]{2,1,0:T(8,128)(2,1)S(1)}, bf16[2,528,256]{2,1,0:T(8,128)(2,1)S(1)}, u32[]{:S(2)}, u32[]{:S(2)}) collective-permute-start(bf16[2,528,256]{2,1,0:T(8,128)(2,1)S(1)} %get-tuple-element.37.refs_2_), channel_id=1, source_target_pairs={{0,1},{1,0},{2,3},{3,2},{4,5},{5,4},{6,7},{7,6},{8,9},{9,8},{10,11... | collective-permute-start | bytes 1622024 | tf_op jit(solution)/shard_map/ppermute | solution.py:21
  4.4 4.5 %collective-permute-start.1 = (bf16[2,528,256]{2,1,0:T(8,128)(2,1)S(1)}, bf16[2,528,256]{2,1,0:T(8,128)(2,1)S(1)}, u32[]{:S(2)}, u32[]{:S(2)}) collective-permute-start(bf16[2,528,256]{2,1,0:T(8,128)(2,1)S(1)} %get-tuple-element.41), channel_id=1, source_target_pairs={{0,1},{1,0},{2,3},{3,2},{4,5},{5,4},{6,7},{7,6},{8,9},{9,8},{10,11... | collective-permute-start | bytes 1622024 | tf_op jit(solution)/shard_map/ppermute | solution.py:21
  5.4 7.4 %collective-permute-start.3 = (bf16[1,528,128]{2,1,0:T(8,128)(2,1)S(1)}, bf16[1,528,128]{2,1,0:T(8,128)(2,1)S(1)}, u32[]{:S(2)}, u32[]{:S(2)}) collective-permute-start(bf16[1,528,128]{2,1,0:T(8,128)(2,1)S(1)} %shard_map.66.refs_3_), channel_id=1, source_target_pairs={{0,2},{1,3},{2,0},{3,1},{4,6},{5,7},{6,4},{7,5},{8,10},{9,11},{10,... | collective-permute-start | bytes 405512 | tf_op jit(solution)/shard_map/ppermute | solution.py:21
  8.9 9.6 %collective-permute-start.2 = (bf16[1,528,128]{2,1,0:T(8,128)(2,1)S(1)}, bf16[1,528,128]{2,1,0:T(8,128)(2,1)S(1)}, u32[]{:S(2)}, u32[]{:S(2)}) collective-permute-start(bf16[1,528,128]{2,1,0:T(8,128)(2,1)S(1)} %shard_map.67.refs_4_), channel_id=1, source_target_pairs={{0,2},{1,3},{2,0},{3,1},{4,6},{5,7},{6,4},{7,5},{8,10},{9,11},{10,... | collective-permute-start | bytes 405512 | tf_op jit(solution)/shard_map/ppermute | solution.py:21
  13.3 10.3 %collective-permute-start.5 = (bf16[1,528,128]{2,1,0:T(8,128)(2,1)S(1)}, bf16[1,528,128]{2,1,0:T(8,128)(2,1)S(1)}, u32[]{:S(2)}, u32[]{:S(2)}) collective-permute-start(bf16[1,528,128]{2,1,0:T(8,128)(2,1)S(1)} %shard_map.68.refs_3_), channel_id=1, source_target_pairs={{0,4},{1,5},{2,6},{3,7},{4,0},{5,1},{6,2},{7,3},{8,12},{9,13},{10,... | collective-permute-start | bytes 405512 | tf_op jit(solution)/shard_map/ppermute | solution.py:21
  16.9 6.7 %collective-permute-start.6 = (bf16[1,528,128]{2,1,0:T(8,128)(2,1)S(1)}, bf16[1,528,128]{2,1,0:T(8,128)(2,1)S(1)}, u32[]{:S(2)}, u32[]{:S(2)}) collective-permute-start(bf16[1,528,128]{2,1,0:T(8,128)(2,1)S(1)} %shard_map.69.refs_4_), channel_id=1, source_target_pairs={{0,2},{1,3},{2,0},{3,1},{4,6},{5,7},{6,4},{7,5},{8,10},{9,11},{10,... | collective-permute-start | bytes 405512 | tf_op jit(solution)/shard_map/ppermute | solution.py:21
  19.4 3.7 %collective-permute-start.4 = (f32[1,768]{1,0:T(1,128)S(1)}, f32[1,768]{1,0:T(1,128)S(1)}, u32[]{:S(2)}, u32[]{:S(2)}) collective-permute-start(f32[1,768]{1,0:T(1,128)S(1)} %get-tuple-element.42.refs_0_), channel_id=1, source_target_pairs={{0,8},{8,0},{16,24},{24,16},{1,9},{9,1},{17,25},{25,17},{2,10},{10... | collective-permute-start | bytes 9224 | tf_op jit(solution)/shard_map/ppermute | solution.py:21
  21.0 7.3 %collective-permute-start.9 = (bf16[1,528,128]{2,1,0:T(8,128)(2,1)S(1)}, bf16[1,528,128]{2,1,0:T(8,128)(2,1)S(1)}, u32[]{:S(2)}, u32[]{:S(2)}) collective-permute-start(bf16[1,528,128]{2,1,0:T(8,128)(2,1)S(1)} %shard_map.70.refs_4_), channel_id=1, source_target_pairs={{0,4},{1,5},{2,6},{3,7},{4,0},{5,1},{6,2},{7,3},{8,12},{9,13},{10,... | collective-permute-start | bytes 405512 | tf_op jit(solution)/shard_map/ppermute | solution.py:21
  21.3 6.8 %collective-permute-start.10 = (bf16[1,528,128]{2,1,0:T(8,128)(2,1)S(1)}, bf16[1,528,128]{2,1,0:T(8,128)(2,1)S(1)}, u32[]{:S(2)}, u32[]{:S(2)}) collective-permute-start(bf16[1,528,128]{2,1,0:T(8,128)(2,1)S(1)} %get-tuple-element.43.refs_2_.refs_5_), channel_id=1, source_target_pairs={{0,2},{1,3},{2,0},{3,1},{4,6},{5,7},{6,4},{7,5},{8,10},{9,11},{10,... | collective-permute-start | bytes 405512 | tf_op jit(solution)/shard_map/ppermute | solution.py:21
  24.1 6.4 %copy-start = (bf16[1,256,2048]{2,1,0:T(8,128)(2,1)S(1)}, bf16[1,256,2048]{2,1,0:T(8,128)(2,1)}, u32[]{:S(2)}) copy-start(bf16[1,256,2048]{2,1,0:T(8,128)(2,1)} %refs_0_.1) | copy-start | bytes 3145732
  24.1 6.4 %copy-start.1 = (bf16[1,512,512]{2,1,0:T(8,128)(2,1)S(1)}, bf16[1,512,512]{2,1,0:T(8,128)(2,1)}, u32[]{:S(2)}) copy-start(bf16[1,512,512]{2,1,0:T(8,128)(2,1)} %refs_1_.1) | copy-start | bytes 1572868
  24.1 6.9 %collective-permute-start.7 = (bf16[528,128]{1,0:T(8,128)(2,1)S(1)}, bf16[528,128]{1,0:T(8,128)(2,1)S(1)}, u32[]{:S(2)}, u32[]{:S(2)}) collective-permute-start(bf16[528,128]{1,0:T(8,128)(2,1)S(1)} %get-tuple-element.48.refs_7_), channel_id=1, source_target_pairs={{0,8},{8,0},{16,24},{24,16},{1,9},{9,1},{17,25},{25,17},{2,10},{10... | collective-permute-start | bytes 405512 | tf_op jit(solution)/shard_map/ppermute | solution.py:21
  28.9 5.1 %collective-permute-start.11 = (bf16[528,128]{1,0:T(8,128)(2,1)S(1)}, bf16[528,128]{1,0:T(8,128)(2,1)S(1)}, u32[]{:S(2)}, u32[]{:S(2)}) collective-permute-start(bf16[528,128]{1,0:T(8,128)(2,1)S(1)} %get-tuple-element.53), channel_id=1, source_target_pairs={{0,16},{8,24},{16,0},{24,8},{1,17},{9,25},{17,1},{25,9},{2,18},{10... | collective-permute-start | bytes 405512 | tf_op jit(solution)/shard_map/ppermute | solution.py:21
  31.5 5.5 %collective-permute-start.8 = (bf16[528,128]{1,0:T(8,128)(2,1)S(1)}, bf16[528,128]{1,0:T(8,128)(2,1)S(1)}, u32[]{:S(2)}, u32[]{:S(2)}) collective-permute-start(bf16[528,128]{1,0:T(8,128)(2,1)S(1)} %get-tuple-element.51), channel_id=1, source_target_pairs={{0,16},{8,24},{16,0},{24,8},{1,17},{9,25},{17,1},{25,9},{2,18},{10... | collective-permute-start | bytes 405512 | tf_op jit(solution)/shard_map/ppermute | solution.py:21
  33.1 19.3 %collective-permute-start.19 = (bf16[1024,256]{1,0:T(8,128)(2,1)S(1)}, bf16[1024,256]{1,0:T(8,128)(2,1)S(1)}, u32[]{:S(2)}, u32[]{:S(2)}) collective-permute-start(bf16[1024,256]{1,0:T(8,128)(2,1)S(1)} %get-tuple-element.56), channel_id=1, source_target_pairs={{0,1},{1,0},{2,3},{3,2},{4,5},{5,4},{6,7},{7,6},{8,9},{9,8},{10,11... | collective-permute-start | bytes 1572872 | tf_op jit(solution)/shard_map/ppermute | solution.py:21
  34.4 6.3 %collective-permute-start.12 = (bf16[528,128]{1,0:T(8,128)(2,1)S(1)}, bf16[528,128]{1,0:T(8,128)(2,1)S(1)}, u32[]{:S(2)}, u32[]{:S(2)}) collective-permute-start(bf16[528,128]{1,0:T(8,128)(2,1)S(1)} %get-tuple-element.55), channel_id=1, source_target_pairs={{0,8},{8,0},{16,24},{24,16},{1,9},{9,1},{17,25},{25,17},{2,10},{10... | collective-permute-start | bytes 405512 | tf_op jit(solution)/shard_map/ppermute | solution.py:21
  37.5 7.2 %collective-permute-start.15 = (bf16[512,128]{1,0:T(8,128)(2,1)S(1)}, bf16[512,128]{1,0:T(8,128)(2,1)S(1)}, u32[]{:S(2)}, u32[]{:S(2)}) collective-permute-start(bf16[512,128]{1,0:T(8,128)(2,1)S(1)} %shard_map.76.refs_5_.refs_1_), channel_id=1, source_target_pairs={{0,2},{1,3},{2,0},{3,1},{4,6},{5,7},{6,4},{7,5},{8,10},{9,11},{10,... | collective-permute-start | bytes 393224 | tf_op jit(solution)/shard_map/ppermute | solution.py:21
  38.3 11.6 %collective-permute-start.13 = (bf16[512,128]{1,0:T(8,128)(2,1)S(1)}, bf16[512,128]{1,0:T(8,128)(2,1)S(1)}, u32[]{:S(2)}, u32[]{:S(2)}) collective-permute-start(bf16[512,128]{1,0:T(8,128)(2,1)S(1)} %shard_map.76.refs_5_.refs_1_), channel_id=1, source_target_pairs={{0,4},{1,5},{2,6},{3,7},{4,0},{5,1},{6,2},{7,3},{8,12},{9,13},{10,... | collective-permute-start | bytes 393224 | tf_op jit(solution)/shard_map/ppermute | solution.py:21
  41.1 10.4 %collective-permute-start.14 = (bf16[512,128]{1,0:T(8,128)(2,1)S(1)}, bf16[512,128]{1,0:T(8,128)(2,1)S(1)}, u32[]{:S(2)}, u32[]{:S(2)}) collective-permute-start(bf16[512,128]{1,0:T(8,128)(2,1)S(1)} %shard_map.79.refs_2_), channel_id=1, source_target_pairs={{0,4},{1,5},{2,6},{3,7},{4,0},{5,1},{6,2},{7,3},{8,12},{9,13},{10,... | collective-permute-start | bytes 393224 | tf_op jit(solution)/shard_map/ppermute | solution.py:21
  41.8 10.9 %collective-permute-start.16 = (bf16[512,128]{1,0:T(8,128)(2,1)S(1)}, bf16[512,128]{1,0:T(8,128)(2,1)S(1)}, u32[]{:S(2)}, u32[]{:S(2)}) collective-permute-start(bf16[512,128]{1,0:T(8,128)(2,1)S(1)} %shard_map.79.refs_2_), channel_id=1, source_target_pairs={{0,2},{1,3},{2,0},{3,1},{4,6},{5,7},{6,4},{7,5},{8,10},{9,11},{10,... | collective-permute-start | bytes 393224 | tf_op jit(solution)/shard_map/ppermute | solution.py:21
  50.0 5.8 %collective-permute-start.17 = (bf16[1,512,128]{2,1,0:T(8,128)(2,1)S(1)}, bf16[1,512,128]{2,1,0:T(8,128)(2,1)S(1)}, u32[]{:S(2)}, u32[]{:S(2)}) collective-permute-start(bf16[1,512,128]{2,1,0:T(8,128)(2,1)S(1)} %shard_map.81), channel_id=1, source_target_pairs={{0,2},{1,3},{2,0},{3,1},{4,6},{5,7},{6,4},{7,5},{8,10},{9,11},{10,... | collective-permute-start | bytes 393224 | tf_op jit(solution)/shard_map/ppermute | solution.py:21
  51.5 5.6 %collective-permute-start.18 = (bf16[512,128]{1,0:T(8,128)(2,1)S(1)}, bf16[512,128]{1,0:T(8,128)(2,1)S(1)}, u32[]{:S(2)}, u32[]{:S(2)}) collective-permute-start(bf16[512,128]{1,0:T(8,128)(2,1)S(1)} %collective-permute-done.14.refs_4_), channel_id=1, source_target_pairs={{0,2},{1,3},{2,0},{3,1},{4,6},{5,7},{6,4},{7,5},{8,10},{9,11},{10,... | collective-permute-start | bytes 393224 | tf_op jit(solution)/shard_map/ppermute | solution.py:21
  57.5 1.6 %collective-permute-start.20 = (bf16[528,256]{1,0:T(8,128)(2,1)S(1)}, bf16[528,256]{1,0:T(8,128)(2,1)S(1)}, u32[]{:S(2)}, u32[]{:S(2)}) collective-permute-start(bf16[528,256]{1,0:T(8,128)(2,1)S(1)} %shard_map.86), channel_id=1, source_target_pairs={{0,1},{1,0},{2,3},{3,2},{4,5},{5,4},{6,7},{7,6},{8,9},{9,8},{10,11... | collective-permute-start | bytes 811016 | tf_op jit(solution)/shard_map/ppermute | solution.py:21
  59.6 5.7 %collective-permute-start.23 = (bf16[528,128]{1,0:T(8,128)(2,1)S(1)}, bf16[528,128]{1,0:T(8,128)(2,1)S(1)}, u32[]{:S(2)}, u32[]{:S(2)}) collective-permute-start(bf16[528,128]{1,0:T(8,128)(2,1)S(1)} %get-tuple-element.62), channel_id=1, source_target_pairs={{0,16},{8,24},{16,0},{24,8},{1,17},{9,25},{17,1},{25,9},{2,18},{10... | collective-permute-start | bytes 405512 | tf_op jit(solution)/shard_map/ppermute | solution.py:21
  59.7 6.2 %collective-permute-start.21 = (bf16[528,128]{1,0:T(8,128)(2,1)S(1)}, bf16[528,128]{1,0:T(8,128)(2,1)S(1)}, u32[]{:S(2)}, u32[]{:S(2)}) collective-permute-start(bf16[528,128]{1,0:T(8,128)(2,1)S(1)} %get-tuple-element.59), channel_id=1, source_target_pairs={{0,8},{8,0},{16,24},{24,16},{1,9},{9,1},{17,25},{25,17},{2,10},{10... | collective-permute-start | bytes 405512 | tf_op jit(solution)/shard_map/ppermute | solution.py:21
  65.7 5.1 %collective-permute-start.24 = (bf16[528,128]{1,0:T(8,128)(2,1)S(1)}, bf16[528,128]{1,0:T(8,128)(2,1)S(1)}, u32[]{:S(2)}, u32[]{:S(2)}) collective-permute-start(bf16[528,128]{1,0:T(8,128)(2,1)S(1)} %get-tuple-element.64), channel_id=1, source_target_pairs={{0,8},{8,0},{16,24},{24,16},{1,9},{9,1},{17,25},{25,17},{2,10},{10... | collective-permute-start | bytes 405512 | tf_op jit(solution)/shard_map/ppermute | solution.py:21
  66.3 5.1 %collective-permute-start.22 = (bf16[528,128]{1,0:T(8,128)(2,1)S(1)}, bf16[528,128]{1,0:T(8,128)(2,1)S(1)}, u32[]{:S(2)}, u32[]{:S(2)}) collective-permute-start(bf16[528,128]{1,0:T(8,128)(2,1)S(1)} %get-tuple-element.61), channel_id=1, source_target_pairs={{0,16},{8,24},{16,0},{24,8},{1,17},{9,25},{17,1},{25,9},{2,18},{10... | collective-permute-start | bytes 405512 | tf_op jit(solution)/shard_map/ppermute | solution.py:21
